TPU v7x, 32 devices: a whole 2x2x4 slice. The times are simulated.
32 devices in a mesh: vox: 2 (over x), row: 4 (over z), wl: 4 (over y, core).
Axes of the slice: x: 2, y: 2, z: 4, core: 2. Of those that a mesh axis runs over, the one named last changes fastest.
Arguments:
- jacobian: bfloat16 [2048, 1280], P(('row', 'wl'), 'vox'), may hold values from -0.15625 to 0.15625
- extinction: float32 [4, 2], replicated, may hold values from 0.3 to 3
- prior_var: float32 [2, 1280], P(None, 'vox'), may hold values from 0.1 to 10
Outputs:
- gram: float32 [2048, 2048], P(('row', 'wl'), 'vox')
All inputs are finite; a program needn't handle non-finite values.
Results may differ from a plain program's by a relative error of at most 0.005.
Values may be sent and summed in bfloat16 or wider, within the bound.
No kernel may reach another device: no remote copies, remote signals or barrier semaphores. Data moves between devices by JAX's collectives and lax.ppermute only.
A program may use at most 128 MiB of HBM per device.

v0:
```python
import jax
import jax.numpy as jnp
from jax import lax
from jax.sharding import PartitionSpec as P


def spectral_table(extinction, prior_var, wave_index):
    coeff = lax.dynamic_index_in_dim(extinction, wave_index, 0, keepdims=True)
    return jnp.dot(extinction * coeff, prior_var, precision=lax.Precision.HIGHEST)


def weigh_rows(portion, table, tile_rows):
    count = portion.shape[0]
    waves = jnp.arange(count, dtype=jnp.int32) // tile_rows % table.shape[0]
    onehot = (waves[:, None] == jnp.arange(table.shape[0], dtype=jnp.int32)[None, :]).astype(
        jnp.float32
    )
    weights = jnp.dot(onehot, table, precision=lax.Precision.HIGHEST)
    return portion.astype(jnp.float32) * weights


def contract(left_rows, right_rows):
    return lax.dot_general(
        left_rows.astype(jnp.float32),
        right_rows,
        (((1,), (1,)), ((), ())),
        precision=lax.Precision.HIGHEST,
        preferred_element_type=jnp.float32,
    )


def on_device(jacobian, extinction, prior_var):
    tile_rows = jacobian.shape[0]
    band_count = lax.axis_size("wl")
    waves_total = extinction.shape[0]
    own_block = lax.axis_index("row") * band_count + lax.axis_index("wl")
    own_table = spectral_table(extinction, prior_var, own_block % waves_total)
    portion = lax.all_gather(jacobian, ("row", "wl"), axis=0, tiled=True)
    count = portion.shape[0]
    empty = jnp.zeros((tile_rows, count), jnp.float32)
    terms = lax.cond(
        jnp.int32(0) < (own_block + 1) * tile_rows,
        lambda: contract(jacobian, weigh_rows(portion, own_table, tile_rows)),
        lambda: empty,
    )
    summed = lax.psum_scatter(terms, "vox", scatter_dimension=1, tiled=True)
    width = summed.shape[1]
    rows_global = own_block * tile_rows + jnp.arange(tile_rows, dtype=jnp.int32)
    cols_global = lax.axis_index("vox") * width + jnp.arange(width, dtype=jnp.int32)
    return jnp.where(cols_global[None, :] <= rows_global[:, None], summed, jnp.float32(0.0))


def solution(mesh):
    return jax.shard_map(
        on_device,
        mesh=mesh,
        in_specs=(P(("row", "wl"), "vox"), P(), P(None, "vox")),
        out_specs=P(("row", "wl"), "vox"),
        check_vma=False,
    )
```

profile of v0, /device:TPU:0, one launch (start us, length us, event | category | flops | bytes accessed | tf_op | source)
XLA Modules:
  0.0 90.2 jit_solution(17142201387924977054)
XLA Ops:
  6.5 0.0 copy-start
  6.5 0.0 all-gather.2.cloned.1.call-start
  6.5 0.7 all-gather.2.cloned.1.call-update
  7.3 0.0 reduce-scatter.2.cloned.1.call-start
  7.3 0.9 dynamic-slice_reduce_fusion
  8.2 0.0 copy-done
  8.2 0.9 %fusion.12 = f32[4,640]{1,0:T(4,128)S(1)} fusion(f32[2,640]{1,0:T(2,128)S(1)} %copy-done, f32[4,2]{0,1:T(2,128)} %param.6, f32[2]{0:T(128)S(1)} %dynamic-slice_reduce_fusion), kind=kOutput, calls=%fused_computation.20 | convolution fusion | flops 61448 | bytes 15400 | tf_op jit(solution)/shard_map/dot_general | solution.py:9
  9.2 46.4 %all-gather.2.cloned.1.call-done = bf16[2048,640]{1,0:T(8,128)(2,1)} async-done(((bf16[128,640]{1,0:T(8,128)(2,1)}), bf16[2048,640]{1,0:T(8,128)(2,1)}) %all-gather.2.cloned.1.call-update) | async-done | bytes 2621456 | tf_op jit(solution)/shard_map/all_gather | solution.py:38
  55.6 5.3 %conditional.1 = (f32[128,2048]{0,1:T(8,128)S(1)}) conditional(s32[]{:T(128)} %convert_element_type.8, () %tuple.11, (bf16[2048,640]{1,0:T(8,128)(2,1)}, f32[4,640]{1,0:T(4,128)S(1)}, bf16[128,640]{1,0:T(8,128)(2,1)}) %tuple.12), branch_computations={%region_0.1_spmd, %region_1.2_spmd} | conditional | flops 2078849024 | bytes 25487424 | solution.py:41
  55.6 0.0 copy-start.1
  55.6 0.0 copy-start.2
  55.6 2.3 %fusion.6 = f32[2048,640]{1,0:T(8,128)S(1)} fusion(f32[4,640]{1,0:T(4,128)S(1)} %get-tuple-element.15, s32[2048]{0:T(1024)S(1)} %add_select_fusion), kind=kOutput, calls=%fused_computation.5 | convolution fusion | flops 62922752 | bytes 5261312 | tf_op jit(solution)/shard_map/cond/branch_1_fun/dot_general | solution.py:18
  57.9 0.0 copy-done.1
  57.9 0.0 copy-done.2
  58.0 3.0 %fusion.3 = f32[128,2048]{0,1:T(8,128)S(1)} fusion(bf16[128,640]{1,0:T(8,128)(2,1)S(1)} %copy-done.2, f32[2048,640]{1,0:T(8,128)S(1)} %fusion.6, bf16[2048,640]{1,0:T(8,128)(2,1)S(1)} %copy-done.1), kind=kOutput, calls=%fused_computation.3 | convolution fusion | flops 2015887360 | bytes 9076736 | tf_op jit(solution)/shard_map/cond/branch_1_fun/dot_general | solution.py:23
  60.9 1.3 %copy.4 = f32[128,2048]{1,0:T(8,128)} copy(f32[128,2048]{0,1:T(8,128)S(1)} %get-tuple-element.17) | data formatting | bytes 2097152 | tf_op jit(solution)/shard_map/cond | solution.py:41
  62.2 0.0 reduce-scatter.2.cloned.1.call-update
  62.3 19.1 %reduce-scatter.2.cloned.1.call-done = f32[128,1024]{1,0:T(8,128)} async-done(((f32[128,2048]{1,0:T(8,128)}), f32[128,1024]{1,0:T(8,128)}) %reduce-scatter.2.cloned.1.call-update) | async-done | bytes 524304 | tf_op jit(solution)/shard_map/reduce_scatter | solution.py:46
  81.4 1.9 %compare_select_fusion = f32[128,1024]{1,0:T(8,128)} fusion(f32[128,1024]{1,0:T(8,128)} %reduce-scatter.2.cloned.1.call-done, s32[1024]{0:T(1024)S(1)} %iota_add_fusion, s32[128]{0:T(128)S(1)} %iota_add_fusion.1), kind=kLoop, calls=%fused_computation.18 | loop fusion | flops 262144 | bytes 1053184 | tf_op jit(solution)/shard_map/jit(_where)/select_n | solution.py:50
  (3 shorter events, 0.0 us)
Async XLA Ops:
  6.5 1.7 %copy-start = (f32[2,640]{1,0:T(2,128)S(1)}, f32[2,640]{1,0:T(2,128)}, u32[]{:S(2)}) copy-start(f32[2,640]{1,0:T(2,128)} %param.7) | copy-start | bytes 15364
  6.5 49.0 %all-gather.2.cloned.1.call-start = ((), (), s32[]{:S(2)}) async-start(), calls=%async_computation.1 | async-start | bytes 2785280 | tf_op jit(solution)/shard_map/all_gather | solution.py:38
  7.3 74.1 %reduce-scatter.2.cloned.1.call-start = ((), (), s32[]{:S(2)}) async-start(), calls=%async_computation.2 | async-start | bytes 1572864 | tf_op jit(solution)/shard_map/reduce_scatter | solution.py:46
  55.6 2.4 %copy-start.1 = (bf16[2048,640]{1,0:T(8,128)(2,1)S(1)}, bf16[2048,640]{1,0:T(8,128)(2,1)}, u32[]{:S(2)}) copy-start(bf16[2048,640]{1,0:T(8,128)(2,1)} %get-tuple-element.14) | copy-start | bytes 7864324 | tf_op jit(solution)/shard_map/cond
  55.6 2.4 %copy-start.2 = (bf16[128,640]{1,0:T(8,128)(2,1)S(1)}, bf16[128,640]{1,0:T(8,128)(2,1)}, u32[]{:S(2)}) copy-start(bf16[128,640]{1,0:T(8,128)(2,1)} %get-tuple-element.16) | copy-start | bytes 491524 | tf_op jit(solution)/shard_map/cond
Sparse Core Ops, SparseCore 0:
  9.6 45.8 all-gather.1
  62.4 18.9 reduce-scatter.1
where the time goes:
time: 90.4 us; the launch traced here: 90.2 us
  waiting for transfers between devices  66.2 us (73%)
  between operations  13.5 us (15%)
  matrix products  6.24 us (7%)
  local copies, waits for them, and re-layouts  2.19 us (2%)
  other arithmetic  1.95 us (2%)
    all_gather x1, waiting for transfers between devices, on_device(): portion = lax.all_gather(jacobian, ('row', 'wl'), axis=0, tiled=True)  46.4 us
    reduce_scatter x1, waiting for transfers between devices, on_device(): summed = lax.psum_scatter(terms, 'vox', scatter_dimension=1, tiled=True)  19.1 us
    dot_general x1, matrix products, contract(): lax.dot_general(left_rows.astype(jnp.float32), right_rows, (((1,), (1,)),...  2.96 us
    dot_general x1, matrix products, weigh_rows(): weights = jnp.dot(onehot, table, precision=lax.Precision.HIGHEST)  2.34 us
    select_n x1, other arithmetic, on_device(): jnp.where(cols_global[None, :] <= rows_global[:, None], summed, jnp.float...  1.94 us
  transfers between devices with their start and end apart: 2, of which 2 were waited for; matrix products, arithmetic and copies ran while one was open for 2% of the time, Pallas kernels for 0%

commit v1 on v0

v1 whole, which is shorter than its diff:
```python
import functools

import jax
import jax.numpy as jnp
import numpy as np
from jax import lax
from jax.experimental import pallas as pl
from jax.experimental.pallas import tpu as pltpu
from jax.sharding import PartitionSpec as P


def shift(x, axis, by):
    size = lax.axis_size(axis)
    return lax.ppermute(x, axis, [(i, (i + by) % size) for i in range(size)])


def swap(x, axis, bit):
    size = lax.axis_size(axis)
    return lax.ppermute(x, axis, [(i, i ^ bit) for i in range(size)])


def plan(vox, levels):
    slots = levels // vox
    ready = [0, 1] + list(range(3, levels + 1))
    ready[levels - 1] = 2
    slot = np.zeros((vox, levels, slots), np.int32)
    dist = np.zeros((vox, levels, slots), np.int32)
    for v in range(vox):
        for z in range(levels):
            ds = [z - (v * slots + s) for s in range(slots)]
            order = sorted(range(slots), key=lambda s: (ready[max(ds[s], 0)], s))
            slot[v, z] = order
            dist[v, z] = [max(ds[s], 0) for s in order]
    return slot, dist


def pick(pieces, dist, v, z, phase):
    here = jnp.asarray(dist[:, :, phase])[v, z]
    used = sorted(set(dist[:, :, phase].ravel().tolist()))
    out = pieces[used[0]]
    for d in used[1:]:
        out = jnp.where(here == d, pieces[d], out)
    return out


def place_kernel(count, where_ref, *refs):
    blocks, out_ref = refs[:count], refs[count]
    tile = blocks[0].shape[0]
    rows = where_ref[count] + lax.broadcasted_iota(jnp.int32, (tile, tile), 0)
    for k in range(count):
        at = pl.multiple_of(where_ref[k] * tile, tile)
        cols = where_ref[count + 1] + at + lax.broadcasted_iota(jnp.int32, (tile, tile), 1)
        out_ref[:, pl.ds(at, tile)] = jnp.where(cols <= rows, blocks[k][...], 0.0)


def place(blocks, where):
    tile = blocks[0].shape[0]
    return pl.pallas_call(
        functools.partial(place_kernel, len(blocks)),
        out_shape=jax.ShapeDtypeStruct((tile, tile * len(blocks)), jnp.float32),
        in_specs=[pl.BlockSpec(memory_space=pltpu.SMEM)]
        + [pl.BlockSpec(memory_space=pltpu.VMEM)] * len(blocks),
        out_specs=pl.BlockSpec(memory_space=pltpu.VMEM),
    )(where, *blocks)


def on_device(jac, extinction, prior_var):
    tile = jac.shape[0]
    vox, levels, lines = (lax.axis_size(a) for a in ("vox", "row", "wl"))
    v, z, w = (lax.axis_index(a) for a in ("vox", "row", "wl"))
    slots = levels // vox
    slot, dist = plan(vox, levels)

    pieces = {0: jac}
    for d in [1, levels - 1] + list(range(2, levels - 1)):
        if d not in pieces and d > 0:
            near = d in (1, levels - 1)
            pieces[d] = shift(jac if near else pieces[d - 1], "row", d if near else 1)

    halves = [jac] + [shift(jac, "vox", -t) for t in range(1, vox)]
    priors = [prior_var] + [shift(prior_var, "vox", -t) for t in range(1, vox)]
    rows = []
    for half in halves:
        got = {0: half}
        bit = lines // 2
        while bit:
            got.update({d ^ bit: swap(x, "wl", bit) for d, x in list(got.items())})
            bit //= 2
        rows.append(got)

    waves = extinction.shape[0]
    mine = extinction[w % waves]
    high, low = [], []
    for t in range(vox):
        for d in range(lines):
            coeff = extinction[(w ^ d) % waves] * mine
            weight = jnp.sum(coeff[:, None] * priors[t], axis=0)
            scaled = rows[t][d].astype(jnp.float32) * weight[None, :]
            top = lax.reduce_precision(scaled, 8, 7)
            high.append(top.astype(jnp.bfloat16))
            low.append((scaled - top).astype(jnp.bfloat16))

    blocks, where = [], []
    for phase in range(slots):
        total = None
        for t in range(vox):
            if t == 0:
                cols = pick(pieces, dist, v, z, phase)
            else:
                cols = pick(pieces, dist, (v - t) % vox, z, phase)
                cols = shift(cols, "vox", -t)
            for part in (high, low):
                left = jnp.concatenate(part[t * lines : (t + 1) * lines], axis=0)
                term = lax.dot_general(
                    left, cols, (((1,), (1,)), ((), ())), preferred_element_type=jnp.float32
                )
                total = term if total is None else total + term
        for d in range(lines):
            block = total[d * tile : (d + 1) * tile]
            blocks.append(block if d == 0 else swap(block, "wl", d))
            where.append(jnp.asarray(slot[:, :, phase])[v, z] * lines + (w ^ d))
    where += [(z * lines + w) * tile, v * slots * lines * tile]
    return place(blocks, jnp.stack(where).astype(jnp.int32))


def solution(mesh):
    return jax.shard_map(
        on_device,
        mesh=mesh,
        in_specs=(P(("row", "wl"), "vox"), P(), P(None, "vox")),
        out_specs=P(("row", "wl"), "vox"),
        check_vma=False,
    )
```

time: 90.4 us -> 53.6 us (0.59)
  waiting for transfers between devices: 66.2 us -> 17.9 us
  starting transfers between devices: 0.04 us -> 15.3 us
  between operations: 13.5 us -> 6.83 us
  matrix products: 6.24 us -> 2.67 us
  local copies, waits for them, and re-layouts: 2.19 us -> 5.17 us
  Pallas kernels: 0 us -> 1.95 us
  other arithmetic: 1.95 us -> 3.35 us
    all_gather x1 -> x0, waiting for transfers between devices: 46.4 us -> none  [on_device(): portion = lax.all_gather(jacobian, ('row', 'wl'), axis=0, tiled=True)]
    reduce_scatter x1 -> x0, waiting for transfers between devices: 19.1 us -> none  [on_device(): summed = lax.psum_scatter(terms, 'vox', scatter_dimension=1, tiled=True)]
    ppermute x0 -> x19, waiting for transfers between devices: none -> 17.9 us  [the longest x7 16.5 us: shift(): return lax.ppermute(x, axis, [(i, (i + by) % size) for i in range(size)])]
    ppermute x0 -> x19, starting transfers between devices: none -> 15.3 us  [the longest x7 9.29 us: shift(): return lax.ppermute(x, axis, [(i, (i + by) % size) for i in range(size)])]
    dot_general x3 -> x8, matrix products: 6.24 us -> 2.67 us  [on_device(): lax.dot_general(left, cols, (((1,), (1,)), ((), ())), preferred_element_t...]
    pallas_call x0 -> x1, Pallas kernels: none -> 1.95 us  [place(): pl.pallas_call(functools.partial(place_kernel, len(blocks)), out_shape=ja...]
    select_n x2 -> x1, other arithmetic: 1.94 us -> 0.09 us  [pick(): out = jnp.where(here == d, pieces[d], out)]
    dynamic_slice x1 -> x3, local copies, waits for them, and re-layouts: 0.87 us -> 2.6 us  [the longest x1 1.42 us: pick(): here = jnp.asarray(dist[:, :, phase])[v, z]]
  transfers between devices with their start and end apart: 2 -> 19, of which waited for: 2 -> 6; matrix products, arithmetic and copies ran while one was open for 2% -> 20% of each run, Pallas kernels for 0% -> 0%
where the time goes in v1:
time: 53.6 us; the launch traced here: 53.2 us
  waiting for transfers between devices  17.9 us (33%)
  starting transfers between devices  15.3 us (29%)
  between operations  6.83 us (13%)
  local copies, waits for them, and re-layouts  5.17 us (10%)
  other arithmetic  3.35 us (6%)
  matrix products  2.67 us (5%)
  Pallas kernels  1.95 us (4%)
    ppermute x7, waiting for transfers between devices, shift(): return lax.ppermute(x, axis, [(i, (i + by) % size) for i in range(size)])  16.5 us
    ppermute x7, starting transfers between devices, shift(): return lax.ppermute(x, axis, [(i, (i + by) % size) for i in range(size)])  9.29 us
    ppermute x12, starting transfers between devices, swap(): return lax.ppermute(x, axis, [(i, i ^ bit) for i in range(size)])  6.05 us
    dot_general x8, matrix products, on_device(): lax.dot_general(left, cols, (((1,), (1,)), ((), ())), preferred_element_t...  2.67 us
    pallas_call x1, Pallas kernels, place(): pl.pallas_call(functools.partial(place_kernel, len(blocks)), out_shape=ja...  1.95 us
    ppermute x12, waiting for transfers between devices, swap(): return lax.ppermute(x, axis, [(i, i ^ bit) for i in range(size)])  1.45 us
    dynamic_slice x1, local copies, waits for them, and re-layouts, pick(): here = jnp.asarray(dist[:, :, phase])[v, z]  1.42 us
    convert_element_type x8, other arithmetic, on_device(): high.append(top.astype(jnp.bfloat16))  1.4 us
  transfers between devices with their start and end apart: 19, of which 6 were waited for; matrix products, arithmetic and copies ran while one was open for 20% of the time, Pallas kernels for 0%

profile of v1, /device:TPU:0, one launch (start us, length us, event | category | flops | bytes accessed | tf_op | source)
XLA Modules:
  0.0 53.2 jit_solution(16515955562354976940)
XLA Ops:
  0.0 3.0 %collective-permute-start.4 = (bf16[128,640]{1,0:T(8,128)(2,1)}, bf16[128,640]{1,0:T(8,128)(2,1)S(1)}, u32[]{:S(2)}, u32[]{:S(2)}) collective-permute-start(bf16[128,640]{1,0:T(8,128)(2,1)} %param.15), channel_id=1, source_target_pairs={{0,4},{4,8},{8,12},{12,0},{1,5},{5,9},{9,13},{13,1},{2,6},{6,10},{... | collective-permute-start | bytes 491528 | tf_op jit(solution)/shard_map/ppermute | solution.py:14
  3.0 2.0 %collective-permute-start.3 = (bf16[128,640]{1,0:T(8,128)(2,1)}, bf16[128,640]{1,0:T(8,128)(2,1)S(1)}, u32[]{:S(2)}, u32[]{:S(2)}) collective-permute-start(bf16[128,640]{1,0:T(8,128)(2,1)} %param.15), channel_id=1, source_target_pairs={{0,12},{4,0},{8,4},{12,8},{1,13},{5,1},{9,5},{13,9},{2,14},{6,2},{... | collective-permute-start | bytes 491528 | tf_op jit(solution)/shard_map/ppermute | solution.py:14
  5.1 1.7 %collective-permute-start.1 = (bf16[128,640]{1,0:T(8,128)(2,1)}, bf16[128,640]{1,0:T(8,128)(2,1)S(1)}, u32[]{:S(2)}, u32[]{:S(2)}) collective-permute-start(bf16[128,640]{1,0:T(8,128)(2,1)} %param.15), channel_id=1, source_target_pairs={{0,2},{1,3},{2,0},{3,1},{4,6},{5,7},{6,4},{7,5},{8,10},{9,11},{10,... | collective-permute-start | bytes 491528 | tf_op jit(solution)/shard_map/ppermute | solution.py:19
  6.8 0.0 collective-permute-start
  6.8 1.5 %collective-permute-start.6 = (f32[2,640]{1,0:T(2,128)}, f32[2,640]{1,0:T(2,128)S(1)}, u32[]{:S(2)}, u32[]{:S(2)}) collective-permute-start(f32[2,640]{1,0:T(2,128)} %param.17), channel_id=1, source_target_pairs={{0,16},{16,0},{1,17},{17,1},{2,18},{18,2},{3,19},{19,3},{4,20},{20... | collective-permute-start | bytes 15368 | tf_op jit(solution)/shard_map/ppermute | solution.py:14
  8.3 1.4 %fusion.28 = (s32[1,1]{1,0:T(1,128)}, s32[1,1]{1,0:T(1,128)}, s32[1,1]{1,0:T(1,128)}, s32[1,1]{1,0:T(1,128)}) fusion(s32[2,4]{1,0:T(2,128)} %constant.102.clone, s32[]{:T(128)S(6)} %select_n.132, s32[]{:T(128)S(6)} %select_n.133, s32[]{:T(128)S(6)} %select_n.147, s32[2,4]{1,0:T(2,128)} %constant.100.clone), kind=kLoop, calls=%fused_computation.75 | loop fusion | bytes 44 | tf_op jit(solution)/shard_map/dynamic_slice | solution.py:38
  14.9 1.0 %multiply_reduce_fusion.11 = (f32[2]{0:T(128)S(1)}, f32[2]{0:T(128)S(1)}, f32[2]{0:T(128)S(1)}, f32[2]{0:T(128)S(1)}) fusion(f32[4,2]{0,1:T(2,128)} %param.16, s32[]{:T(128)S(6)} %select_n.135, s32[]{:T(128)S(6)} %select_n.137, s32[]{:T(128)S(6)} %select_n.141, s32[]{:T(128)S(6)} %select_n.139), kind=kLoop, calls=%fused_computation.63 | loop fusion | flops 8 | bytes 80 | tf_op jit(solution)/shard_map/mul | solution.py:96
  16.0 0.0 collective-permute-done.6
  16.0 0.6 %collective-permute-start.5 = (bf16[128,640]{1,0:T(8,128)(2,1)}, bf16[128,640]{1,0:T(8,128)(2,1)S(1)}, u32[]{:S(2)}, u32[]{:S(2)}) collective-permute-start(bf16[128,640]{1,0:T(8,128)(2,1)} %param.15), channel_id=1, source_target_pairs={{0,16},{16,0},{1,17},{17,1},{2,18},{18,2},{3,19},{19,3},{4,20},{20... | collective-permute-start | bytes 491528 | tf_op jit(solution)/shard_map/ppermute | solution.py:14
  16.6 0.8 %multiply_reduce_fusion.3 = (f32[640]{0:T(1024)S(1)}, f32[640]{0:T(1024)S(1)}, f32[640]{0:T(1024)S(1)}, f32[640]{0:T(1024)S(1)}, f32[640]{0:T(1024)S(1)}, /*inde...) fusion(f32[2,640]{1,0:T(2,128)S(1)} %collective-permute-done.6, f32[2]{0:T(128)S(1)} %get-tuple-element.17, ...), kind=kLoop, calls=%fused_computation.55 | loop fusion | flops 15360 | bytes 30752 | tf_op jit(solution)/shard_map/reduce_sum | solution.py:97
  17.4 1.0 %reduce-precision_convert_fusion.7 = (bf16[128,640]{1,0:T(8,128)(2,1)S(1)}, bf16[128,640]{1,0:T(8,128)(2,1)S(1)}) fusion(bf16[128,640]{1,0:T(8,128)(2,1)} %param.15, f32[640]{0:T(1024)S(1)} %get-tuple-element.16), kind=kLoop, calls=%fused_computation.25 | loop fusion | flops 491520 | bytes 494080 | tf_op jit(solution)/shard_map/convert_element_type | solution.py:100
  18.4 0.0 collective-permute-done.1
  18.4 0.1 collective-permute-start.2
  18.5 4.1 %collective-permute-done.5 = bf16[128,640]{1,0:T(8,128)(2,1)S(1)} collective-permute-done((bf16[128,640]{1,0:T(8,128)(2,1)}, bf16[128,640]{1,0:T(8,128)(2,1)S(1)}, u32[]{:S(2)}, u32[]{:S(2)}) %collective-permute-start.5) | collective-permute-done | bytes 163872 | tf_op jit(solution)/shard_map/ppermute | solution.py:14
  22.6 0.5 collective-permute-start.8
  23.1 0.1 reduce-precision_convert_fusion.3
  23.1 0.0 copy-start
  23.2 0.1 reduce-precision_convert_fusion.5
  23.2 0.0 collective-permute-done.4
  23.2 0.1 collective-permute-start.7
  23.3 0.0 collective-permute-done
  23.3 0.1 collective-permute-start.14
  23.4 0.1 reduce-precision_convert_fusion.6
  23.5 0.0 collective-permute-done.3
  23.5 8.2 %collective-permute-done.14 = bf16[128,640]{1,0:T(8,128)(2,1)S(1)} collective-permute-done((bf16[128,640]{1,0:T(8,128)(2,1)S(1)}, bf16[128,640]{1,0:T(8,128)(2,1)S(1)}, u32[]{:S(2)}, u32[]{:S(2)}) %collective-permute-start.14) | collective-permute-done | bytes 163872 | tf_op jit(solution)/shard_map/ppermute | solution.py:14
  31.7 0.1 select_select_fusion.1
  31.8 0.4 collective-permute-start.15
  32.2 1.7 %collective-permute-start.10 = (bf16[128,640]{1,0:T(8,128)(2,1)S(1)}, bf16[128,640]{1,0:T(8,128)(2,1)S(1)}, u32[]{:S(2)}, u32[]{:S(2)}) collective-permute-start(bf16[128,640]{1,0:T(8,128)(2,1)S(1)} %get-tuple-element.25), channel_id=1, source_target_pairs={{0,16},{16,0},{1,17},{17,1},{2,18},{18,2},{3,19},{19,3},{4,20},{20... | collective-permute-start | bytes 491528 | tf_op jit(solution)/shard_map/ppermute | solution.py:14
  33.9 0.0 collective-permute-start.9
  33.9 0.1 reduce-precision_convert_fusion.1
  34.0 0.0 collective-permute-done.2
  34.0 0.1 reduce-precision_convert_fusion.4
  34.1 0.3 fusion.16
  34.4 0.0 collective-permute-done.7
  34.4 0.1 reduce-precision_convert_fusion.2
  34.5 0.3 fusion.17
  34.8 0.5 collective-permute-done.9
  35.3 0.1 reduce-precision_convert_fusion
  35.4 3.6 %collective-permute-done.15 = bf16[128,640]{1,0:T(8,128)(2,1)S(1)} collective-permute-done((bf16[128,640]{1,0:T(8,128)(2,1)S(1)}, bf16[128,640]{1,0:T(8,128)(2,1)S(1)}, u32[]{:S(2)}, u32[]{:S(2)}) %collective-permute-start.15) | collective-permute-done | bytes 163872 | tf_op jit(solution)/shard_map/ppermute | solution.py:14
  39.0 0.3 fusion.14
  39.3 0.3 fusion.12
  39.7 0.3 fusion.3
  40.0 0.6 %fusion.26 = (f32[128,128]{1,0:T(8,128)S(1)}, f32[128,128]{1,0:T(8,128)S(1)}, f32[128,128]{1,0:T(8,128)S(1)}, f32[128,128]{1,0:T(8,128)}) fusion(f32[512,128]{1,0:T(8,128)S(1)} %fusion.3), kind=kLoop, calls=%fused_computation.73 | loop fusion | bytes 524288 | tf_op jit(solution)/shard_map/slice | solution.py:119
  40.7 0.5 collective-permute-done.10
  41.1 0.3 fusion.15
  41.5 0.3 fusion.13
  41.8 0.3 fusion.1
  42.2 0.0 copy-start.8
  42.2 0.0 copy-start.7
  42.2 0.6 %fusion.27 = (f32[128,128]{1,0:T(8,128)S(1)}, f32[128,128]{1,0:T(8,128)S(1)}, f32[128,128]{1,0:T(8,128)S(1)}, f32[128,128]{1,0:T(8,128)}) fusion(f32[512,128]{1,0:T(8,128)S(1)} %fusion.1), kind=kLoop, calls=%fused_computation.74 | loop fusion | bytes 524288 | tf_op jit(solution)/shard_map/slice | solution.py:119
  42.8 1.5 %collective-permute-start.17 = (f32[128,128]{1,0:T(8,128)S(1)}, f32[128,128]{1,0:T(8,128)S(1)}, u32[]{:S(2)}, u32[]{:S(2)}) collective-permute-start(f32[128,128]{1,0:T(8,128)S(1)} %get-tuple-element.28), channel_id=1, source_target_pairs={{0,2},{1,3},{2,0},{3,1},{4,6},{5,7},{6,4},{7,5},{8,10},{9,11},{10,... | collective-permute-start | bytes 196616 | tf_op jit(solution)/shard_map/ppermute | solution.py:19
  44.4 1.0 %collective-permute-start.13 = (f32[128,128]{1,0:T(8,128)S(1)}, f32[128,128]{1,0:T(8,128)S(1)}, u32[]{:S(2)}, u32[]{:S(2)}) collective-permute-start(f32[128,128]{1,0:T(8,128)S(1)} %get-tuple-element.31), channel_id=1, source_target_pairs={{0,3},{1,2},{2,1},{3,0},{4,7},{5,6},{6,5},{7,4},{8,11},{9,10},{10,... | collective-permute-start | bytes 196616 | tf_op jit(solution)/shard_map/ppermute | solution.py:19
  45.3 1.1 %collective-permute-start.12 = (f32[128,128]{1,0:T(8,128)S(1)}, f32[128,128]{1,0:T(8,128)S(1)}, u32[]{:S(2)}, u32[]{:S(2)}) collective-permute-start(f32[128,128]{1,0:T(8,128)S(1)} %get-tuple-element.32), channel_id=1, source_target_pairs={{0,2},{1,3},{2,0},{3,1},{4,6},{5,7},{6,4},{7,5},{8,10},{9,11},{10,... | collective-permute-start | bytes 196616 | tf_op jit(solution)/shard_map/ppermute | solution.py:19
  46.5 0.0 collective-permute-done.18.refs_7_
  46.5 0.0 collective-permute-start.11
  46.5 0.6 %dynamic_slice.57 = s32[1,1]{1,0:T(1,128)} dynamic-slice(s32[2,4]{1,0:T(2,128)S(1)} %copy-done.8, s32[]{:T(128)S(6)} %select_n.132, s32[]{:T(128)S(6)} %select_n.133), dynamic_slice_sizes={1,1} | dynamic-slice | bytes 12 | tf_op jit(solution)/shard_map/dynamic_slice | solution.py:121
  47.8 0.6 %dynamic_slice.53 = s32[1,1]{1,0:T(1,128)} dynamic-slice(s32[2,4]{1,0:T(2,128)S(1)} %copy-done.7, s32[]{:T(128)S(6)} %select_n.132, s32[]{:T(128)S(6)} %select_n.133), dynamic_slice_sizes={1,1} | dynamic-slice | bytes 12 | tf_op jit(solution)/shard_map/dynamic_slice | solution.py:121
  49.0 0.6 %stack.43.where_ref = s32[10]{0:T(128)} concatenate(s32[1]{0:T(128)} %bitcast.1, s32[1]{0:T(128)} %bitcast.2, s32[1]{0:T(128)} %bitcast.3, s32[1]{0:T(128)} %bitcast.4, s32[1]{0:T(128)} %bitcast.6, s32[1]{0:T(128)} %bitcast.7, s32[1]{0:T(128)} %bitcast.8, s32[1]{0:T(128)} %bitcast.9, s32[1]{0:T(128)} %bitcast.10, s32[1]{0:T(128)} %bitcast.11), dimensions={0} | concatenate | bytes 80 | tf_op jit(solution)/shard_map/stack | solution.py:123
  49.6 0.0 collective-permute-done.16.refs_5_
  49.7 0.0 collective-permute-done.13.refs_3_
  49.7 0.9 %collective-permute-done.12.refs_2_ = f32[128,128]{1,0:T(8,128)S(1)} collective-permute-done((f32[128,128]{1,0:T(8,128)S(1)}, f32[128,128]{1,0:T(8,128)S(1)}, u32[]{:S(2)}, u32[]{:S(2)}) %collective-permute-start.12) | collective-permute-done | bytes 65568 | tf_op jit(solution)/shard_map/ppermute | solution.py:19
  50.7 0.6 %copy-done.5 = f32[128,128]{1,0:T(8,128)} copy-done((f32[128,128]{1,0:T(8,128)}, f32[128,128]{1,0:T(8,128)S(1)}, u32[]{:S(2)}) %copy-start.5) | copy-done | bytes 65560
  51.2 0.1 copy-done.6
  51.3 1.9 %shard_map.145 = f32[128,1024]{1,0:T(8,128)} custom-call(s32[10]{0:T(128)} %stack.43.where_ref, f32[128,128]{1,0:T(8,128)} %get-tuple-element.34.refs_0_, f32[128,128]{1,0:T(8,128)} %copy-done.6, f32[128,128]{1,0:T(8,128)} %copy-done.5, f32[128,128]{1,0:T(8,128)} %copy-done.4, f32[128,128]{1,0:T(8,128)} %get-tuple-element.30.refs_4_, f32[128,128]{1,0:T(8,128)} %copy-done.3, ...), custom_call_target="tpu_custom_call" | custom-call | tf_op jit(solution)/shard_map/pallas_call | solution.py:58
  (18 shorter events, 0.0 us)
Async XLA Ops:
  0.0 23.2 %collective-permute-start.4 = (bf16[128,640]{1,0:T(8,128)(2,1)}, bf16[128,640]{1,0:T(8,128)(2,1)S(1)}, u32[]{:S(2)}, u32[]{:S(2)}) collective-permute-start(bf16[128,640]{1,0:T(8,128)(2,1)} %param.15), channel_id=1, source_target_pairs={{0,4},{4,8},{8,12},{12,0},{1,5},{5,9},{9,13},{13,1},{2,6},{6,10},{... | collective-permute-start | bytes 491528 | tf_op jit(solution)/shard_map/ppermute | solution.py:14
  3.0 20.4 %collective-permute-start.3 = (bf16[128,640]{1,0:T(8,128)(2,1)}, bf16[128,640]{1,0:T(8,128)(2,1)S(1)}, u32[]{:S(2)}, u32[]{:S(2)}) collective-permute-start(bf16[128,640]{1,0:T(8,128)(2,1)} %param.15), channel_id=1, source_target_pairs={{0,12},{4,0},{8,4},{12,8},{1,13},{5,1},{9,5},{13,9},{2,14},{6,2},{... | collective-permute-start | bytes 491528 | tf_op jit(solution)/shard_map/ppermute | solution.py:14
  5.1 13.3 %collective-permute-start.1 = (bf16[128,640]{1,0:T(8,128)(2,1)}, bf16[128,640]{1,0:T(8,128)(2,1)S(1)}, u32[]{:S(2)}, u32[]{:S(2)}) collective-permute-start(bf16[128,640]{1,0:T(8,128)(2,1)} %param.15), channel_id=1, source_target_pairs={{0,2},{1,3},{2,0},{3,1},{4,6},{5,7},{6,4},{7,5},{8,10},{9,11},{10,... | collective-permute-start | bytes 491528 | tf_op jit(solution)/shard_map/ppermute | solution.py:19
  6.8 16.5 %collective-permute-start = (bf16[128,640]{1,0:T(8,128)(2,1)}, bf16[128,640]{1,0:T(8,128)(2,1)S(1)}, u32[]{:S(2)}, u32[]{:S(2)}) collective-permute-start(bf16[128,640]{1,0:T(8,128)(2,1)} %param.15), channel_id=1, source_target_pairs={{0,1},{1,0},{2,3},{3,2},{4,5},{5,4},{6,7},{7,6},{8,9},{9,8},{10,11... | collective-permute-start | bytes 491528 | tf_op jit(solution)/shard_map/ppermute | solution.py:19
  6.8 9.2 %collective-permute-start.6 = (f32[2,640]{1,0:T(2,128)}, f32[2,640]{1,0:T(2,128)S(1)}, u32[]{:S(2)}, u32[]{:S(2)}) collective-permute-start(f32[2,640]{1,0:T(2,128)} %param.17), channel_id=1, source_target_pairs={{0,16},{16,0},{1,17},{17,1},{2,18},{18,2},{3,19},{19,3},{4,20},{20... | collective-permute-start | bytes 15368 | tf_op jit(solution)/shard_map/ppermute | solution.py:14
  16.0 6.6 %collective-permute-start.5 = (bf16[128,640]{1,0:T(8,128)(2,1)}, bf16[128,640]{1,0:T(8,128)(2,1)S(1)}, u32[]{:S(2)}, u32[]{:S(2)}) collective-permute-start(bf16[128,640]{1,0:T(8,128)(2,1)} %param.15), channel_id=1, source_target_pairs={{0,16},{16,0},{1,17},{17,1},{2,18},{18,2},{3,19},{19,3},{4,20},{20... | collective-permute-start | bytes 491528 | tf_op jit(solution)/shard_map/ppermute | solution.py:14
  18.4 15.6 %collective-permute-start.2 = (bf16[128,640]{1,0:T(8,128)(2,1)S(1)}, bf16[128,640]{1,0:T(8,128)(2,1)S(1)}, u32[]{:S(2)}, u32[]{:S(2)}) collective-permute-start(bf16[128,640]{1,0:T(8,128)(2,1)S(1)} %collective-permute-done.1), channel_id=1, source_target_pairs={{0,1},{1,0},{2,3},{3,2},{4,5},{5,4},{6,7},{7,6},{8,9},{9,8},{10,11... | collective-permute-start | bytes 491528 | tf_op jit(solution)/shard_map/ppermute | solution.py:19
  22.6 11.3 %collective-permute-start.8 = (bf16[128,640]{1,0:T(8,128)(2,1)S(1)}, bf16[128,640]{1,0:T(8,128)(2,1)S(1)}, u32[]{:S(2)}, u32[]{:S(2)}) collective-permute-start(bf16[128,640]{1,0:T(8,128)(2,1)S(1)} %collective-permute-done.5), channel_id=1, source_target_pairs={{0,2},{1,3},{2,0},{3,1},{4,6},{5,7},{6,4},{7,5},{8,10},{9,11},{10,... | collective-permute-start | bytes 491528 | tf_op jit(solution)/shard_map/ppermute | solution.py:19
  23.1 8.6 %copy-start = (bf16[128,640]{1,0:T(8,128)(2,1)S(1)}, bf16[128,640]{1,0:T(8,128)(2,1)}, u32[]{:S(2)}) copy-start(bf16[128,640]{1,0:T(8,128)(2,1)} %param.15) | copy-start | bytes 491524
  23.2 11.2 %collective-permute-start.7 = (bf16[128,640]{1,0:T(8,128)(2,1)S(1)}, bf16[128,640]{1,0:T(8,128)(2,1)S(1)}, u32[]{:S(2)}, u32[]{:S(2)}) collective-permute-start(bf16[128,640]{1,0:T(8,128)(2,1)S(1)} %collective-permute-done.5), channel_id=1, source_target_pairs={{0,1},{1,0},{2,3},{3,2},{4,5},{5,4},{6,7},{7,6},{8,9},{9,8},{10,11... | collective-permute-start | bytes 491528 | tf_op jit(solution)/shard_map/ppermute | solution.py:19
  23.3 8.4 %collective-permute-start.14 = (bf16[128,640]{1,0:T(8,128)(2,1)S(1)}, bf16[128,640]{1,0:T(8,128)(2,1)S(1)}, u32[]{:S(2)}, u32[]{:S(2)}) collective-permute-start(bf16[128,640]{1,0:T(8,128)(2,1)S(1)} %collective-permute-done.4), channel_id=1, source_target_pairs={{0,4},{4,8},{8,12},{12,0},{1,5},{5,9},{9,13},{13,1},{2,6},{6,10},{... | collective-permute-start | bytes 491528 | tf_op jit(solution)/shard_map/ppermute | solution.py:14
  31.8 7.2 %collective-permute-start.15 = (bf16[128,640]{1,0:T(8,128)(2,1)S(1)}, bf16[128,640]{1,0:T(8,128)(2,1)S(1)}, u32[]{:S(2)}, u32[]{:S(2)}) collective-permute-start(bf16[128,640]{1,0:T(8,128)(2,1)S(1)} %get-tuple-element.22), channel_id=1, source_target_pairs={{0,16},{16,0},{1,17},{17,1},{2,18},{18,2},{3,19},{19,3},{4,20},{20... | collective-permute-start | bytes 491528 | tf_op jit(solution)/shard_map/ppermute | solution.py:14
  32.2 8.9 %collective-permute-start.10 = (bf16[128,640]{1,0:T(8,128)(2,1)S(1)}, bf16[128,640]{1,0:T(8,128)(2,1)S(1)}, u32[]{:S(2)}, u32[]{:S(2)}) collective-permute-start(bf16[128,640]{1,0:T(8,128)(2,1)S(1)} %get-tuple-element.25), channel_id=1, source_target_pairs={{0,16},{16,0},{1,17},{17,1},{2,18},{18,2},{3,19},{19,3},{4,20},{20... | collective-permute-start | bytes 491528 | tf_op jit(solution)/shard_map/ppermute | solution.py:14
  33.9 1.4 %collective-permute-start.9 = (bf16[128,640]{1,0:T(8,128)(2,1)S(1)}, bf16[128,640]{1,0:T(8,128)(2,1)S(1)}, u32[]{:S(2)}, u32[]{:S(2)}) collective-permute-start(bf16[128,640]{1,0:T(8,128)(2,1)S(1)} %collective-permute-done.8), channel_id=1, source_target_pairs={{0,1},{1,0},{2,3},{3,2},{4,5},{5,4},{6,7},{7,6},{8,9},{9,8},{10,11... | collective-permute-start | bytes 491528 | tf_op jit(solution)/shard_map/ppermute | solution.py:19
  40.7 5.8 %collective-permute-start.18 = (f32[128,128]{1,0:T(8,128)S(1)}, f32[128,128]{1,0:T(8,128)S(1)}, u32[]{:S(2)}, u32[]{:S(2)}) collective-permute-start(f32[128,128]{1,0:T(8,128)S(1)} %get-tuple-element.27), channel_id=1, source_target_pairs={{0,3},{1,2},{2,1},{3,0},{4,7},{5,6},{6,5},{7,4},{8,11},{9,10},{10,... | collective-permute-start | bytes 196616 | tf_op jit(solution)/shard_map/ppermute | solution.py:19
  42.2 4.3 %copy-start.8 = (s32[2,4]{1,0:T(2,128)S(1)}, s32[2,4]{1,0:T(2,128)}, u32[]{:S(2)}) copy-start(s32[2,4]{1,0:T(2,128)} %constant.103.clone) | copy-start | bytes 100
  42.2 5.6 %copy-start.7 = (s32[2,4]{1,0:T(2,128)S(1)}, s32[2,4]{1,0:T(2,128)}, u32[]{:S(2)}) copy-start(s32[2,4]{1,0:T(2,128)} %constant.101.clone) | copy-start | bytes 100
  42.8 6.8 %collective-permute-start.17 = (f32[128,128]{1,0:T(8,128)S(1)}, f32[128,128]{1,0:T(8,128)S(1)}, u32[]{:S(2)}, u32[]{:S(2)}) collective-permute-start(f32[128,128]{1,0:T(8,128)S(1)} %get-tuple-element.28), channel_id=1, source_target_pairs={{0,2},{1,3},{2,0},{3,1},{4,6},{5,7},{6,4},{7,5},{8,10},{9,11},{10,... | collective-permute-start | bytes 196616 | tf_op jit(solution)/shard_map/ppermute | solution.py:19
  44.3 5.3 %collective-permute-start.16 = (f32[128,128]{1,0:T(8,128)S(1)}, f32[128,128]{1,0:T(8,128)S(1)}, u32[]{:S(2)}, u32[]{:S(2)}) collective-permute-start(f32[128,128]{1,0:T(8,128)S(1)} %get-tuple-element.29), channel_id=1, source_target_pairs={{0,1},{1,0},{2,3},{3,2},{4,5},{5,4},{6,7},{7,6},{8,9},{9,8},{10,11... | collective-permute-start | bytes 196616 | tf_op jit(solution)/shard_map/ppermute | solution.py:19
  44.4 5.3 %collective-permute-start.13 = (f32[128,128]{1,0:T(8,128)S(1)}, f32[128,128]{1,0:T(8,128)S(1)}, u32[]{:S(2)}, u32[]{:S(2)}) collective-permute-start(f32[128,128]{1,0:T(8,128)S(1)} %get-tuple-element.31), channel_id=1, source_target_pairs={{0,3},{1,2},{2,1},{3,0},{4,7},{5,6},{6,5},{7,4},{8,11},{9,10},{10,... | collective-permute-start | bytes 196616 | tf_op jit(solution)/shard_map/ppermute | solution.py:19
  45.3 5.3 %collective-permute-start.12 = (f32[128,128]{1,0:T(8,128)S(1)}, f32[128,128]{1,0:T(8,128)S(1)}, u32[]{:S(2)}, u32[]{:S(2)}) collective-permute-start(f32[128,128]{1,0:T(8,128)S(1)} %get-tuple-element.32), channel_id=1, source_target_pairs={{0,2},{1,3},{2,0},{3,1},{4,6},{5,7},{6,4},{7,5},{8,10},{9,11},{10,... | collective-permute-start | bytes 196616 | tf_op jit(solution)/shard_map/ppermute | solution.py:19
  46.5 4.1 %copy-start.1 = (f32[128,128]{1,0:T(8,128)}, f32[128,128]{1,0:T(8,128)S(1)}, u32[]{:S(2)}) copy-start(f32[128,128]{1,0:T(8,128)S(1)} %collective-permute-done.18.refs_7_) | copy-start | bytes 196612
  46.5 4.1 %collective-permute-start.11 = (f32[128,128]{1,0:T(8,128)S(1)}, f32[128,128]{1,0:T(8,128)S(1)}, u32[]{:S(2)}, u32[]{:S(2)}) collective-permute-start(f32[128,128]{1,0:T(8,128)S(1)} %get-tuple-element.33), channel_id=1, source_target_pairs={{0,1},{1,0},{2,3},{3,2},{4,5},{5,4},{6,7},{7,6},{8,9},{9,8},{10,11... | collective-permute-start | bytes 196616 | tf_op jit(solution)/shard_map/ppermute | solution.py:19
  49.6 1.0 %copy-start.2 = (f32[128,128]{1,0:T(8,128)}, f32[128,128]{1,0:T(8,128)S(1)}, u32[]{:S(2)}) copy-start(f32[128,128]{1,0:T(8,128)S(1)} %collective-permute-done.17.refs_6_) | copy-start | bytes 196612
  49.6 1.0 %copy-start.3 = (f32[128,128]{1,0:T(8,128)}, f32[128,128]{1,0:T(8,128)S(1)}, u32[]{:S(2)}) copy-start(f32[128,128]{1,0:T(8,128)S(1)} %collective-permute-done.16.refs_5_) | copy-start | bytes 196612
  49.7 1.0 %copy-start.4 = (f32[128,128]{1,0:T(8,128)}, f32[128,128]{1,0:T(8,128)S(1)}, u32[]{:S(2)}) copy-start(f32[128,128]{1,0:T(8,128)S(1)} %collective-permute-done.13.refs_3_) | copy-start | bytes 196612
  50.6 0.6 %copy-start.5 = (f32[128,128]{1,0:T(8,128)}, f32[128,128]{1,0:T(8,128)S(1)}, u32[]{:S(2)}) copy-start(f32[128,128]{1,0:T(8,128)S(1)} %collective-permute-done.12.refs_2_) | copy-start | bytes 196612
  50.6 0.7 %copy-start.6 = (f32[128,128]{1,0:T(8,128)}, f32[128,128]{1,0:T(8,128)S(1)}, u32[]{:S(2)}) copy-start(f32[128,128]{1,0:T(8,128)S(1)} %collective-permute-done.11.refs_1_) | copy-start | bytes 196612

commit v2 on v1

v2 whole, which is shorter than its diff:
```python
import functools

import jax
import jax.numpy as jnp
from jax import lax
from jax.experimental import pallas as pl
from jax.experimental.pallas import tpu as pltpu
from jax.sharding import PartitionSpec as P

VMEM = pl.BlockSpec(memory_space=pltpu.VMEM)
LIMIT = 16 * 2**20
SMEM = pl.BlockSpec(memory_space=pltpu.SMEM)


def shift(x, axis, by):
    size = lax.axis_size(axis)
    return lax.ppermute(x, axis, [(i, (i + by) % size) for i in range(size)])


def swap(x, axis, bit):
    size = lax.axis_size(axis)
    return lax.ppermute(x, axis, [(i, i ^ bit) for i in range(size)])


def ready(dist, levels):
    return jnp.where(dist <= 1, dist, jnp.where(dist == levels - 1, 2, dist + 1))


def choose(vox, level, phase, slots, levels):
    dists = [jnp.maximum(level - (vox * slots + s), 0) for s in range(slots)]
    keys = [ready(d, levels) for d in dists]
    slot = dist = jnp.int32(0)
    for s in range(slots):
        rank = jnp.int32(0)
        for o in range(slots):
            if o != s:
                first = keys[o] <= keys[s] if o < s else keys[o] < keys[s]
                rank += first.astype(jnp.int32)
        slot = jnp.where(rank == phase, s, slot)
        dist = jnp.where(rank == phase, dists[s], dist)
    return slot, dist


def used(phase, slots, levels):
    out = set()
    rank = lambda d: d if d <= 1 else 2 if d == levels - 1 else d + 1
    for v in range(levels // slots):
        for z in range(levels):
            ds = [max(z - (v * slots + s), 0) for s in range(slots)]
            out.add(sorted(ds, key=rank)[phase])
    return sorted(out)


def pick_kernel(phase, slots, levels, vox, dists, *refs):
    pieces, outs = refs[: len(dists)], refs[len(dists) :]
    v, z = lax.axis_index("vox"), lax.axis_index("row")
    for t, out in enumerate(outs):
        _, dist = choose(lax.rem(v + vox - t, vox), z, phase, slots, levels)
        for d, piece in zip(dists, pieces):

            @pl.when(dist == d)
            def _():
                out[...] = piece[...]


def pick(pieces, phase, slots, levels, vox):
    dists = used(phase, slots, levels)
    like = jax.ShapeDtypeStruct(pieces[0].shape, pieces[0].dtype)
    return pl.pallas_call(
        functools.partial(pick_kernel, phase, slots, levels, vox, dists),
        out_shape=[like] * vox,
        compiler_params=pltpu.CompilerParams(vmem_limit_bytes=LIMIT),
        in_specs=[VMEM] * len(dists),
        out_specs=[VMEM] * vox,
    )(*[pieces[d] for d in dists])


def weigh_kernel(vox, lines, extinction_ref, *refs):
    priors, rows, (high_ref, low_ref) = refs[:vox], refs[vox:-2], refs[-2:]
    waves, chroms = extinction_ref.shape
    tile = rows[0].shape[0]
    w = lax.axis_index("wl")
    for t in range(vox):
        for d in range(lines):
            weight = 0.0
            for c in range(chroms):
                coeff = extinction_ref[lax.rem(w ^ d, waves), c] * extinction_ref[lax.rem(w, waves), c]
                weight += coeff * priors[t][c : c + 1, :]
            scaled = rows[t * lines + d][...].astype(jnp.float32) * weight
            top = scaled.astype(jnp.bfloat16)
            high_ref[t, d * tile : (d + 1) * tile, :] = top
            low_ref[t, d * tile : (d + 1) * tile, :] = (scaled - top.astype(jnp.float32)).astype(jnp.bfloat16)


def weigh(extinction, priors, rows):
    vox, lines = len(rows), len(rows[0])
    tile, depth = rows[0][0].shape
    like = jax.ShapeDtypeStruct((vox, lines * tile, depth), jnp.bfloat16)
    flat = [rows[t][d] for t in range(vox) for d in range(lines)]
    return pl.pallas_call(
        functools.partial(weigh_kernel, vox, lines),
        out_shape=[like, like],
        compiler_params=pltpu.CompilerParams(vmem_limit_bytes=LIMIT),
        in_specs=[SMEM] + [VMEM] * (vox + len(flat)),
        out_specs=[VMEM, VMEM],
    )(extinction, *priors, *flat)


def multiply_kernel(vox, high_ref, low_ref, *refs):
    cols, outs = refs[:vox], refs[vox:]
    tile = cols[0].shape[0]
    total = 0.0
    for t in range(vox):
        for part in (high_ref, low_ref):
            total += lax.dot_general(
                part[t], cols[t][...], (((1,), (1,)), ((), ())), preferred_element_type=jnp.float32
            )
    for d, out in enumerate(outs):
        out[...] = total[d * tile : (d + 1) * tile]


def multiply(high, low, cols, lines):
    vox, tile = len(cols), cols[0].shape[0]
    like = jax.ShapeDtypeStruct((tile, tile), jnp.float32)
    return pl.pallas_call(
        functools.partial(multiply_kernel, vox),
        out_shape=[like] * lines,
        compiler_params=pltpu.CompilerParams(vmem_limit_bytes=LIMIT),
        in_specs=[VMEM] * (2 + vox),
        out_specs=[VMEM] * lines,
    )(high, low, *cols)


def place_kernel(slots, lines, levels, *refs):
    blocks, out_ref = refs[:-1], refs[-1]
    tile = blocks[0].shape[0]
    v, z, w = (lax.axis_index(a) for a in ("vox", "row", "wl"))
    rows = (z * lines + w) * tile + lax.broadcasted_iota(jnp.int32, (tile, tile), 0)
    for p in range(slots):
        slot, _ = choose(v, z, p, slots, levels)
        for d in range(lines):
            at = pl.multiple_of((slot * lines + (w ^ d)) * tile, tile)
            cols = v * (slots * lines * tile) + at + lax.broadcasted_iota(jnp.int32, (tile, tile), 1)
            out_ref[:, pl.ds(at, tile)] = jnp.where(cols <= rows, blocks[p * lines + d][...], 0.0)


def place(blocks, slots, lines, levels):
    tile = blocks[0].shape[0]
    return pl.pallas_call(
        functools.partial(place_kernel, slots, lines, levels),
        out_shape=jax.ShapeDtypeStruct((tile, tile * len(blocks)), jnp.float32),
        compiler_params=pltpu.CompilerParams(vmem_limit_bytes=LIMIT),
        in_specs=[VMEM] * len(blocks),
        out_specs=VMEM,
    )(*blocks)


def on_device(jac, extinction, prior_var):
    vox, levels, lines = (lax.axis_size(a) for a in ("vox", "row", "wl"))
    slots = levels // vox

    pieces = {0: jac}
    for d in [1, levels - 1] + list(range(2, levels - 1)):
        if d not in pieces and d > 0:
            near = d in (1, levels - 1)
            pieces[d] = shift(jac if near else pieces[d - 1], "row", d if near else 1)

    halves = [jac] + [shift(jac, "vox", -t) for t in range(1, vox)]
    priors = [prior_var] + [shift(prior_var, "vox", -t) for t in range(1, vox)]
    rows = []
    for half in halves:
        got = {0: half}
        bit = lines // 2
        while bit:
            got.update({d ^ bit: swap(x, "wl", bit) for d, x in list(got.items())})
            bit //= 2
        rows.append([got[d] for d in range(lines)])
    high, low = weigh(extinction, priors, rows)

    blocks = []
    for phase in range(slots):
        cols = pick(pieces, phase, slots, levels, vox)
        cols = [cols[0]] + [shift(cols[t], "vox", -t) for t in range(1, vox)]
        done = multiply(high, low, cols, lines)
        blocks += [done[0]] + [swap(done[d], "wl", d) for d in range(1, lines)]
    return place(blocks, slots, lines, levels)


def solution(mesh):
    return jax.shard_map(
        on_device,
        mesh=mesh,
        in_specs=(P(("row", "wl"), "vox"), P(), P(None, "vox")),
        out_specs=P(("row", "wl"), "vox"),
        check_vma=False,
    )
```

time: 53.6 us -> 40.6 us (0.76)
  between operations: 6.83 us -> 0.09 us
  other arithmetic: 3.35 us -> 0 us
  starting transfers between devices: 15.3 us -> 18.2 us
  waiting for transfers between devices: 17.9 us -> 15.1 us
  matrix products: 2.67 us -> 0 us
  local copies, waits for them, and re-layouts: 5.17 us -> 3.28 us
  Pallas kernels: 1.95 us -> 3.79 us
    ppermute x7, waiting for transfers between devices: 16.5 us -> 11.2 us  [shift(): return lax.ppermute(x, axis, [(i, (i + by) % size) for i in range(size)])]
    dot_general x8 -> x0, matrix products: 2.67 us -> none  [on_device(): lax.dot_general(left, cols, (((1,), (1,)), ((), ())), preferred_element_t...]
    unnamed x18 -> x7, local copies, waits for them, and re-layouts: 0.67 us -> 3.28 us
    dynamic_slice x3 -> x0, local copies, waits for them, and re-layouts: 2.6 us -> none  [the longest x1 1.42 us: pick(): here = jnp.asarray(dist[:, :, phase])[v, z]]
    ppermute x12, waiting for transfers between devices: 1.45 us -> 3.87 us  [swap(): return lax.ppermute(x, axis, [(i, i ^ bit) for i in range(size)])]
    ppermute x7, starting transfers between devices: 9.29 us -> 11.7 us  [shift(): return lax.ppermute(x, axis, [(i, (i + by) % size) for i in range(size)])]
    pallas_call x1 -> x6, Pallas kernels: 1.95 us -> 3.79 us  [the longest x2 1.72 us: multiply(): pl.pallas_call(functools.partial(multiply_kernel, vox), out_shape=[like]...]
    convert_element_type x8 -> x0, other arithmetic: 1.4 us -> none  [on_device(): high.append(top.astype(jnp.bfloat16))]
  transfers between devices with their start and end apart: 19 -> 19, of which waited for: 6 -> 8; matrix products, arithmetic and copies ran while one was open for 20% -> 2% of each run, Pallas kernels for 0% -> 7%
where the time goes in v2:
time: 40.6 us; the launch traced here: 40.4 us
  starting transfers between devices  18.2 us (45%)
  waiting for transfers between devices  15.1 us (37%)
  Pallas kernels  3.79 us (9%)
  local copies, waits for them, and re-layouts  3.28 us (8%)
    ppermute x7, starting transfers between devices, shift(): return lax.ppermute(x, axis, [(i, (i + by) % size) for i in range(size)])  11.7 us
    ppermute x7, waiting for transfers between devices, shift(): return lax.ppermute(x, axis, [(i, (i + by) % size) for i in range(size)])  11.2 us
    ppermute x12, starting transfers between devices, swap(): return lax.ppermute(x, axis, [(i, i ^ bit) for i in range(size)])  6.49 us
    ppermute x12, waiting for transfers between devices, swap(): return lax.ppermute(x, axis, [(i, i ^ bit) for i in range(size)])  3.87 us
    unnamed x7, local copies, waits for them, and re-layouts  3.28 us
    pallas_call x2, Pallas kernels, multiply(): pl.pallas_call(functools.partial(multiply_kernel, vox), out_shape=[like]...  1.72 us
    pallas_call x1, Pallas kernels, weigh(): pl.pallas_call(functools.partial(weigh_kernel, vox, lines), out_shape=[li...  1.09 us
    pallas_call x1, Pallas kernels, place(): pl.pallas_call(functools.partial(place_kernel, slots, lines, levels), out...  0.88 us
  transfers between devices with their start and end apart: 19, of which 8 were waited for; matrix products, arithmetic and copies ran while one was open for 2% of the time, Pallas kernels for 7%

profile of v2, /device:TPU:0, one launch (start us, length us, event | category | flops | bytes accessed | tf_op | source)
XLA Modules:
  0.0 40.4 jit_solution(1248833482427573429)
XLA Ops:
  0.0 3.0 %collective-permute-start.8 = (bf16[128,640]{1,0:T(8,128)(2,1)}, bf16[128,640]{1,0:T(8,128)(2,1)S(1)}, u32[]{:S(2)}, u32[]{:S(2)}) collective-permute-start(bf16[128,640]{1,0:T(8,128)(2,1)} %refs_0_.5), channel_id=1, source_target_pairs={{0,4},{4,8},{8,12},{12,0},{1,5},{5,9},{9,13},{13,1},{2,6},{6,10},{... | collective-permute-start | bytes 491528 | tf_op jit(solution)/shard_map/ppermute | solution.py:17
  3.0 1.5 %collective-permute-start.4 = (bf16[128,640]{1,0:T(8,128)(2,1)}, bf16[128,640]{1,0:T(8,128)(2,1)S(1)}, u32[]{:S(2)}, u32[]{:S(2)}) collective-permute-start(bf16[128,640]{1,0:T(8,128)(2,1)} %refs_0_.5), channel_id=1, source_target_pairs={{0,16},{16,0},{1,17},{17,1},{2,18},{18,2},{3,19},{19,3},{4,20},{20... | collective-permute-start | bytes 491528 | tf_op jit(solution)/shard_map/ppermute | solution.py:17
  4.5 4.9 %collective-permute-done.8.refs_1_ = bf16[128,640]{1,0:T(8,128)(2,1)S(1)} collective-permute-done((bf16[128,640]{1,0:T(8,128)(2,1)}, bf16[128,640]{1,0:T(8,128)(2,1)S(1)}, u32[]{:S(2)}, u32[]{:S(2)}) %collective-permute-start.8) | collective-permute-done | bytes 163872 | tf_op jit(solution)/shard_map/ppermute | solution.py:17
  9.5 0.0 collective-permute-start.14
  9.5 1.5 %collective-permute-start.2 = (bf16[128,640]{1,0:T(8,128)(2,1)}, bf16[128,640]{1,0:T(8,128)(2,1)S(1)}, u32[]{:S(2)}, u32[]{:S(2)}) collective-permute-start(bf16[128,640]{1,0:T(8,128)(2,1)} %refs_0_.5), channel_id=1, source_target_pairs={{0,2},{1,3},{2,0},{3,1},{4,6},{5,7},{6,4},{7,5},{8,10},{9,11},{10,... | collective-permute-start | bytes 491528 | tf_op jit(solution)/shard_map/ppermute | solution.py:22
  11.0 0.0 collective-permute-done.4.refs_6_
  11.0 0.5 %collective-permute-start.6 = (bf16[128,640]{1,0:T(8,128)(2,1)S(1)}, bf16[128,640]{1,0:T(8,128)(2,1)S(1)}, u32[]{:S(2)}, u32[]{:S(2)}) collective-permute-start(bf16[128,640]{1,0:T(8,128)(2,1)S(1)} %collective-permute-done.4.refs_6_), channel_id=1, source_target_pairs={{0,2},{1,3},{2,0},{3,1},{4,6},{5,7},{6,4},{7,5},{8,10},{9,11},{10,... | collective-permute-start | bytes 491528 | tf_op jit(solution)/shard_map/ppermute | solution.py:22
  11.5 3.8 %collective-permute-start.9 = (bf16[128,640]{1,0:T(8,128)(2,1)}, bf16[128,640]{1,0:T(8,128)(2,1)S(1)}, u32[]{:S(2)}, u32[]{:S(2)}) collective-permute-start(bf16[128,640]{1,0:T(8,128)(2,1)} %refs_0_.5), channel_id=1, source_target_pairs={{0,12},{4,0},{8,4},{12,8},{1,13},{5,1},{9,5},{13,9},{2,14},{6,2},{... | collective-permute-start | bytes 491528 | tf_op jit(solution)/shard_map/ppermute | solution.py:17
  15.3 0.0 collective-permute-start.1
  15.3 3.1 %collective-permute-done.14.refs_2_ = bf16[128,640]{1,0:T(8,128)(2,1)S(1)} collective-permute-done((bf16[128,640]{1,0:T(8,128)(2,1)S(1)}, bf16[128,640]{1,0:T(8,128)(2,1)S(1)}, u32[]{:S(2)}, u32[]{:S(2)}) %collective-permute-start.14) | collective-permute-done | bytes 163872 | tf_op jit(solution)/shard_map/ppermute | solution.py:17
  18.4 1.3 %collective-permute-start = (f32[2,640]{1,0:T(2,128)}, f32[2,640]{1,0:T(2,128)S(1)}, u32[]{:S(2)}, u32[]{:S(2)}) collective-permute-start(f32[2,640]{1,0:T(2,128)} %refs_0_.3), channel_id=1, source_target_pairs={{0,16},{16,0},{1,17},{17,1},{2,18},{18,2},{3,19},{19,3},{4,20},{20... | collective-permute-start | bytes 15368 | tf_op jit(solution)/shard_map/ppermute | solution.py:17
  19.7 0.0 copy-start
  19.7 0.9 %copy-done = bf16[128,640]{1,0:T(8,128)(2,1)S(1)} copy-done((bf16[128,640]{1,0:T(8,128)(2,1)S(1)}, bf16[128,640]{1,0:T(8,128)(2,1)}, u32[]{:S(2)}) %copy-start) | copy-done | bytes 163864
  20.6 0.1 shard_map.40
  20.6 1.6 %collective-permute-done.refs_1_ = f32[2,640]{1,0:T(2,128)S(1)} collective-permute-done((f32[2,640]{1,0:T(2,128)}, f32[2,640]{1,0:T(2,128)S(1)}, u32[]{:S(2)}, u32[]{:S(2)}) %collective-permute-start) | collective-permute-done | bytes 5152 | tf_op jit(solution)/shard_map/ppermute | solution.py:17
  22.2 0.0 collective-permute-start.5
  22.2 0.0 collective-permute-done.2.refs_4_
  22.2 0.5 %collective-permute-start.3 = (bf16[128,640]{1,0:T(8,128)(2,1)S(1)}, bf16[128,640]{1,0:T(8,128)(2,1)S(1)}, u32[]{:S(2)}, u32[]{:S(2)}) collective-permute-start(bf16[128,640]{1,0:T(8,128)(2,1)S(1)} %collective-permute-done.2.refs_4_), channel_id=1, source_target_pairs={{0,1},{1,0},{2,3},{3,2},{4,5},{5,4},{6,7},{7,6},{8,9},{9,8},{10,11... | collective-permute-start | bytes 491528 | tf_op jit(solution)/shard_map/ppermute | solution.py:22
  22.8 0.0 collective-permute-done.6.refs_8_
  22.8 0.1 collective-permute-start.7
  22.8 0.0 collective-permute-done.9.refs_2_
  22.8 1.3 %collective-permute-start.15 = (bf16[128,640]{1,0:T(8,128)(2,1)S(1)}, bf16[128,640]{1,0:T(8,128)(2,1)S(1)}, u32[]{:S(2)}, u32[]{:S(2)}) collective-permute-start(bf16[128,640]{1,0:T(8,128)(2,1)S(1)} %get-tuple-element.28), channel_id=1, source_target_pairs={{0,16},{16,0},{1,17},{17,1},{2,18},{18,2},{3,19},{19,3},{4,20},{20... | collective-permute-start | bytes 491528 | tf_op jit(solution)/shard_map/ppermute | solution.py:17
  24.1 0.1 shard_map.38
  24.1 0.0 collective-permute-done.1.refs_3_
  24.2 0.8 %collective-permute-start.10 = (bf16[128,640]{1,0:T(8,128)(2,1)S(1)}, bf16[128,640]{1,0:T(8,128)(2,1)S(1)}, u32[]{:S(2)}, u32[]{:S(2)}) collective-permute-start(bf16[128,640]{1,0:T(8,128)(2,1)S(1)} %get-tuple-element.22), channel_id=1, source_target_pairs={{0,16},{16,0},{1,17},{17,1},{2,18},{18,2},{3,19},{19,3},{4,20},{20... | collective-permute-start | bytes 491528 | tf_op jit(solution)/shard_map/ppermute | solution.py:17
  25.0 0.8 %copy.4.extinction_ref = f32[4,2]{1,0:T(4,128)S(1)} copy(f32[4,2]{0,1:T(2,128)} %param.4) | data formatting | bytes 64 | tf_op args[1]
  25.8 0.0 collective-permute-done.5.refs_7_
  25.8 0.0 collective-permute-done.3.refs_5_
  25.8 0.0 collective-permute-done.7.refs_9_
  25.8 0.0 copy-start.1
  25.8 0.9 %copy-done.1 = bf16[128,640]{1,0:T(8,128)(2,1)S(1)} copy-done((bf16[128,640]{1,0:T(8,128)(2,1)S(1)}, bf16[128,640]{1,0:T(8,128)(2,1)}, u32[]{:S(2)}) %copy-start.1) | copy-done | bytes 163864
  26.7 0.0 copy-start.2
  26.7 0.7 %copy-done.2 = f32[2,640]{1,0:T(2,128)S(1)} copy-done((f32[2,640]{1,0:T(2,128)S(1)}, f32[2,640]{1,0:T(2,128)}, u32[]{:S(2)}) %copy-start.2) | copy-done | bytes 5144
  27.4 1.1 %shard_map.37 = (bf16[2,512,640]{2,1,0:T(8,128)(2,1)S(1)}, bf16[2,512,640]{2,1,0:T(8,128)(2,1)S(1)}) custom-call(f32[4,2]{1,0:T(4,128)S(1)} %copy.4.extinction_ref, f32[2,640]{1,0:T(2,128)S(1)} %copy-done.2, f32[2,640]{1,0:T(2,128)S(1)} %collective-permute-done.refs_1_, bf16[128,640]{1,0:T(8,128)(2,1)S(1)} %copy-done.1, ...), custom_call_target="tpu_custom_call" | custom-call | tf_op jit(solution)/shard_map/pallas_call | solution.py:100
  28.5 1.4 %collective-permute-done.15.refs_1_ = bf16[128,640]{1,0:T(8,128)(2,1)S(1)} collective-permute-done((bf16[128,640]{1,0:T(8,128)(2,1)S(1)}, bf16[128,640]{1,0:T(8,128)(2,1)S(1)}, u32[]{:S(2)}, u32[]{:S(2)}) %collective-permute-start.15) | collective-permute-done | bytes 163872 | tf_op jit(solution)/shard_map/ppermute | solution.py:17
  29.8 0.9 %shard_map.41 = (f32[128,128]{1,0:T(8,128)S(1)}, f32[128,128]{1,0:T(8,128)S(1)}, f32[128,128]{1,0:T(8,128)S(1)}, f32[128,128]{1,0:T(8,128)S(1)}) custom-call(bf16[2,512,640]{2,1,0:T(8,128)(2,1)S(1)} %get-tuple-element.19.high_ref, bf16[2,512,640]{2,1,0:T(8,128)(2,1)S(1)} %get-tuple-element.20.low_ref, bf16[128,640]{1,0:T(8,128)(2,1)S(1)} %get-tuple-element.27.refs_0_, ...), custom_call_target="tpu_custom_call" | custom-call | tf_op jit(solution)/shard_map/pallas_call | solution.py:125
  30.7 0.1 collective-permute-start.16
  30.8 1.4 %collective-permute-start.17 = (f32[128,128]{1,0:T(8,128)S(1)}, f32[128,128]{1,0:T(8,128)S(1)}, u32[]{:S(2)}, u32[]{:S(2)}) collective-permute-start(f32[128,128]{1,0:T(8,128)S(1)} %get-tuple-element.31), channel_id=1, source_target_pairs={{0,2},{1,3},{2,0},{3,1},{4,6},{5,7},{6,4},{7,5},{8,10},{9,11},{10,... | collective-permute-start | bytes 196616 | tf_op jit(solution)/shard_map/ppermute | solution.py:22
  32.1 0.5 %collective-permute-start.18 = (f32[128,128]{1,0:T(8,128)S(1)}, f32[128,128]{1,0:T(8,128)S(1)}, u32[]{:S(2)}, u32[]{:S(2)}) collective-permute-start(f32[128,128]{1,0:T(8,128)S(1)} %get-tuple-element.32), channel_id=1, source_target_pairs={{0,3},{1,2},{2,1},{3,0},{4,7},{5,6},{6,5},{7,4},{8,11},{9,10},{10,... | collective-permute-start | bytes 196616 | tf_op jit(solution)/shard_map/ppermute | solution.py:22
  32.6 0.2 collective-permute-done.10.refs_1_
  32.9 0.9 %shard_map.39 = (f32[128,128]{1,0:T(8,128)S(1)}, f32[128,128]{1,0:T(8,128)S(1)}, f32[128,128]{1,0:T(8,128)S(1)}, f32[128,128]{1,0:T(8,128)S(1)}) custom-call(bf16[2,512,640]{2,1,0:T(8,128)(2,1)S(1)} %get-tuple-element.19.high_ref, bf16[2,512,640]{2,1,0:T(8,128)(2,1)S(1)} %get-tuple-element.20.low_ref, bf16[128,640]{1,0:T(8,128)(2,1)S(1)} %get-tuple-element.21.refs_0_, ...), custom_call_target="tpu_custom_call" | custom-call | tf_op jit(solution)/shard_map/pallas_call | solution.py:125
  33.8 0.2 collective-permute-start.11
  33.9 1.3 %collective-permute-start.12 = (f32[128,128]{1,0:T(8,128)S(1)}, f32[128,128]{1,0:T(8,128)S(1)}, u32[]{:S(2)}, u32[]{:S(2)}) collective-permute-start(f32[128,128]{1,0:T(8,128)S(1)} %get-tuple-element.25), channel_id=1, source_target_pairs={{0,2},{1,3},{2,0},{3,1},{4,6},{5,7},{6,4},{7,5},{8,10},{9,11},{10,... | collective-permute-start | bytes 196616 | tf_op jit(solution)/shard_map/ppermute | solution.py:22
  35.2 0.0 collective-permute-done.16.refs_5_
  35.2 0.5 %collective-permute-start.13 = (f32[128,128]{1,0:T(8,128)S(1)}, f32[128,128]{1,0:T(8,128)S(1)}, u32[]{:S(2)}, u32[]{:S(2)}) collective-permute-start(f32[128,128]{1,0:T(8,128)S(1)} %get-tuple-element.26), channel_id=1, source_target_pairs={{0,3},{1,2},{2,1},{3,0},{4,7},{5,6},{6,5},{7,4},{8,11},{9,10},{10,... | collective-permute-start | bytes 196616 | tf_op jit(solution)/shard_map/ppermute | solution.py:22
  35.7 0.0 collective-permute-done.17.refs_6_
  35.7 0.8 %collective-permute-done.18.refs_7_ = f32[128,128]{1,0:T(8,128)S(1)} collective-permute-done((f32[128,128]{1,0:T(8,128)S(1)}, f32[128,128]{1,0:T(8,128)S(1)}, u32[]{:S(2)}, u32[]{:S(2)}) %collective-permute-start.18) | collective-permute-done | bytes 65568 | tf_op jit(solution)/shard_map/ppermute | solution.py:22
  36.5 0.0 collective-permute-done.11.refs_1_
  36.5 2.1 %collective-permute-done.12.refs_2_ = f32[128,128]{1,0:T(8,128)S(1)} collective-permute-done((f32[128,128]{1,0:T(8,128)S(1)}, f32[128,128]{1,0:T(8,128)S(1)}, u32[]{:S(2)}, u32[]{:S(2)}) %collective-permute-start.12) | collective-permute-done | bytes 65568 | tf_op jit(solution)/shard_map/ppermute | solution.py:22
  38.5 1.0 %collective-permute-done.13.refs_3_ = f32[128,128]{1,0:T(8,128)S(1)} collective-permute-done((f32[128,128]{1,0:T(8,128)S(1)}, f32[128,128]{1,0:T(8,128)S(1)}, u32[]{:S(2)}, u32[]{:S(2)}) %collective-permute-start.13) | collective-permute-done | bytes 65568 | tf_op jit(solution)/shard_map/ppermute | solution.py:22
  39.6 0.9 %shard_map.42 = f32[128,1024]{1,0:T(8,128)} custom-call(f32[128,128]{1,0:T(8,128)S(1)} %get-tuple-element.23.refs_0_, f32[128,128]{1,0:T(8,128)S(1)} %collective-permute-done.11.refs_1_, f32[128,128]{1,0:T(8,128)S(1)} %collective-permute-done.12.refs_2_, f32[128,128]{1,0:T(8,128)S(1)} %collective-permute-done.13.refs_3_, ...), custom_call_target="tpu_custom_call" | custom-call | tf_op jit(solution)/shard_map/pallas_call | solution.py:149
Async XLA Ops:
  0.0 9.5 %collective-permute-start.8 = (bf16[128,640]{1,0:T(8,128)(2,1)}, bf16[128,640]{1,0:T(8,128)(2,1)S(1)}, u32[]{:S(2)}, u32[]{:S(2)}) collective-permute-start(bf16[128,640]{1,0:T(8,128)(2,1)} %refs_0_.5), channel_id=1, source_target_pairs={{0,4},{4,8},{8,12},{12,0},{1,5},{5,9},{9,13},{13,1},{2,6},{6,10},{... | collective-permute-start | bytes 491528 | tf_op jit(solution)/shard_map/ppermute | solution.py:17
  3.0 8.0 %collective-permute-start.4 = (bf16[128,640]{1,0:T(8,128)(2,1)}, bf16[128,640]{1,0:T(8,128)(2,1)S(1)}, u32[]{:S(2)}, u32[]{:S(2)}) collective-permute-start(bf16[128,640]{1,0:T(8,128)(2,1)} %refs_0_.5), channel_id=1, source_target_pairs={{0,16},{16,0},{1,17},{17,1},{2,18},{18,2},{3,19},{19,3},{4,20},{20... | collective-permute-start | bytes 491528 | tf_op jit(solution)/shard_map/ppermute | solution.py:17
  9.5 9.0 %collective-permute-start.14 = (bf16[128,640]{1,0:T(8,128)(2,1)S(1)}, bf16[128,640]{1,0:T(8,128)(2,1)S(1)}, u32[]{:S(2)}, u32[]{:S(2)}) collective-permute-start(bf16[128,640]{1,0:T(8,128)(2,1)S(1)} %collective-permute-done.8.refs_1_), channel_id=1, source_target_pairs={{0,4},{4,8},{8,12},{12,0},{1,5},{5,9},{9,13},{13,1},{2,6},{6,10},{... | collective-permute-start | bytes 491528 | tf_op jit(solution)/shard_map/ppermute | solution.py:17
  9.5 12.8 %collective-permute-start.2 = (bf16[128,640]{1,0:T(8,128)(2,1)}, bf16[128,640]{1,0:T(8,128)(2,1)S(1)}, u32[]{:S(2)}, u32[]{:S(2)}) collective-permute-start(bf16[128,640]{1,0:T(8,128)(2,1)} %refs_0_.5), channel_id=1, source_target_pairs={{0,2},{1,3},{2,0},{3,1},{4,6},{5,7},{6,4},{7,5},{8,10},{9,11},{10,... | collective-permute-start | bytes 491528 | tf_op jit(solution)/shard_map/ppermute | solution.py:22
  11.0 11.8 %collective-permute-start.6 = (bf16[128,640]{1,0:T(8,128)(2,1)S(1)}, bf16[128,640]{1,0:T(8,128)(2,1)S(1)}, u32[]{:S(2)}, u32[]{:S(2)}) collective-permute-start(bf16[128,640]{1,0:T(8,128)(2,1)S(1)} %collective-permute-done.4.refs_6_), channel_id=1, source_target_pairs={{0,2},{1,3},{2,0},{3,1},{4,6},{5,7},{6,4},{7,5},{8,10},{9,11},{10,... | collective-permute-start | bytes 491528 | tf_op jit(solution)/shard_map/ppermute | solution.py:22
  11.5 11.3 %collective-permute-start.9 = (bf16[128,640]{1,0:T(8,128)(2,1)}, bf16[128,640]{1,0:T(8,128)(2,1)S(1)}, u32[]{:S(2)}, u32[]{:S(2)}) collective-permute-start(bf16[128,640]{1,0:T(8,128)(2,1)} %refs_0_.5), channel_id=1, source_target_pairs={{0,12},{4,0},{8,4},{12,8},{1,13},{5,1},{9,5},{13,9},{2,14},{6,2},{... | collective-permute-start | bytes 491528 | tf_op jit(solution)/shard_map/ppermute | solution.py:17
  15.3 8.8 %collective-permute-start.1 = (bf16[128,640]{1,0:T(8,128)(2,1)}, bf16[128,640]{1,0:T(8,128)(2,1)S(1)}, u32[]{:S(2)}, u32[]{:S(2)}) collective-permute-start(bf16[128,640]{1,0:T(8,128)(2,1)} %refs_0_.5), channel_id=1, source_target_pairs={{0,1},{1,0},{2,3},{3,2},{4,5},{5,4},{6,7},{7,6},{8,9},{9,8},{10,11... | collective-permute-start | bytes 491528 | tf_op jit(solution)/shard_map/ppermute | solution.py:22
  18.4 3.8 %collective-permute-start = (f32[2,640]{1,0:T(2,128)}, f32[2,640]{1,0:T(2,128)S(1)}, u32[]{:S(2)}, u32[]{:S(2)}) collective-permute-start(f32[2,640]{1,0:T(2,128)} %refs_0_.3), channel_id=1, source_target_pairs={{0,16},{16,0},{1,17},{17,1},{2,18},{18,2},{3,19},{19,3},{4,20},{20... | collective-permute-start | bytes 15368 | tf_op jit(solution)/shard_map/ppermute | solution.py:17
  19.7 0.9 %copy-start = (bf16[128,640]{1,0:T(8,128)(2,1)S(1)}, bf16[128,640]{1,0:T(8,128)(2,1)}, u32[]{:S(2)}) copy-start(bf16[128,640]{1,0:T(8,128)(2,1)} %refs_0_.5) | copy-start | bytes 491524
  22.2 3.5 %collective-permute-start.5 = (bf16[128,640]{1,0:T(8,128)(2,1)S(1)}, bf16[128,640]{1,0:T(8,128)(2,1)S(1)}, u32[]{:S(2)}, u32[]{:S(2)}) collective-permute-start(bf16[128,640]{1,0:T(8,128)(2,1)S(1)} %collective-permute-done.4.refs_6_), channel_id=1, source_target_pairs={{0,1},{1,0},{2,3},{3,2},{4,5},{5,4},{6,7},{7,6},{8,9},{9,8},{10,11... | collective-permute-start | bytes 491528 | tf_op jit(solution)/shard_map/ppermute | solution.py:22
  22.2 3.5 %collective-permute-start.3 = (bf16[128,640]{1,0:T(8,128)(2,1)S(1)}, bf16[128,640]{1,0:T(8,128)(2,1)S(1)}, u32[]{:S(2)}, u32[]{:S(2)}) collective-permute-start(bf16[128,640]{1,0:T(8,128)(2,1)S(1)} %collective-permute-done.2.refs_4_), channel_id=1, source_target_pairs={{0,1},{1,0},{2,3},{3,2},{4,5},{5,4},{6,7},{7,6},{8,9},{9,8},{10,11... | collective-permute-start | bytes 491528 | tf_op jit(solution)/shard_map/ppermute | solution.py:22
  22.8 3.0 %collective-permute-start.7 = (bf16[128,640]{1,0:T(8,128)(2,1)S(1)}, bf16[128,640]{1,0:T(8,128)(2,1)S(1)}, u32[]{:S(2)}, u32[]{:S(2)}) collective-permute-start(bf16[128,640]{1,0:T(8,128)(2,1)S(1)} %collective-permute-done.6.refs_8_), channel_id=1, source_target_pairs={{0,1},{1,0},{2,3},{3,2},{4,5},{5,4},{6,7},{7,6},{8,9},{9,8},{10,11... | collective-permute-start | bytes 491528 | tf_op jit(solution)/shard_map/ppermute | solution.py:22
  22.8 7.0 %collective-permute-start.15 = (bf16[128,640]{1,0:T(8,128)(2,1)S(1)}, bf16[128,640]{1,0:T(8,128)(2,1)S(1)}, u32[]{:S(2)}, u32[]{:S(2)}) collective-permute-start(bf16[128,640]{1,0:T(8,128)(2,1)S(1)} %get-tuple-element.28), channel_id=1, source_target_pairs={{0,16},{16,0},{1,17},{17,1},{2,18},{18,2},{3,19},{19,3},{4,20},{20... | collective-permute-start | bytes 491528 | tf_op jit(solution)/shard_map/ppermute | solution.py:17
  24.2 8.7 %collective-permute-start.10 = (bf16[128,640]{1,0:T(8,128)(2,1)S(1)}, bf16[128,640]{1,0:T(8,128)(2,1)S(1)}, u32[]{:S(2)}, u32[]{:S(2)}) collective-permute-start(bf16[128,640]{1,0:T(8,128)(2,1)S(1)} %get-tuple-element.22), channel_id=1, source_target_pairs={{0,16},{16,0},{1,17},{17,1},{2,18},{18,2},{3,19},{19,3},{4,20},{20... | collective-permute-start | bytes 491528 | tf_op jit(solution)/shard_map/ppermute | solution.py:17
  25.8 0.9 %copy-start.1 = (bf16[128,640]{1,0:T(8,128)(2,1)S(1)}, bf16[128,640]{1,0:T(8,128)(2,1)}, u32[]{:S(2)}) copy-start(bf16[128,640]{1,0:T(8,128)(2,1)} %refs_0_.5) | copy-start | bytes 491524
  26.7 0.7 %copy-start.2 = (f32[2,640]{1,0:T(2,128)S(1)}, f32[2,640]{1,0:T(2,128)}, u32[]{:S(2)}) copy-start(f32[2,640]{1,0:T(2,128)} %refs_0_.3) | copy-start | bytes 15364
  30.7 4.5 %collective-permute-start.16 = (f32[128,128]{1,0:T(8,128)S(1)}, f32[128,128]{1,0:T(8,128)S(1)}, u32[]{:S(2)}, u32[]{:S(2)}) collective-permute-start(f32[128,128]{1,0:T(8,128)S(1)} %get-tuple-element.30), channel_id=1, source_target_pairs={{0,1},{1,0},{2,3},{3,2},{4,5},{5,4},{6,7},{7,6},{8,9},{9,8},{10,11... | collective-permute-start | bytes 196616 | tf_op jit(solution)/shard_map/ppermute | solution.py:22
  30.8 4.9 %collective-permute-start.17 = (f32[128,128]{1,0:T(8,128)S(1)}, f32[128,128]{1,0:T(8,128)S(1)}, u32[]{:S(2)}, u32[]{:S(2)}) collective-permute-start(f32[128,128]{1,0:T(8,128)S(1)} %get-tuple-element.31), channel_id=1, source_target_pairs={{0,2},{1,3},{2,0},{3,1},{4,6},{5,7},{6,4},{7,5},{8,10},{9,11},{10,... | collective-permute-start | bytes 196616 | tf_op jit(solution)/shard_map/ppermute | solution.py:22
  32.1 4.3 %collective-permute-start.18 = (f32[128,128]{1,0:T(8,128)S(1)}, f32[128,128]{1,0:T(8,128)S(1)}, u32[]{:S(2)}, u32[]{:S(2)}) collective-permute-start(f32[128,128]{1,0:T(8,128)S(1)} %get-tuple-element.32), channel_id=1, source_target_pairs={{0,3},{1,2},{2,1},{3,0},{4,7},{5,6},{6,5},{7,4},{8,11},{9,10},{10,... | collective-permute-start | bytes 196616 | tf_op jit(solution)/shard_map/ppermute | solution.py:22
  33.8 2.7 %collective-permute-start.11 = (f32[128,128]{1,0:T(8,128)S(1)}, f32[128,128]{1,0:T(8,128)S(1)}, u32[]{:S(2)}, u32[]{:S(2)}) collective-permute-start(f32[128,128]{1,0:T(8,128)S(1)} %get-tuple-element.24), channel_id=1, source_target_pairs={{0,1},{1,0},{2,3},{3,2},{4,5},{5,4},{6,7},{7,6},{8,9},{9,8},{10,11... | collective-permute-start | bytes 196616 | tf_op jit(solution)/shard_map/ppermute | solution.py:22
  33.9 4.6 %collective-permute-start.12 = (f32[128,128]{1,0:T(8,128)S(1)}, f32[128,128]{1,0:T(8,128)S(1)}, u32[]{:S(2)}, u32[]{:S(2)}) collective-permute-start(f32[128,128]{1,0:T(8,128)S(1)} %get-tuple-element.25), channel_id=1, source_target_pairs={{0,2},{1,3},{2,0},{3,1},{4,6},{5,7},{6,4},{7,5},{8,10},{9,11},{10,... | collective-permute-start | bytes 196616 | tf_op jit(solution)/shard_map/ppermute | solution.py:22
  35.2 4.3 %collective-permute-start.13 = (f32[128,128]{1,0:T(8,128)S(1)}, f32[128,128]{1,0:T(8,128)S(1)}, u32[]{:S(2)}, u32[]{:S(2)}) collective-permute-start(f32[128,128]{1,0:T(8,128)S(1)} %get-tuple-element.26), channel_id=1, source_target_pairs={{0,3},{1,2},{2,1},{3,0},{4,7},{5,6},{6,5},{7,4},{8,11},{9,10},{10,... | collective-permute-start | bytes 196616 | tf_op jit(solution)/shard_map/ppermute | solution.py:22

commit v3 on v0

v3 whole, which is shorter than its diff:
```python
import functools

import jax
import jax.numpy as jnp
from jax import lax
from jax.experimental import pallas as pl
from jax.experimental.pallas import tpu as pltpu
from jax.sharding import PartitionSpec as P

LIMIT = 16 * 2**20
EXTRA = 16
SMEM = pl.BlockSpec(memory_space=pltpu.SMEM)
VMEM = pl.BlockSpec(memory_space=pltpu.VMEM)


def shift(x, axis, by):
    size = lax.axis_size(axis)
    return lax.ppermute(x, axis, [(i, (i + by) % size) for i in range(size)])


def swap(x, axis, bit):
    size = lax.axis_size(axis)
    return lax.ppermute(x, axis, [(i, i ^ bit) for i in range(size)])


def send(x, by, bit):
    vox, lines = lax.axis_size("vox"), lax.axis_size("wl")
    pairs = [
        (v * lines + w, (v + by) % vox * lines + (w ^ bit)) for v in range(vox) for w in range(lines)
    ]
    return lax.ppermute(x, ("vox", "wl"), pairs)


def kernel_call(kernel, ins, outs, scratch=()):
    return functools.partial(
        pl.pallas_call,
        kernel,
        in_specs=ins,
        out_specs=[VMEM] * len(outs),
        out_shape=outs,
        scratch_shapes=scratch,
        compiler_params=pltpu.CompilerParams(vmem_limit_bytes=LIMIT),
    )()


def weigh_kernel(far, near, extinction_ref, prior_ref, *refs):
    rows, (high_ref, low_ref) = refs[:-2], refs[-2:]
    chroms, waves = extinction_ref.shape
    tile = rows[0].shape[0]
    w = lax.axis_index("wl")
    for i, e in enumerate(near):
        for j, f in enumerate(far):
            weight = 0.0
            for c in range(chroms):
                coeff = extinction_ref[c, lax.rem(w ^ f, waves)] * extinction_ref[c, lax.rem(w ^ e, waves)]
                weight += coeff * prior_ref[c : c + 1, :]
            scaled = rows[j][...].astype(jnp.float32) * weight
            top = scaled.astype(jnp.bfloat16)
            high_ref[i, j * tile : (j + 1) * tile, :] = top
            low_ref[i, j * tile : (j + 1) * tile, :] = (scaled - top.astype(jnp.float32)).astype(jnp.bfloat16)


def weigh(extinction, prior, rows, far, near):
    tile, depth = rows[0].shape
    like = jax.ShapeDtypeStruct((len(near), len(far) * tile, depth), jnp.bfloat16)
    call = kernel_call(
        functools.partial(weigh_kernel, far, near), [SMEM] + [VMEM] * (1 + len(rows)), [like, like]
    )
    return call(extinction, prior, *rows)


def multiply_kernel(vox, levels, far, near, high_ref, low_ref, *refs):
    count = levels * len(near)
    pieces, outs, cols_ref = refs[:count], refs[count:-1], refs[-1]
    tile, slots = pieces[0].shape[0], levels // vox
    v, z = lax.axis_index("vox"), lax.axis_index("row")
    for t in range(vox):
        owner = lax.rem(v + t, vox)
        for s in range(slots):
            dist = jnp.maximum(z - (owner * slots + s), 0)
            at = (t * slots + s) * tile
            for d in range(levels):

                @pl.when(dist == d)
                def _():
                    for i in range(len(near)):
                        cols_ref[i, at : at + tile] = pieces[d * len(near) + i][...]

    for i in range(len(near)):
        total = 0.0
        for part in (high_ref, low_ref):
            total += lax.dot_general(
                part[i], cols_ref[i], (((1,), (1,)), ((), ())), preferred_element_type=jnp.float32
            )
        for t in range(vox):
            for j in range(len(far)):
                for s in range(slots):
                    to, at = (s * len(near) + i) * tile, (t * slots + s) * tile
                    outs[t * len(far) + j][:tile, to : to + tile] = total[
                        j * tile : (j + 1) * tile, at : at + tile
                    ]
    for out in outs[1:]:
        largest = jnp.max(jnp.abs(out[:tile]), axis=(0, 1), keepdims=True)
        power = jnp.floor(jnp.log2(jnp.maximum(largest, 1e-30))) - 13.0
        out[:tile] *= jnp.exp2(-power)
        out[tile:] = jnp.broadcast_to(power, out[tile:].shape)


def multiply(high, low, pieces, vox, far, near):
    levels = len(pieces)
    tile, depth = pieces[0][0].shape
    width = levels // vox * len(near) * tile
    flat = [pieces[d][i] for d in range(levels) for i in range(len(near))]
    call = kernel_call(
        functools.partial(multiply_kernel, vox, levels, far, near),
        [VMEM] * (2 + len(flat)),
        [jax.ShapeDtypeStruct((tile + (EXTRA if k else 0), width), jnp.float32) for k in range(vox * len(far))],
        [pltpu.VMEM((len(near), levels * tile, depth), jnp.bfloat16)],
    )
    return call(high, low, *flat)


def place_kernel(vox, slots, lines, far, near, *refs):
    blocks, out_ref = refs[:-1], refs[-1]
    tile = out_ref.shape[0]
    v, z, w = (lax.axis_index(a) for a in ("vox", "row", "wl"))
    rows = (z * lines + w) * tile + lax.broadcasted_iota(jnp.int32, (tile, tile), 0)
    for j, f in enumerate(far):
        for s in range(slots):
            for i, e in enumerate(near):
                src = slice((s * len(near) + i) * tile, (s * len(near) + i + 1) * tile)
                total = 0.0
                for t in range(vox):
                    block = blocks[t * len(far) + j]
                    scale = 1.0 if t == j == 0 else jnp.exp2(block[tile : tile + 1, :1])
                    total += block[:tile, src] * scale
                at = pl.multiple_of((s * lines + (w ^ f ^ e)) * tile, tile)
                cols = v * (slots * lines * tile) + at + lax.broadcasted_iota(jnp.int32, (tile, tile), 1)
                out_ref[:, pl.ds(at, tile)] = jnp.where(cols <= rows, total, 0.0)


def place(blocks, vox, slots, lines, far, near):
    tile = blocks[0].shape[0]
    call = kernel_call(
        functools.partial(place_kernel, vox, slots, lines, far, near),
        [VMEM] * len(blocks),
        [jax.ShapeDtypeStruct((tile, slots * lines * tile), jnp.float32)],
    )
    return call(*blocks)[0]


def on_device(jac, extinction, prior_var):
    vox, levels, lines = (lax.axis_size(a) for a in ("vox", "row", "wl"))
    slots = levels // vox
    far = [0, lines // 2] if lines > 1 else [0]
    near = list(range(max(lines // 2, 1)))

    rows = [jac] + [swap(jac, "wl", f) for f in far[1:]]

    below = {0: jac}
    for d in [1, levels - 1] + list(range(2, levels - 1)):
        if d not in below and d > 0:
            direct = d in (1, levels - 1)
            if d == 2:
                below[1], *rows[1:] = lax.optimization_barrier([below[1]] + rows[1:])
            below[d] = shift(jac if direct else below[d - 1], "row", d if direct else 1)
    high, low = weigh(extinction.T, prior_var, rows, far, near)
    for d in range(2, levels - 1):
        below[d], high, low = lax.optimization_barrier([below[d], high, low])
    pieces = [[below[d]] + [swap(below[d], "wl", e) for e in near[1:]] for d in range(levels)]

    shares = multiply(high, low, pieces, vox, far, near)
    blocks = []
    for t in range(vox):
        for j, f in enumerate(far):
            share = shares[t * len(far) + j]
            if t or f:
                share = send(share.astype(jnp.float16), t, f).astype(jnp.float32)
            blocks.append(share)
    return place(blocks, vox, slots, lines, far, near)


def solution(mesh):
    return jax.shard_map(
        on_device,
        mesh=mesh,
        in_specs=(P(("row", "wl"), "vox"), P(), P(None, "vox")),
        out_specs=P(("row", "wl"), "vox"),
        check_vma=False,
    )
```

time: 90.4 us -> 33.3 us (0.37)
  waiting for transfers between devices: 66.2 us -> 17.1 us
  between operations: 13.5 us -> 0.1 us
  starting transfers between devices: 0.04 us -> 11 us
  matrix products: 6.24 us -> 0 us
  Pallas kernels: 0 us -> 3.16 us
  other arithmetic: 1.95 us -> 0.13 us
    all_gather x1 -> x0, waiting for transfers between devices: 46.4 us -> none  [on_device(): portion = lax.all_gather(jacobian, ('row', 'wl'), axis=0, tiled=True)]
    reduce_scatter x1 -> x0, waiting for transfers between devices: 19.1 us -> none  [on_device(): summed = lax.psum_scatter(terms, 'vox', scatter_dimension=1, tiled=True)]
    ppermute x0 -> x11, waiting for transfers between devices: none -> 17.1 us  [the longest x3 8.82 us: shift(): return lax.ppermute(x, axis, [(i, (i + by) % size) for i in range(size)])]
    ppermute x0 -> x11, starting transfers between devices: none -> 11 us  [the longest x3 3.83 us: shift(): return lax.ppermute(x, axis, [(i, (i + by) % size) for i in range(size)])]
    dot_general x3 -> x0, matrix products: 6.24 us -> none  [the longest x1 2.96 us: contract(): lax.dot_general(left_rows.astype(jnp.float32), right_rows, (((1,), (1,)),...]
    pallas_call x0 -> x3, Pallas kernels: none -> 3.16 us  [the longest x1 1.36 us: multiply(): return call(high, low, *flat)]
    select_n x2 -> x0, other arithmetic: 1.94 us -> none  [the longest x1 1.94 us: on_device(): jnp.where(cols_global[None, :] <= rows_global[:, None], summed, jnp.float...]
    unnamed x2 -> x8, local copies, waits for them, and re-layouts: 0.01 us -> 1.61 us
  transfers between devices with their start and end apart: 2 -> 11, of which waited for: 2 -> 7; matrix products, arithmetic and copies ran while one was open for 2% -> 0% of each run, Pallas kernels for 0% -> 2%
where the time goes in v3:
time: 33.3 us; the launch traced here: 33.1 us
  waiting for transfers between devices  17.1 us (51%)
  starting transfers between devices  11 us (33%)
  Pallas kernels  3.16 us (9%)
  local copies, waits for them, and re-layouts  1.61 us (5%)
    ppermute x3, waiting for transfers between devices, shift(): return lax.ppermute(x, axis, [(i, (i + by) % size) for i in range(size)])  8.82 us
    ppermute x3, waiting for transfers between devices, send(): return lax.ppermute(x, ('vox', 'wl'), pairs)  6.31 us
    ppermute x3, starting transfers between devices, shift(): return lax.ppermute(x, axis, [(i, (i + by) % size) for i in range(size)])  3.83 us
    ppermute x3, starting transfers between devices, send(): return lax.ppermute(x, ('vox', 'wl'), pairs)  3.62 us
    ppermute x5, starting transfers between devices, swap(): return lax.ppermute(x, axis, [(i, i ^ bit) for i in range(size)])  3.55 us
    ppermute x5, waiting for transfers between devices, swap(): return lax.ppermute(x, axis, [(i, i ^ bit) for i in range(size)])  1.96 us
    unnamed x8, local copies, waits for them, and re-layouts  1.61 us
    pallas_call x1, Pallas kernels, multiply(): return call(high, low, *flat)  1.36 us
  transfers between devices with their start and end apart: 11, of which 7 were waited for; matrix products, arithmetic and copies ran while one was open for 0% of the time, Pallas kernels for 2%

profile of v3, /device:TPU:0, one launch (start us, length us, event | category | flops | bytes accessed | tf_op | source)
XLA Modules:
  0.0 33.1 jit_solution(5235088498538807139)
XLA Ops:
  0.0 0.0 copy-start.3
  0.0 3.0 %collective-permute-start.1 = (bf16[128,640]{1,0:T(8,128)(2,1)}, bf16[128,640]{1,0:T(8,128)(2,1)S(1)}, u32[]{:S(2)}, u32[]{:S(2)}) collective-permute-start(bf16[128,640]{1,0:T(8,128)(2,1)} %refs_0_.3), channel_id=1, source_target_pairs={{0,2},{1,3},{2,0},{3,1},{4,6},{5,7},{6,4},{7,5},{8,10},{9,11},{10,... | collective-permute-start | bytes 491528 | tf_op jit(solution)/shard_map/ppermute | solution.py:23
  3.0 1.6 %collective-permute-start = (bf16[128,640]{1,0:T(8,128)(2,1)}, bf16[128,640]{1,0:T(8,128)(2,1)S(1)}, u32[]{:S(2)}, u32[]{:S(2)}) collective-permute-start(bf16[128,640]{1,0:T(8,128)(2,1)} %refs_0_.3), channel_id=1, source_target_pairs={{0,4},{4,8},{8,12},{12,0},{1,5},{5,9},{9,13},{13,1},{2,6},{6,10},{... | collective-permute-start | bytes 491528 | tf_op jit(solution)/shard_map/ppermute | solution.py:18
  4.5 2.2 %collective-permute-start.6 = (bf16[128,640]{1,0:T(8,128)(2,1)}, bf16[128,640]{1,0:T(8,128)(2,1)S(1)}, u32[]{:S(2)}, u32[]{:S(2)}) collective-permute-start(bf16[128,640]{1,0:T(8,128)(2,1)} %refs_0_.3), channel_id=1, source_target_pairs={{0,12},{4,0},{8,4},{12,8},{1,13},{5,1},{9,5},{13,9},{2,14},{6,2},{... | collective-permute-start | bytes 491528 | tf_op jit(solution)/shard_map/ppermute | solution.py:18
  6.8 0.6 %collective-permute-done.1.refs_1_ = bf16[128,640]{1,0:T(8,128)(2,1)S(1)} collective-permute-done((bf16[128,640]{1,0:T(8,128)(2,1)}, bf16[128,640]{1,0:T(8,128)(2,1)S(1)}, u32[]{:S(2)}, u32[]{:S(2)}) %collective-permute-start.1) | collective-permute-done | bytes 163872 | tf_op jit(solution)/shard_map/ppermute | solution.py:23
  7.4 4.7 %collective-permute-done.refs_2_ = bf16[128,640]{1,0:T(8,128)(2,1)S(1)} collective-permute-done((bf16[128,640]{1,0:T(8,128)(2,1)}, bf16[128,640]{1,0:T(8,128)(2,1)S(1)}, u32[]{:S(2)}, u32[]{:S(2)}) %collective-permute-start) | collective-permute-done | bytes 163872 | tf_op jit(solution)/shard_map/ppermute | solution.py:18
  12.1 0.0 collective-permute-start.2
  12.1 0.0 collective-permute-start.3
  12.1 0.5 %collective-permute-start.4 = (bf16[128,640]{1,0:T(8,128)(2,1)S(1)}, bf16[128,640]{1,0:T(8,128)(2,1)S(1)}, u32[]{:S(2)}, u32[]{:S(2)}) collective-permute-start(bf16[128,640]{1,0:T(8,128)(2,1)S(1)} %collective-permute-done.refs_2_), channel_id=1, source_target_pairs={{0,1},{1,0},{2,3},{3,2},{4,5},{5,4},{6,7},{7,6},{8,9},{9,8},{10,11... | collective-permute-start | bytes 491528 | tf_op jit(solution)/shard_map/ppermute | solution.py:23
  12.6 0.0 copy-done.3
  12.6 0.0 copy-start
  12.6 0.9 %copy-done = bf16[128,640]{1,0:T(8,128)(2,1)S(1)} copy-done((bf16[128,640]{1,0:T(8,128)(2,1)S(1)}, bf16[128,640]{1,0:T(8,128)(2,1)}, u32[]{:S(2)}) %copy-start) | copy-done | bytes 163864
  13.6 0.0 copy-start.2
  13.6 0.7 %copy-done.2 = f32[2,640]{1,0:T(2,128)S(1)} copy-done((f32[2,640]{1,0:T(2,128)S(1)}, f32[2,640]{1,0:T(2,128)}, u32[]{:S(2)}) %copy-start.2) | copy-done | bytes 5144
  14.2 0.0 copy-start.1
  14.2 0.8 %shard_map.37 = (bf16[2,256,640]{2,1,0:T(8,128)(2,1)S(1)}, bf16[2,256,640]{2,1,0:T(8,128)(2,1)S(1)}) custom-call(f32[2,4]{1,0:T(2,128)S(1)} %bitcast.1, f32[2,640]{1,0:T(2,128)S(1)} %copy-done.2, bf16[128,640]{1,0:T(8,128)(2,1)S(1)} %copy-done, bf16[128,640]{1,0:T(8,128)(2,1)S(1)} %collective-permute-done.1.refs_1_), custom_call_target="tpu_custom_call" | custom-call | tf_op jit(solution)/shard_map/pallas_call | solution.py:69
  15.1 0.0 collective-permute-done.6.refs_6_
  15.1 0.1 collective-permute-start.7
  15.2 4.1 %collective-permute-done.2.refs_4_ = bf16[128,640]{1,0:T(8,128)(2,1)S(1)} collective-permute-done((bf16[128,640]{1,0:T(8,128)(2,1)S(1)}, bf16[128,640]{1,0:T(8,128)(2,1)S(1)}, u32[]{:S(2)}, u32[]{:S(2)}) %collective-permute-start.2) | collective-permute-done | bytes 163872 | tf_op jit(solution)/shard_map/ppermute | solution.py:18
  19.2 0.0 collective-permute-start.5
  19.2 0.0 collective-permute-done.3.refs_1_
  19.2 0.0 collective-permute-done.4.refs_3_
  19.3 0.0 collective-permute-done.7.refs_7_
  19.3 1.4 %collective-permute-done.5.refs_5_ = bf16[128,640]{1,0:T(8,128)(2,1)S(1)} collective-permute-done((bf16[128,640]{1,0:T(8,128)(2,1)S(1)}, bf16[128,640]{1,0:T(8,128)(2,1)S(1)}, u32[]{:S(2)}, u32[]{:S(2)}) %collective-permute-start.5) | collective-permute-done | bytes 163872 | tf_op jit(solution)/shard_map/ppermute | solution.py:23
  20.6 0.0 copy-done.1
  20.6 1.4 %shard_map.38 = (f32[128,512]{1,0:T(8,128)S(1)}, f32[144,512]{1,0:T(8,128)S(1)}, f32[144,512]{1,0:T(8,128)S(1)}, f32[144,512]{1,0:T(8,128)S(1)}) custom-call(bf16[2,256,640]{2,1,0:T(8,128)(2,1)S(1)} %get-tuple-element.20.high_ref, bf16[2,256,640]{2,1,0:T(8,128)(2,1)S(1)} %get-tuple-element.21.low_ref, bf16[128,640]{1,0:T(8,128)(2,1)S(1)} %copy-done.1, ...), custom_call_target="tpu_custom_call" | custom-call | tf_op jit(solution)/shard_map/pallas_call | solution.py:120
  22.1 1.5 %collective-permute-start.10 = (f16[144,512]{1,0:T(8,128)(2,1)S(1)}, f16[144,512]{1,0:T(8,128)(2,1)S(1)}, u32[]{:S(2)}, u32[]{:S(2)}) collective-permute-start(f16[144,512]{1,0:T(8,128)(2,1)S(1)} %convert_element_type.22), channel_id=1, source_target_pairs={{0,18},{1,19},{2,16},{3,17},{16,2},{17,3},{18,0},{19,1},{4,22},{5,... | collective-permute-start | bytes 442376 | tf_op jit(solution)/shard_map/ppermute | solution.py:31
  23.6 0.3 %collective-permute-start.9 = (f16[144,512]{1,0:T(8,128)(2,1)S(1)}, f16[144,512]{1,0:T(8,128)(2,1)S(1)}, u32[]{:S(2)}, u32[]{:S(2)}) collective-permute-start(f16[144,512]{1,0:T(8,128)(2,1)S(1)} %convert_element_type.20), channel_id=1, source_target_pairs={{0,16},{1,17},{2,18},{3,19},{16,0},{17,1},{18,2},{19,3},{4,20},{5,... | collective-permute-start | bytes 442376 | tf_op jit(solution)/shard_map/ppermute | solution.py:31
  23.9 1.8 %collective-permute-start.8 = (f16[144,512]{1,0:T(8,128)(2,1)S(1)}, f16[144,512]{1,0:T(8,128)(2,1)S(1)}, u32[]{:S(2)}, u32[]{:S(2)}) collective-permute-start(f16[144,512]{1,0:T(8,128)(2,1)S(1)} %convert_element_type.18), channel_id=1, source_target_pairs={{0,2},{1,3},{2,0},{3,1},{16,18},{17,19},{18,16},{19,17},{4,6},{5,7... | collective-permute-start | bytes 442376 | tf_op jit(solution)/shard_map/ppermute | solution.py:31
  25.7 4.1 %collective-permute-done.10 = f16[144,512]{1,0:T(8,128)(2,1)S(1)} collective-permute-done((f16[144,512]{1,0:T(8,128)(2,1)S(1)}, f16[144,512]{1,0:T(8,128)(2,1)S(1)}, u32[]{:S(2)}, u32[]{:S(2)}) %collective-permute-start.10) | collective-permute-done | bytes 147488 | tf_op jit(solution)/shard_map/ppermute | solution.py:31
  29.8 1.1 %collective-permute-done.9 = f16[144,512]{1,0:T(8,128)(2,1)S(1)} collective-permute-done((f16[144,512]{1,0:T(8,128)(2,1)S(1)}, f16[144,512]{1,0:T(8,128)(2,1)S(1)}, u32[]{:S(2)}, u32[]{:S(2)}) %collective-permute-start.9) | collective-permute-done | bytes 147488 | tf_op jit(solution)/shard_map/ppermute | solution.py:31
  31.0 1.1 %collective-permute-done.8 = f16[144,512]{1,0:T(8,128)(2,1)S(1)} collective-permute-done((f16[144,512]{1,0:T(8,128)(2,1)S(1)}, f16[144,512]{1,0:T(8,128)(2,1)S(1)}, u32[]{:S(2)}, u32[]{:S(2)}) %collective-permute-start.8) | collective-permute-done | bytes 147488 | tf_op jit(solution)/shard_map/ppermute | solution.py:31
  32.1 1.0 %shard_map.39 = f32[128,1024]{1,0:T(8,128)} custom-call(f32[128,512]{1,0:T(8,128)S(1)} %get-tuple-element.23.refs_0_, f32[144,512]{1,0:T(8,128)S(1)} %convert_element_type.19.refs_1_, f32[144,512]{1,0:T(8,128)S(1)} %convert_element_type.21.refs_2_, f32[144,512]{1,0:T(8,128)S(1)} %convert_element_type.23.refs_3_), custom_call_target="tpu_custom_call" | custom-call | tf_op jit(solution)/shard_map/pallas_call | solution.py:149
  (6 shorter events, 0.1 us)
Async XLA Ops:
  0.0 12.6 %copy-start.3 = (f32[4,2]{0,1:T(2,128)S(1)}, f32[4,2]{0,1:T(2,128)}, u32[]{:S(2)}) copy-start(f32[4,2]{0,1:T(2,128)} %param.4) | copy-start | bytes 100
  0.0 7.4 %collective-permute-start.1 = (bf16[128,640]{1,0:T(8,128)(2,1)}, bf16[128,640]{1,0:T(8,128)(2,1)S(1)}, u32[]{:S(2)}, u32[]{:S(2)}) collective-permute-start(bf16[128,640]{1,0:T(8,128)(2,1)} %refs_0_.3), channel_id=1, source_target_pairs={{0,2},{1,3},{2,0},{3,1},{4,6},{5,7},{6,4},{7,5},{8,10},{9,11},{10,... | collective-permute-start | bytes 491528 | tf_op jit(solution)/shard_map/ppermute | solution.py:23
  3.0 9.2 %collective-permute-start = (bf16[128,640]{1,0:T(8,128)(2,1)}, bf16[128,640]{1,0:T(8,128)(2,1)S(1)}, u32[]{:S(2)}, u32[]{:S(2)}) collective-permute-start(bf16[128,640]{1,0:T(8,128)(2,1)} %refs_0_.3), channel_id=1, source_target_pairs={{0,4},{4,8},{8,12},{12,0},{1,5},{5,9},{9,13},{13,1},{2,6},{6,10},{... | collective-permute-start | bytes 491528 | tf_op jit(solution)/shard_map/ppermute | solution.py:18
  4.5 10.5 %collective-permute-start.6 = (bf16[128,640]{1,0:T(8,128)(2,1)}, bf16[128,640]{1,0:T(8,128)(2,1)S(1)}, u32[]{:S(2)}, u32[]{:S(2)}) collective-permute-start(bf16[128,640]{1,0:T(8,128)(2,1)} %refs_0_.3), channel_id=1, source_target_pairs={{0,12},{4,0},{8,4},{12,8},{1,13},{5,1},{9,5},{13,9},{2,14},{6,2},{... | collective-permute-start | bytes 491528 | tf_op jit(solution)/shard_map/ppermute | solution.py:18
  12.1 7.1 %collective-permute-start.2 = (bf16[128,640]{1,0:T(8,128)(2,1)S(1)}, bf16[128,640]{1,0:T(8,128)(2,1)S(1)}, u32[]{:S(2)}, u32[]{:S(2)}) collective-permute-start(bf16[128,640]{1,0:T(8,128)(2,1)S(1)} %collective-permute-done.refs_2_), channel_id=1, source_target_pairs={{0,4},{4,8},{8,12},{12,0},{1,5},{5,9},{9,13},{13,1},{2,6},{6,10},{... | collective-permute-start | bytes 491528 | tf_op jit(solution)/shard_map/ppermute | solution.py:18
  12.1 7.1 %collective-permute-start.3 = (bf16[128,640]{1,0:T(8,128)(2,1)}, bf16[128,640]{1,0:T(8,128)(2,1)S(1)}, u32[]{:S(2)}, u32[]{:S(2)}) collective-permute-start(bf16[128,640]{1,0:T(8,128)(2,1)} %refs_0_.3), channel_id=1, source_target_pairs={{0,1},{1,0},{2,3},{3,2},{4,5},{5,4},{6,7},{7,6},{8,9},{9,8},{10,11... | collective-permute-start | bytes 491528 | tf_op jit(solution)/shard_map/ppermute | solution.py:23
  12.1 7.1 %collective-permute-start.4 = (bf16[128,640]{1,0:T(8,128)(2,1)S(1)}, bf16[128,640]{1,0:T(8,128)(2,1)S(1)}, u32[]{:S(2)}, u32[]{:S(2)}) collective-permute-start(bf16[128,640]{1,0:T(8,128)(2,1)S(1)} %collective-permute-done.refs_2_), channel_id=1, source_target_pairs={{0,1},{1,0},{2,3},{3,2},{4,5},{5,4},{6,7},{7,6},{8,9},{9,8},{10,11... | collective-permute-start | bytes 491528 | tf_op jit(solution)/shard_map/ppermute | solution.py:23
  12.6 0.9 %copy-start = (bf16[128,640]{1,0:T(8,128)(2,1)S(1)}, bf16[128,640]{1,0:T(8,128)(2,1)}, u32[]{:S(2)}) copy-start(bf16[128,640]{1,0:T(8,128)(2,1)} %refs_0_.3) | copy-start | bytes 491524
  13.6 0.7 %copy-start.2 = (f32[2,640]{1,0:T(2,128)S(1)}, f32[2,640]{1,0:T(2,128)}, u32[]{:S(2)}) copy-start(f32[2,640]{1,0:T(2,128)} %prior_ref.1) | copy-start | bytes 15364
  14.2 6.4 %copy-start.1 = (bf16[128,640]{1,0:T(8,128)(2,1)S(1)}, bf16[128,640]{1,0:T(8,128)(2,1)}, u32[]{:S(2)}) copy-start(bf16[128,640]{1,0:T(8,128)(2,1)} %refs_0_.3) | copy-start | bytes 491524
  15.1 4.2 %collective-permute-start.7 = (bf16[128,640]{1,0:T(8,128)(2,1)S(1)}, bf16[128,640]{1,0:T(8,128)(2,1)S(1)}, u32[]{:S(2)}, u32[]{:S(2)}) collective-permute-start(bf16[128,640]{1,0:T(8,128)(2,1)S(1)} %collective-permute-done.6.refs_6_), channel_id=1, source_target_pairs={{0,1},{1,0},{2,3},{3,2},{4,5},{5,4},{6,7},{7,6},{8,9},{9,8},{10,11... | collective-permute-start | bytes 491528 | tf_op jit(solution)/shard_map/ppermute | solution.py:23
  19.2 1.4 %collective-permute-start.5 = (bf16[128,640]{1,0:T(8,128)(2,1)S(1)}, bf16[128,640]{1,0:T(8,128)(2,1)S(1)}, u32[]{:S(2)}, u32[]{:S(2)}) collective-permute-start(bf16[128,640]{1,0:T(8,128)(2,1)S(1)} %collective-permute-done.2.refs_4_), channel_id=1, source_target_pairs={{0,1},{1,0},{2,3},{3,2},{4,5},{5,4},{6,7},{7,6},{8,9},{9,8},{10,11... | collective-permute-start | bytes 491528 | tf_op jit(solution)/shard_map/ppermute | solution.py:23
  22.1 7.7 %collective-permute-start.10 = (f16[144,512]{1,0:T(8,128)(2,1)S(1)}, f16[144,512]{1,0:T(8,128)(2,1)S(1)}, u32[]{:S(2)}, u32[]{:S(2)}) collective-permute-start(f16[144,512]{1,0:T(8,128)(2,1)S(1)} %convert_element_type.22), channel_id=1, source_target_pairs={{0,18},{1,19},{2,16},{3,17},{16,2},{17,3},{18,0},{19,1},{4,22},{5,... | collective-permute-start | bytes 442376 | tf_op jit(solution)/shard_map/ppermute | solution.py:31
  23.6 7.4 %collective-permute-start.9 = (f16[144,512]{1,0:T(8,128)(2,1)S(1)}, f16[144,512]{1,0:T(8,128)(2,1)S(1)}, u32[]{:S(2)}, u32[]{:S(2)}) collective-permute-start(f16[144,512]{1,0:T(8,128)(2,1)S(1)} %convert_element_type.20), channel_id=1, source_target_pairs={{0,16},{1,17},{2,18},{3,19},{16,0},{17,1},{18,2},{19,3},{4,20},{5,... | collective-permute-start | bytes 442376 | tf_op jit(solution)/shard_map/ppermute | solution.py:31
  23.9 8.2 %collective-permute-start.8 = (f16[144,512]{1,0:T(8,128)(2,1)S(1)}, f16[144,512]{1,0:T(8,128)(2,1)S(1)}, u32[]{:S(2)}, u32[]{:S(2)}) collective-permute-start(f16[144,512]{1,0:T(8,128)(2,1)S(1)} %convert_element_type.18), channel_id=1, source_target_pairs={{0,2},{1,3},{2,0},{3,1},{16,18},{17,19},{18,16},{19,17},{4,6},{5,7... | collective-permute-start | bytes 442376 | tf_op jit(solution)/shard_map/ppermute | solution.py:31

commit v4 on v3

v4 whole, which is shorter than its diff:
```python
import functools

import jax
import jax.numpy as jnp
from jax import lax
from jax.experimental import pallas as pl
from jax.experimental.pallas import tpu as pltpu
from jax.sharding import PartitionSpec as P

LIMIT = 16 * 2**20
EXTRA = 16
SMEM = pl.BlockSpec(memory_space=pltpu.SMEM)
VMEM = pl.BlockSpec(memory_space=pltpu.VMEM)


def shift(x, axis, by):
    size = lax.axis_size(axis)
    return lax.ppermute(x, axis, [(i, (i + by) % size) for i in range(size)])


def climb(x, by, lowest, count):
    return lax.ppermute(x, "row", [(i - by, i) for i in range(lowest, lowest + count)])


def swap(x, axis, bit):
    size = lax.axis_size(axis)
    return lax.ppermute(x, axis, [(i, i ^ bit) for i in range(size)])


def send(x, by, bit):
    vox, lines = lax.axis_size("vox"), lax.axis_size("wl")
    pairs = [
        (v * lines + w, (v + by) % vox * lines + (w ^ bit)) for v in range(vox) for w in range(lines)
    ]
    return lax.ppermute(x, ("vox", "wl"), pairs)


def kernel_call(kernel, ins, outs, scratch=()):
    return functools.partial(
        pl.pallas_call,
        kernel,
        in_specs=ins,
        out_specs=[VMEM] * len(outs),
        out_shape=outs,
        scratch_shapes=scratch,
        compiler_params=pltpu.CompilerParams(vmem_limit_bytes=LIMIT),
    )()


def ready(dist, levels):
    return jnp.where(dist <= 1, dist, jnp.where(dist == levels - 1, 2, dist + 1))


def choose(vox, level, phase, slots, levels):
    dists = [jnp.maximum(level - (vox * slots + s), 0) for s in range(slots)]
    keys = [ready(d, levels) for d in dists]
    slot = dist = jnp.int32(0)
    for s in range(slots):
        rank = jnp.int32(0)
        for o in range(slots):
            if o != s:
                first = keys[o] <= keys[s] if o < s else keys[o] < keys[s]
                rank += first.astype(jnp.int32)
        slot = jnp.where(rank == phase, s, slot)
        dist = jnp.where(rank == phase, dists[s], dist)
    return slot, dist


def used(phase, slots, levels):
    out = set()
    rank = lambda d: d if d <= 1 else 2 if d == levels - 1 else d + 1
    for v in range(levels // slots):
        for z in range(levels):
            ds = [max(z - (v * slots + s), 0) for s in range(slots)]
            out.add(sorted(ds, key=rank)[phase])
    return sorted(out)


def prepare_kernel(far, near, extinction_ref, prior_ref, jac_ref, weights_ref, own_ref):
    chroms, waves = extinction_ref.shape
    w = lax.axis_index("wl")
    for i, e in enumerate(near):
        for j, f in enumerate(far):
            weight = 0.0
            for c in range(chroms):
                coeff = extinction_ref[c, lax.rem(w ^ f, waves)] * extinction_ref[c, lax.rem(w ^ e, waves)]
                weight += coeff * prior_ref[c : c + 1, :]
            weights_ref[i * len(far) + j : i * len(far) + j + 1, :] = weight
    own_ref[...] = jac_ref[...]


def prepare(extinction, prior, jac, far, near):
    weights = jax.ShapeDtypeStruct((len(far) * len(near), jac.shape[1]), jnp.float32)
    own = jax.ShapeDtypeStruct(jac.shape, jac.dtype)
    call = kernel_call(functools.partial(prepare_kernel, far, near), [SMEM, VMEM, VMEM], [weights, own])
    return call(extinction, prior, jac)


def weigh_kernel(far, near, weights_ref, *refs):
    rows, (high_ref, low_ref) = refs[:-2], refs[-2:]
    tile = rows[0].shape[0]
    for i in range(len(near)):
        for j in range(len(far)):
            k = i * len(far) + j
            scaled = rows[j][...].astype(jnp.float32) * weights_ref[k : k + 1, :]
            top = scaled.astype(jnp.bfloat16)
            high_ref[i, j * tile : (j + 1) * tile, :] = top
            low_ref[i, j * tile : (j + 1) * tile, :] = (scaled - top.astype(jnp.float32)).astype(jnp.bfloat16)


def weigh(weights, rows, far, near):
    tile, depth = rows[0].shape
    like = jax.ShapeDtypeStruct((len(near), len(far) * tile, depth), jnp.bfloat16)
    call = kernel_call(functools.partial(weigh_kernel, far, near), [VMEM] * (1 + len(rows)), [like, like])
    return call(weights, *rows)


def multiply_kernel(vox, levels, phases, dists, far, near, high_ref, low_ref, *refs):
    count = len(dists) * len(near)
    pieces, outs, cols_ref = refs[:count], refs[count:-1], refs[-1]
    tile = pieces[0].shape[0]
    v, z = lax.axis_index("vox"), lax.axis_index("row")
    parts = [(t, p) for t in range(vox) for p in range(len(phases))]
    for n, (t, p) in enumerate(parts):
        _, dist = choose(lax.rem(v + t, vox), z, phases[p], levels // vox, levels)
        for k, d in enumerate(dists):

            @pl.when(dist == d)
            def _():
                for i in range(len(near)):
                    cols_ref[i, n * tile : (n + 1) * tile] = pieces[k * len(near) + i][...]

    for i in range(len(near)):
        total = 0.0
        for part in (high_ref, low_ref):
            total += lax.dot_general(
                part[i], cols_ref[i], (((1,), (1,)), ((), ())), preferred_element_type=jnp.float32
            )
        for n, (t, p) in enumerate(parts):
            to = (p * len(near) + i) * tile
            for j in range(len(far)):
                outs[t * len(far) + j][:tile, to : to + tile] = total[
                    j * tile : (j + 1) * tile, n * tile : (n + 1) * tile
                ]
    for out in outs[1:]:
        largest = jnp.max(jnp.abs(out[:tile]), axis=(0, 1), keepdims=True)
        power = jnp.floor(jnp.log2(jnp.maximum(largest, 1e-30))) - 13.0
        out[:tile] *= jnp.exp2(-power)
        out[tile:] = jnp.broadcast_to(power, out[tile:].shape)


def multiply(high, low, pieces, vox, phases, far, near):
    levels = len(pieces)
    tile, depth = pieces[0][0].shape
    dists = sorted(set().union(*[used(p, levels // vox, levels) for p in phases]))
    flat = [pieces[d][i] for d in dists for i in range(len(near))]
    heights = [tile] + [tile + EXTRA] * (vox * len(far) - 1)
    width = len(phases) * len(near) * tile
    call = kernel_call(
        functools.partial(multiply_kernel, vox, levels, phases, dists, far, near),
        [VMEM] * (2 + len(flat)),
        [jax.ShapeDtypeStruct((height, width), jnp.float32) for height in heights],
        [pltpu.VMEM((len(near), vox * len(phases) * tile, depth), jnp.bfloat16)],
    )
    return call(high, low, *flat)


def place_kernel(vox, levels, lines, groups, far, near, *refs):
    blocks, out_ref = refs[:-1], refs[-1]
    tile, slots = out_ref.shape[0], levels // vox
    v, z, w = (lax.axis_index(a) for a in ("vox", "row", "wl"))
    rows = (z * lines + w) * tile + lax.broadcasted_iota(jnp.int32, (tile, tile), 0)
    for g, phases in enumerate(groups):
        for p, phase in enumerate(phases):
            slot, _ = choose(v, z, phase, slots, levels)
            for j, f in enumerate(far):
                for i, e in enumerate(near):
                    src = slice((p * len(near) + i) * tile, (p * len(near) + i + 1) * tile)
                    total = 0.0
                    for t in range(vox):
                        block = blocks[(g * vox + t) * len(far) + j]
                        scale = 1.0 if t == j == 0 else jnp.exp2(block[tile : tile + 1, :1])
                        total += block[:tile, src] * scale
                    at = pl.multiple_of((slot * lines + (w ^ f ^ e)) * tile, tile)
                    cols = v * (slots * lines * tile) + at + lax.broadcasted_iota(jnp.int32, (tile, tile), 1)
                    out_ref[:, pl.ds(at, tile)] = jnp.where(cols <= rows, total, 0.0)


def place(blocks, vox, levels, lines, groups, far, near):
    tile = blocks[0].shape[0]
    call = kernel_call(
        functools.partial(place_kernel, vox, levels, lines, groups, far, near),
        [VMEM] * len(blocks),
        [jax.ShapeDtypeStruct((tile, levels // vox * lines * tile), jnp.float32)],
    )
    return call(*blocks)[0]


def on_device(jac, extinction, prior_var):
    vox, levels, lines = (lax.axis_size(a) for a in ("vox", "row", "wl"))
    slots = levels // vox
    far = [0, lines // 2] if lines > 1 else [0]
    near = list(range(max(lines // 2, 1)))

    groups = [list(range(slots))]

    below = {0: jac}
    if levels > 1:
        below[1] = shift(jac, "row", 1)
    others = [swap(jac, "wl", f) for f in far[1:]]
    if levels > 2:
        below[levels - 1] = climb(jac, levels - 1, levels - 1, 1)
    weights, own = prepare(extinction.T, prior_var, jac, far, near)
    if levels > 1:
        below[1], weights, own = lax.optimization_barrier([below[1], weights, own])
    for d in range(2, levels - 1):
        below[d] = climb(below[d - 1], 1, d, levels - d)
    high, low = weigh(weights, [own] + others, far, near)
    below[0] = own
    for d in range(2, levels - 1):
        below[d], high, low = lax.optimization_barrier([below[d], high, low])
    pieces = [[below[d]] + [swap(below[d], "wl", e) for e in near[1:]] for d in range(levels)]

    blocks = []
    for phases in groups:
        shares = multiply(high, low, pieces, vox, phases, far, near)
        for t in range(vox):
            for j, f in enumerate(far):
                share = shares[t * len(far) + j]
                if t or f:
                    share = send(share.astype(jnp.float16), t, f).astype(jnp.float32)
                blocks.append(share)
    return place(blocks, vox, levels, lines, groups, far, near)


def solution(mesh):
    return jax.shard_map(
        on_device,
        mesh=mesh,
        in_specs=(P(("row", "wl"), "vox"), P(), P(None, "vox")),
        out_specs=P(("row", "wl"), "vox"),
        check_vma=False,
    )
```

time: 33.3 us -> 27.9 us (0.84)
  waiting for transfers between devices: 17.1 us -> 8.52 us
  starting transfers between devices: 11 us -> 13.8 us
    ppermute x3 -> x1, waiting for transfers between devices: 8.82 us -> 0.01 us  [shift(): return lax.ppermute(x, axis, [(i, (i + by) % size) for i in range(size)])]
    ppermute x0 -> x2, starting transfers between devices: none -> 4.74 us  [climb(): lax.ppermute(x, 'row', [(i - by, i) for i in range(lowest, lowest + count)])]
    ppermute x5, starting transfers between devices: 3.55 us -> 2.38 us  [swap(): return lax.ppermute(x, axis, [(i, i ^ bit) for i in range(size)])]
    ppermute x3 -> x1, starting transfers between devices: 3.83 us -> 3.02 us  [shift(): return lax.ppermute(x, axis, [(i, (i + by) % size) for i in range(size)])]
    unnamed x8 -> x6, local copies, waits for them, and re-layouts: 1.61 us -> 1.64 us
    pallas_call x1 -> x2, Pallas kernels: 0.82 us -> 0.83 us  [the longest x1 0.58 us: prepare(): return call(extinction, prior, jac)]
  transfers between devices with their start and end apart: 11 -> 11, of which waited for: 7 -> 5; matrix products, arithmetic and copies ran while one was open for 0% -> 0% of each run, Pallas kernels for 2% -> 3%
where the time goes in v4:
time: 27.9 us; the launch traced here: 27.4 us
  starting transfers between devices  13.8 us (49%)
  waiting for transfers between devices  8.52 us (31%)
  Pallas kernels  3.19 us (11%)
  local copies, waits for them, and re-layouts  1.64 us (6%)
    ppermute x3, waiting for transfers between devices, send(): return lax.ppermute(x, ('vox', 'wl'), pairs)  6.44 us
    ppermute x2, starting transfers between devices, climb(): lax.ppermute(x, 'row', [(i - by, i) for i in range(lowest, lowest + count)])  4.74 us
    ppermute x3, starting transfers between devices, send(): return lax.ppermute(x, ('vox', 'wl'), pairs)  3.62 us
    ppermute x1, starting transfers between devices, shift(): return lax.ppermute(x, axis, [(i, (i + by) % size) for i in range(size)])  3.02 us
    ppermute x5, starting transfers between devices, swap(): return lax.ppermute(x, axis, [(i, i ^ bit) for i in range(size)])  2.38 us
    ppermute x5, waiting for transfers between devices, swap(): return lax.ppermute(x, axis, [(i, i ^ bit) for i in range(size)])  2.07 us
    unnamed x6, local copies, waits for them, and re-layouts  1.64 us
    pallas_call x1, Pallas kernels, multiply(): return call(high, low, *flat)  1.36 us
  transfers between devices with their start and end apart: 11, of which 5 were waited for; matrix products, arithmetic and copies ran while one was open for 0% of the time, Pallas kernels for 3%

profile of v4, /device:TPU:0, one launch (start us, length us, event | category | flops | bytes accessed | tf_op | source)
XLA Modules:
  0.0 27.4 jit_solution(2208301274944746097)
XLA Ops:
  0.0 0.0 copy-start.2
  0.0 3.0 %collective-permute-start = (bf16[128,640]{1,0:T(8,128)(2,1)}, bf16[128,640]{1,0:T(8,128)(2,1)S(1)}, u32[]{:S(2)}, u32[]{:S(2)}) collective-permute-start(bf16[128,640]{1,0:T(8,128)(2,1)} %jac_ref.1), channel_id=1, source_target_pairs={{0,4},{4,8},{8,12},{12,0},{1,5},{5,9},{9,13},{13,1},{2,6},{6,10},{... | collective-permute-start | bytes 491528 | tf_op jit(solution)/shard_map/ppermute | solution.py:18
  3.0 4.1 %collective-permute-start.6 = (bf16[128,640]{1,0:T(8,128)(2,1)}, bf16[128,640]{1,0:T(8,128)(2,1)S(1)}, u32[]{:S(2)}, u32[]{:S(2)}) collective-permute-start(bf16[128,640]{1,0:T(8,128)(2,1)} %jac_ref.1), channel_id=1, source_target_pairs={{0,12},{1,13},{2,14},{3,15},{16,28},{17,29},{18,30},{19,31}} | collective-permute-start | bytes 491528 | tf_op jit(solution)/shard_map/ppermute | solution.py:22
  7.1 1.7 %collective-permute-start.2 = (bf16[128,640]{1,0:T(8,128)(2,1)}, bf16[128,640]{1,0:T(8,128)(2,1)S(1)}, u32[]{:S(2)}, u32[]{:S(2)}) collective-permute-start(bf16[128,640]{1,0:T(8,128)(2,1)} %jac_ref.1), channel_id=1, source_target_pairs={{0,2},{1,3},{2,0},{3,1},{4,6},{5,7},{6,4},{7,5},{8,10},{9,11},{10,... | collective-permute-start | bytes 491528 | tf_op jit(solution)/shard_map/ppermute | solution.py:27
  8.8 0.0 copy-done.2
  8.8 0.0 copy-start
  8.8 0.9 %copy-done = bf16[128,640]{1,0:T(8,128)(2,1)S(1)} copy-done((bf16[128,640]{1,0:T(8,128)(2,1)S(1)}, bf16[128,640]{1,0:T(8,128)(2,1)}, u32[]{:S(2)}) %copy-start) | copy-done | bytes 163864
  9.7 0.0 copy-start.1
  9.7 0.7 %copy-done.1 = f32[2,640]{1,0:T(2,128)S(1)} copy-done((f32[2,640]{1,0:T(2,128)S(1)}, f32[2,640]{1,0:T(2,128)}, u32[]{:S(2)}) %copy-start.1) | copy-done | bytes 5144
  10.4 0.6 %shard_map.37 = (f32[4,640]{1,0:T(4,128)S(1)}, bf16[128,640]{1,0:T(8,128)(2,1)S(1)}) custom-call(f32[2,4]{1,0:T(2,128)S(1)} %bitcast.1, f32[2,640]{1,0:T(2,128)S(1)} %copy-done.1, bf16[128,640]{1,0:T(8,128)(2,1)S(1)} %copy-done), custom_call_target="tpu_custom_call" | custom-call | tf_op jit(solution)/shard_map/pallas_call | solution.py:96
  11.0 0.0 collective-permute-done.refs_2_
  11.0 0.7 %collective-permute-start.1 = (bf16[128,640]{1,0:T(8,128)(2,1)S(1)}, bf16[128,640]{1,0:T(8,128)(2,1)S(1)}, u32[]{:S(2)}, u32[]{:S(2)}) collective-permute-start(bf16[128,640]{1,0:T(8,128)(2,1)S(1)} %collective-permute-done.refs_2_), channel_id=1, source_target_pairs={{4,8},{8,12},{5,9},{9,13},{6,10},{10,14},{7,11},{11,15},{20,24},{2... | collective-permute-start | bytes 491528 | tf_op jit(solution)/shard_map/ppermute | solution.py:22
  11.7 0.1 collective-permute-start.4
  11.8 0.5 %collective-permute-start.3 = (bf16[128,640]{1,0:T(8,128)(2,1)S(1)}, bf16[128,640]{1,0:T(8,128)(2,1)S(1)}, u32[]{:S(2)}, u32[]{:S(2)}) collective-permute-start(bf16[128,640]{1,0:T(8,128)(2,1)S(1)} %get-tuple-element.23.refs_0_), channel_id=1, source_target_pairs={{0,1},{1,0},{2,3},{3,2},{4,5},{5,4},{6,7},{7,6},{8,9},{9,8},{10,11... | collective-permute-start | bytes 491528 | tf_op jit(solution)/shard_map/ppermute | solution.py:27
  12.3 0.0 collective-permute-done.6.refs_6_
  12.3 0.1 collective-permute-start.7
  12.3 0.7 %collective-permute-done.2.refs_1_ = bf16[128,640]{1,0:T(8,128)(2,1)S(1)} collective-permute-done((bf16[128,640]{1,0:T(8,128)(2,1)}, bf16[128,640]{1,0:T(8,128)(2,1)S(1)}, u32[]{:S(2)}, u32[]{:S(2)}) %collective-permute-start.2) | collective-permute-done | bytes 163872 | tf_op jit(solution)/shard_map/ppermute | solution.py:27
  13.0 0.3 shard_map.38
  13.3 0.0 collective-permute-done.1.refs_4_
  13.3 0.1 collective-permute-start.5
  13.4 0.3 %collective-permute-done.7.refs_7_ = bf16[128,640]{1,0:T(8,128)(2,1)S(1)} collective-permute-done((bf16[128,640]{1,0:T(8,128)(2,1)S(1)}, bf16[128,640]{1,0:T(8,128)(2,1)S(1)}, u32[]{:S(2)}, u32[]{:S(2)}) %collective-permute-start.7) | collective-permute-done | bytes 163872 | tf_op jit(solution)/shard_map/ppermute | solution.py:27
  13.7 0.0 collective-permute-done.4.refs_3_
  13.7 0.0 collective-permute-done.3.refs_1_
  13.7 1.1 %collective-permute-done.5.refs_5_ = bf16[128,640]{1,0:T(8,128)(2,1)S(1)} collective-permute-done((bf16[128,640]{1,0:T(8,128)(2,1)S(1)}, bf16[128,640]{1,0:T(8,128)(2,1)S(1)}, u32[]{:S(2)}, u32[]{:S(2)}) %collective-permute-start.5) | collective-permute-done | bytes 163872 | tf_op jit(solution)/shard_map/ppermute | solution.py:27
  14.8 1.4 %shard_map.39 = (f32[128,512]{1,0:T(8,128)S(1)}, f32[144,512]{1,0:T(8,128)S(1)}, f32[144,512]{1,0:T(8,128)S(1)}, f32[144,512]{1,0:T(8,128)S(1)}) custom-call(bf16[2,256,640]{2,1,0:T(8,128)(2,1)S(1)} %get-tuple-element.26.high_ref, bf16[2,256,640]{2,1,0:T(8,128)(2,1)S(1)} %get-tuple-element.27.low_ref, bf16[128,640]{1,0:T(8,128)(2,1)S(1)} %get-tuple-element.23.refs_0_, ...), custom_call_target="tpu_custom_call" | custom-call | tf_op jit(solution)/shard_map/pallas_call | solution.py:165
  16.2 2.5 %collective-permute-start.10 = (f16[144,512]{1,0:T(8,128)(2,1)S(1)}, f16[144,512]{1,0:T(8,128)(2,1)S(1)}, u32[]{:S(2)}, u32[]{:S(2)}) collective-permute-start(f16[144,512]{1,0:T(8,128)(2,1)S(1)} %convert_element_type.22), channel_id=1, source_target_pairs={{0,18},{1,19},{2,16},{3,17},{16,2},{17,3},{18,0},{19,1},{4,22},{5,... | collective-permute-start | bytes 442376 | tf_op jit(solution)/shard_map/ppermute | solution.py:35
  18.7 0.5 %collective-permute-start.9 = (f16[144,512]{1,0:T(8,128)(2,1)S(1)}, f16[144,512]{1,0:T(8,128)(2,1)S(1)}, u32[]{:S(2)}, u32[]{:S(2)}) collective-permute-start(f16[144,512]{1,0:T(8,128)(2,1)S(1)} %convert_element_type.20), channel_id=1, source_target_pairs={{0,16},{1,17},{2,18},{3,19},{16,0},{17,1},{18,2},{19,3},{4,20},{5,... | collective-permute-start | bytes 442376 | tf_op jit(solution)/shard_map/ppermute | solution.py:35
  19.3 0.6 %collective-permute-start.8 = (f16[144,512]{1,0:T(8,128)(2,1)S(1)}, f16[144,512]{1,0:T(8,128)(2,1)S(1)}, u32[]{:S(2)}, u32[]{:S(2)}) collective-permute-start(f16[144,512]{1,0:T(8,128)(2,1)S(1)} %convert_element_type.18), channel_id=1, source_target_pairs={{0,2},{1,3},{2,0},{3,1},{16,18},{17,19},{18,16},{19,17},{4,6},{5,7... | collective-permute-start | bytes 442376 | tf_op jit(solution)/shard_map/ppermute | solution.py:35
  19.8 4.0 %collective-permute-done.10 = f16[144,512]{1,0:T(8,128)(2,1)S(1)} collective-permute-done((f16[144,512]{1,0:T(8,128)(2,1)S(1)}, f16[144,512]{1,0:T(8,128)(2,1)S(1)}, u32[]{:S(2)}, u32[]{:S(2)}) %collective-permute-start.10) | collective-permute-done | bytes 147488 | tf_op jit(solution)/shard_map/ppermute | solution.py:35
  23.9 2.4 %collective-permute-done.9 = f16[144,512]{1,0:T(8,128)(2,1)S(1)} collective-permute-done((f16[144,512]{1,0:T(8,128)(2,1)S(1)}, f16[144,512]{1,0:T(8,128)(2,1)S(1)}, u32[]{:S(2)}, u32[]{:S(2)}) %collective-permute-start.9) | collective-permute-done | bytes 147488 | tf_op jit(solution)/shard_map/ppermute | solution.py:35
  26.3 0.0 collective-permute-done.8
  26.4 1.0 %shard_map.40 = f32[128,1024]{1,0:T(8,128)} custom-call(f32[128,512]{1,0:T(8,128)S(1)} %get-tuple-element.29.refs_0_, f32[144,512]{1,0:T(8,128)S(1)} %convert_element_type.19.refs_1_, f32[144,512]{1,0:T(8,128)S(1)} %convert_element_type.21.refs_2_, f32[144,512]{1,0:T(8,128)S(1)} %convert_element_type.23.refs_3_), custom_call_target="tpu_custom_call" | custom-call | tf_op jit(solution)/shard_map/pallas_call | solution.py:196
  (6 shorter events, 0.1 us)
Async XLA Ops:
  0.0 8.8 %copy-start.2 = (f32[4,2]{0,1:T(2,128)S(1)}, f32[4,2]{0,1:T(2,128)}, u32[]{:S(2)}) copy-start(f32[4,2]{0,1:T(2,128)} %param.4) | copy-start | bytes 100
  0.0 11.0 %collective-permute-start = (bf16[128,640]{1,0:T(8,128)(2,1)}, bf16[128,640]{1,0:T(8,128)(2,1)S(1)}, u32[]{:S(2)}, u32[]{:S(2)}) collective-permute-start(bf16[128,640]{1,0:T(8,128)(2,1)} %jac_ref.1), channel_id=1, source_target_pairs={{0,4},{4,8},{8,12},{12,0},{1,5},{5,9},{9,13},{13,1},{2,6},{6,10},{... | collective-permute-start | bytes 491528 | tf_op jit(solution)/shard_map/ppermute | solution.py:18
  3.0 9.2 %collective-permute-start.6 = (bf16[128,640]{1,0:T(8,128)(2,1)}, bf16[128,640]{1,0:T(8,128)(2,1)S(1)}, u32[]{:S(2)}, u32[]{:S(2)}) collective-permute-start(bf16[128,640]{1,0:T(8,128)(2,1)} %jac_ref.1), channel_id=1, source_target_pairs={{0,12},{1,13},{2,14},{3,15},{16,28},{17,29},{18,30},{19,31}} | collective-permute-start | bytes 491528 | tf_op jit(solution)/shard_map/ppermute | solution.py:22
  7.1 5.9 %collective-permute-start.2 = (bf16[128,640]{1,0:T(8,128)(2,1)}, bf16[128,640]{1,0:T(8,128)(2,1)S(1)}, u32[]{:S(2)}, u32[]{:S(2)}) collective-permute-start(bf16[128,640]{1,0:T(8,128)(2,1)} %jac_ref.1), channel_id=1, source_target_pairs={{0,2},{1,3},{2,0},{3,1},{4,6},{5,7},{6,4},{7,5},{8,10},{9,11},{10,... | collective-permute-start | bytes 491528 | tf_op jit(solution)/shard_map/ppermute | solution.py:27
  8.8 0.9 %copy-start = (bf16[128,640]{1,0:T(8,128)(2,1)S(1)}, bf16[128,640]{1,0:T(8,128)(2,1)}, u32[]{:S(2)}) copy-start(bf16[128,640]{1,0:T(8,128)(2,1)} %jac_ref.1) | copy-start | bytes 491524
  9.7 0.7 %copy-start.1 = (f32[2,640]{1,0:T(2,128)S(1)}, f32[2,640]{1,0:T(2,128)}, u32[]{:S(2)}) copy-start(f32[2,640]{1,0:T(2,128)} %prior_ref.1) | copy-start | bytes 15364
  11.0 2.3 %collective-permute-start.1 = (bf16[128,640]{1,0:T(8,128)(2,1)S(1)}, bf16[128,640]{1,0:T(8,128)(2,1)S(1)}, u32[]{:S(2)}, u32[]{:S(2)}) collective-permute-start(bf16[128,640]{1,0:T(8,128)(2,1)S(1)} %collective-permute-done.refs_2_), channel_id=1, source_target_pairs={{4,8},{8,12},{5,9},{9,13},{6,10},{10,14},{7,11},{11,15},{20,24},{2... | collective-permute-start | bytes 491528 | tf_op jit(solution)/shard_map/ppermute | solution.py:22
  11.7 2.0 %collective-permute-start.4 = (bf16[128,640]{1,0:T(8,128)(2,1)S(1)}, bf16[128,640]{1,0:T(8,128)(2,1)S(1)}, u32[]{:S(2)}, u32[]{:S(2)}) collective-permute-start(bf16[128,640]{1,0:T(8,128)(2,1)S(1)} %collective-permute-done.refs_2_), channel_id=1, source_target_pairs={{0,1},{1,0},{2,3},{3,2},{4,5},{5,4},{6,7},{7,6},{8,9},{9,8},{10,11... | collective-permute-start | bytes 491528 | tf_op jit(solution)/shard_map/ppermute | solution.py:27
  11.8 1.9 %collective-permute-start.3 = (bf16[128,640]{1,0:T(8,128)(2,1)S(1)}, bf16[128,640]{1,0:T(8,128)(2,1)S(1)}, u32[]{:S(2)}, u32[]{:S(2)}) collective-permute-start(bf16[128,640]{1,0:T(8,128)(2,1)S(1)} %get-tuple-element.23.refs_0_), channel_id=1, source_target_pairs={{0,1},{1,0},{2,3},{3,2},{4,5},{5,4},{6,7},{7,6},{8,9},{9,8},{10,11... | collective-permute-start | bytes 491528 | tf_op jit(solution)/shard_map/ppermute | solution.py:27
  12.3 1.4 %collective-permute-start.7 = (bf16[128,640]{1,0:T(8,128)(2,1)S(1)}, bf16[128,640]{1,0:T(8,128)(2,1)S(1)}, u32[]{:S(2)}, u32[]{:S(2)}) collective-permute-start(bf16[128,640]{1,0:T(8,128)(2,1)S(1)} %collective-permute-done.6.refs_6_), channel_id=1, source_target_pairs={{0,1},{1,0},{2,3},{3,2},{4,5},{5,4},{6,7},{7,6},{8,9},{9,8},{10,11... | collective-permute-start | bytes 491528 | tf_op jit(solution)/shard_map/ppermute | solution.py:27
  13.3 1.5 %collective-permute-start.5 = (bf16[128,640]{1,0:T(8,128)(2,1)S(1)}, bf16[128,640]{1,0:T(8,128)(2,1)S(1)}, u32[]{:S(2)}, u32[]{:S(2)}) collective-permute-start(bf16[128,640]{1,0:T(8,128)(2,1)S(1)} %collective-permute-done.1.refs_4_), channel_id=1, source_target_pairs={{0,1},{1,0},{2,3},{3,2},{4,5},{5,4},{6,7},{7,6},{8,9},{9,8},{10,11... | collective-permute-start | bytes 491528 | tf_op jit(solution)/shard_map/ppermute | solution.py:27
  16.2 7.7 %collective-permute-start.10 = (f16[144,512]{1,0:T(8,128)(2,1)S(1)}, f16[144,512]{1,0:T(8,128)(2,1)S(1)}, u32[]{:S(2)}, u32[]{:S(2)}) collective-permute-start(f16[144,512]{1,0:T(8,128)(2,1)S(1)} %convert_element_type.22), channel_id=1, source_target_pairs={{0,18},{1,19},{2,16},{3,17},{16,2},{17,3},{18,0},{19,1},{4,22},{5,... | collective-permute-start | bytes 442376 | tf_op jit(solution)/shard_map/ppermute | solution.py:35
  18.7 7.6 %collective-permute-start.9 = (f16[144,512]{1,0:T(8,128)(2,1)S(1)}, f16[144,512]{1,0:T(8,128)(2,1)S(1)}, u32[]{:S(2)}, u32[]{:S(2)}) collective-permute-start(f16[144,512]{1,0:T(8,128)(2,1)S(1)} %convert_element_type.20), channel_id=1, source_target_pairs={{0,16},{1,17},{2,18},{3,19},{16,0},{17,1},{18,2},{19,3},{4,20},{5,... | collective-permute-start | bytes 442376 | tf_op jit(solution)/shard_map/ppermute | solution.py:35
  19.3 7.1 %collective-permute-start.8 = (f16[144,512]{1,0:T(8,128)(2,1)S(1)}, f16[144,512]{1,0:T(8,128)(2,1)S(1)}, u32[]{:S(2)}, u32[]{:S(2)}) collective-permute-start(f16[144,512]{1,0:T(8,128)(2,1)S(1)} %convert_element_type.18), channel_id=1, source_target_pairs={{0,2},{1,3},{2,0},{3,1},{16,18},{17,19},{18,16},{19,17},{4,6},{5,7... | collective-permute-start | bytes 442376 | tf_op jit(solution)/shard_map/ppermute | solution.py:35

commit v5 on v4

v5 whole, which is shorter than its diff:
```python
import functools

import jax
import jax.numpy as jnp
from jax import lax
from jax.experimental import pallas as pl
from jax.experimental.pallas import tpu as pltpu
from jax.sharding import PartitionSpec as P

LIMIT = 16 * 2**20
EXTRA = 16
SMEM = pl.BlockSpec(memory_space=pltpu.SMEM)
VMEM = pl.BlockSpec(memory_space=pltpu.VMEM)


def shift(x, axis, by):
    size = lax.axis_size(axis)
    return lax.ppermute(x, axis, [(i, (i + by) % size) for i in range(size)])


def climb(x, by, lowest, count):
    return lax.ppermute(x, "row", [(i - by, i) for i in range(lowest, lowest + count)])


def swap(x, axis, bit):
    size = lax.axis_size(axis)
    return lax.ppermute(x, axis, [(i, i ^ bit) for i in range(size)])


def send(x, by, bit):
    vox, lines = lax.axis_size("vox"), lax.axis_size("wl")
    pairs = [
        (v * lines + w, (v + by) % vox * lines + (w ^ bit)) for v in range(vox) for w in range(lines)
    ]
    return lax.ppermute(x, ("vox", "wl"), pairs)


def kernel_call(kernel, ins, outs, scratch=()):
    return functools.partial(
        pl.pallas_call,
        kernel,
        in_specs=ins,
        out_specs=[VMEM] * len(outs),
        out_shape=outs,
        scratch_shapes=scratch,
        compiler_params=pltpu.CompilerParams(vmem_limit_bytes=LIMIT),
    )()


def prepare_kernel(far, near, extinction_ref, prior_ref, jac_ref, weights_ref, own_ref):
    chroms, waves = extinction_ref.shape
    w = lax.axis_index("wl")
    for i, e in enumerate(near):
        for j, f in enumerate(far):
            weight = 0.0
            for c in range(chroms):
                coeff = extinction_ref[c, lax.rem(w ^ f, waves)] * extinction_ref[c, lax.rem(w ^ e, waves)]
                weight += coeff * prior_ref[c : c + 1, :]
            weights_ref[i * len(far) + j : i * len(far) + j + 1, :] = weight
    own_ref[...] = jac_ref[...]


def prepare(extinction, prior, jac, far, near):
    weights = jax.ShapeDtypeStruct((len(far) * len(near), jac.shape[1]), jnp.float32)
    own = jax.ShapeDtypeStruct(jac.shape, jac.dtype)
    call = kernel_call(functools.partial(prepare_kernel, far, near), [SMEM, VMEM, VMEM], [weights, own])
    return call(extinction, prior, jac)


def weigh_kernel(far, near, weights_ref, *refs):
    rows, (high_ref, low_ref) = refs[:-2], refs[-2:]
    tile = rows[0].shape[0]
    for i in range(len(near)):
        for j in range(len(far)):
            k = i * len(far) + j
            scaled = rows[j][...].astype(jnp.float32) * weights_ref[k : k + 1, :]
            top = scaled.astype(jnp.bfloat16)
            high_ref[i, j * tile : (j + 1) * tile, :] = top
            low_ref[i, j * tile : (j + 1) * tile, :] = (scaled - top.astype(jnp.float32)).astype(jnp.bfloat16)


def weigh(weights, rows, far, near):
    tile, depth = rows[0].shape
    like = jax.ShapeDtypeStruct((len(near), len(far) * tile, depth), jnp.bfloat16)
    call = kernel_call(functools.partial(weigh_kernel, far, near), [VMEM] * (1 + len(rows)), [like, like])
    return call(weights, *rows)


def emit(out, total, at):
    tile = total.shape[0]
    if out.shape[0] > tile:
        largest = jnp.max(jnp.abs(total), axis=(0, 1), keepdims=True)
        power = jnp.floor(jnp.log2(jnp.maximum(largest, 1e-30))) - 13.0
        out[tile:, at : at + tile] = jnp.broadcast_to(power, (EXTRA, tile))
        total = total * jnp.exp2(-power)
    out[:tile, at : at + tile] = total


def product(high, low, cols):
    dims = (((1,), (1,)), ((), ()))
    return lax.dot_general(high, cols, dims, preferred_element_type=jnp.float32) + lax.dot_general(
        low, cols, dims, preferred_element_type=jnp.float32
    )


def first_kernel(vox, levels, have, far, near, high_ref, low_ref, *refs):
    pieces = dict(zip(have, refs))
    outs, cols_ref = refs[len(have) : -1], refs[-1]
    tile, slots = refs[0].shape[0], levels // vox
    v, z = lax.axis_index("vox"), lax.axis_index("row")
    parts = [(t, s) for t in range(vox) for s in range(slots)]
    for n, (t, s) in enumerate(parts):
        dist = jnp.maximum(z - (lax.rem(v + t, vox) * slots + s), 0)
        for d in range(levels):

            @pl.when(dist == d)
            def _():
                for i in range(len(near)):
                    if (d, i) in pieces:
                        cols_ref[i, n * tile : (n + 1) * tile] = pieces[d, i][...]

    for i in range(len(near)):
        total = product(high_ref[i], low_ref[i], cols_ref[i])
        for n, (t, s) in enumerate(parts):
            for j in range(len(far)):
                block = total[j * tile : (j + 1) * tile, n * tile : (n + 1) * tile]
                emit(outs[t * len(far) + j], block, (s * len(near) + i) * tile)


def second_kernel(vox, levels, have, far, near, high_ref, low_ref, *refs):
    pieces = dict(zip(have, refs))
    ins, outs = refs[len(have) : -vox * len(far)], refs[-vox * len(far) :]
    for known, out in zip(ins, outs):
        out[...] = known[...]
    tile, slots = refs[0].shape[0], levels // vox
    v, z = lax.axis_index("vox"), lax.axis_index("row")
    for t in range(vox):
        for s in range(slots):
            dist = z - (lax.rem(v + t, vox) * slots + s)
            for (d, i), piece in pieces.items():

                @pl.when(dist == d)
                def _():
                    total = product(high_ref[i], low_ref[i], piece[...])
                    for j in range(len(far)):
                        block = total[j * tile : (j + 1) * tile]
                        emit(outs[t * len(far) + j], block, (s * len(near) + i) * tile)


def multiply(high, low, first, second, levels, vox, far, near):
    tile, depth = first[0, 0].shape
    heights = [tile] + [tile + EXTRA] * (vox * len(far) - 1)
    likes = [jax.ShapeDtypeStruct((h, levels // vox * len(near) * tile), jnp.float32) for h in heights]
    shares = kernel_call(
        functools.partial(first_kernel, vox, levels, list(first), far, near),
        [VMEM] * (2 + len(first)),
        likes,
        [pltpu.VMEM((len(near), levels * tile, depth), jnp.bfloat16)],
    )(high, low, *first.values())
    if second:
        shares = kernel_call(
            functools.partial(second_kernel, vox, levels, list(second), far, near),
            [VMEM] * (2 + len(second) + len(likes)),
            likes,
        )(high, low, *second.values(), *shares)
    return shares


def place_kernel(vox, levels, lines, far, near, *refs):
    blocks, out_ref, held, sems = refs[:-3], refs[-3], refs[-2], refs[-1]
    tile, slots = blocks[0].shape[0], levels // vox
    v, z, w = (lax.axis_index(a) for a in ("vox", "row", "wl"))
    rows = (z * lines + w) * tile + lax.broadcasted_iota(jnp.int32, (tile, tile), 0)
    copies = []
    for j, f in enumerate(far):
        for s in range(slots):
            for i, e in enumerate(near):
                k = (s * len(near) + i) * tile
                total = 0.0
                for t in range(vox):
                    block = blocks[t * len(far) + j]
                    scale = 1.0 if t == j == 0 else jnp.exp2(block[tile : tile + 1, k : k + 1])
                    total += block[:tile, k : k + tile] * scale
                at = pl.multiple_of((s * lines + (w ^ f ^ e)) * tile, tile)
                cols = v * (slots * lines * tile) + at + lax.broadcasted_iota(jnp.int32, (tile, tile), 1)
                n = len(copies)
                held[n] = jnp.where(cols <= rows, total, 0.0)
                copies.append(pltpu.make_async_copy(held.at[n], out_ref.at[:, pl.ds(at, tile)], sems.at[n]))
                copies[-1].start()
    for copy in copies:
        copy.wait()


def place(blocks, vox, levels, lines, far, near):
    tile = blocks[0].shape[0]
    count = levels // vox * lines
    return pl.pallas_call(
        functools.partial(place_kernel, vox, levels, lines, far, near),
        in_specs=[VMEM] * len(blocks),
        out_specs=pl.BlockSpec(memory_space=pl.ANY),
        out_shape=jax.ShapeDtypeStruct((tile, count * tile), jnp.float32),
        scratch_shapes=[pltpu.VMEM((count, tile, tile), jnp.float32), pltpu.SemaphoreType.DMA((count,))],
        compiler_params=pltpu.CompilerParams(vmem_limit_bytes=LIMIT),
    )(*blocks)


def on_device(jac, extinction, prior_var):
    vox, levels, lines = (lax.axis_size(a) for a in ("vox", "row", "wl"))
    slots = levels // vox
    far = [0, lines // 2] if lines > 1 else [0]
    near = list(range(max(lines // 2, 1)))

    below = {0: jac}
    if levels > 1:
        below[1] = shift(jac, "row", 1)
    others = [swap(jac, "wl", f) for f in far[1:]]
    if levels > 2:
        below[levels - 1] = climb(jac, levels - 1, levels - 1, 1)
    weights, own = prepare(extinction.T, prior_var, jac, far, near)
    if levels > 1:
        below[1], weights, own = lax.optimization_barrier([below[1], weights, own])
    for d in range(2, levels - 1):
        below[d] = climb(below[d - 1], 1, d, levels - d)
    high, low = weigh(weights, [own] + others, far, near)
    below[0] = own
    for d in range(2, levels - 1):
        below[d], high, low = lax.optimization_barrier([below[d], high, low])
    pieces = {(d, 0): x for d, x in below.items()}
    pieces.update({(d, i): swap(x, "wl", e) for d, x in below.items() for i, e in enumerate(near) if i})

    second = {k: x for k, x in pieces.items() if k[0] == levels - 2 > 1 and k[1]}
    first = {k: x for k, x in pieces.items() if k not in second}
    shares = list(multiply(high, low, first, second, levels, vox, far, near))
    for k in range(1, len(shares)):
        t, j = divmod(k, len(far))
        shares[k] = send(shares[k].astype(jnp.float16), t, far[j]).astype(jnp.float32)
    return place(shares, vox, levels, lines, far, near)


def solution(mesh):
    return jax.shard_map(
        on_device,
        mesh=mesh,
        in_specs=(P(("row", "wl"), "vox"), P(), P(None, "vox")),
        out_specs=P(("row", "wl"), "vox"),
        check_vma=False,
    )
```

time: 27.9 us -> 27.4 us (0.982)
  the two profiles are of different devices: /device:TPU:0 before, /device:TPU:19 now
where the time goes in v5:
time: 27.4 us; the launch traced here: 27.2 us
  starting transfers between devices  13.4 us (49%)
  waiting for transfers between devices  8.19 us (30%)
  Pallas kernels  3.74 us (14%)
  local copies, waits for them, and re-layouts  1.64 us (6%)
    ppermute x3, waiting for transfers between devices, send(): return lax.ppermute(x, ('vox', 'wl'), pairs)  7.03 us
    ppermute x5, starting transfers between devices, swap(): return lax.ppermute(x, axis, [(i, i ^ bit) for i in range(size)])  5.68 us
    ppermute x2, starting transfers between devices, climb(): lax.ppermute(x, 'row', [(i - by, i) for i in range(lowest, lowest + count)])  3.62 us
    ppermute x3, starting transfers between devices, send(): return lax.ppermute(x, ('vox', 'wl'), pairs)  2.78 us
    unnamed x6, local copies, waits for them, and re-layouts  1.64 us
    pallas_call x1, Pallas kernels, multiply(): kernel_call(functools.partial(first_kernel, vox, levels, list(first), far...  1.4 us
    ppermute x1, starting transfers between devices, shift(): return lax.ppermute(x, axis, [(i, (i + by) % size) for i in range(size)])  1.3 us
    ppermute x2, waiting for transfers between devices, climb(): lax.ppermute(x, 'row', [(i - by, i) for i in range(lowest, lowest + count)])  1.15 us
  transfers between devices with their start and end apart: 11, of which 4 were waited for; matrix products, arithmetic and copies ran while one was open for 0% of the time, Pallas kernels for 8%

profile of v5, /device:TPU:19, one launch (start us, length us, event | category | flops | bytes accessed | tf_op | source)
XLA Modules:
  0.0 27.2 jit_solution(7514825374775906405)
XLA Ops:
  0.0 0.0 copy-start.2
  0.0 1.3 %collective-permute-start = (bf16[128,640]{1,0:T(8,128)(2,1)}, bf16[128,640]{1,0:T(8,128)(2,1)S(1)}, u32[]{:S(2)}, u32[]{:S(2)}) collective-permute-start(bf16[128,640]{1,0:T(8,128)(2,1)} %jac_ref.1), channel_id=1, source_target_pairs={{0,4},{4,8},{8,12},{12,0},{1,5},{5,9},{9,13},{13,1},{2,6},{6,10},{... | collective-permute-start | bytes 491528 | tf_op jit(solution)/shard_map/ppermute | solution.py:18
  1.3 0.7 %collective-permute-start.4 = (bf16[128,640]{1,0:T(8,128)(2,1)}, bf16[128,640]{1,0:T(8,128)(2,1)S(1)}, u32[]{:S(2)}, u32[]{:S(2)}) collective-permute-start(bf16[128,640]{1,0:T(8,128)(2,1)} %jac_ref.1), channel_id=1, source_target_pairs={{0,12},{1,13},{2,14},{3,15},{16,28},{17,29},{18,30},{19,31}} | collective-permute-start | bytes 491528 | tf_op jit(solution)/shard_map/ppermute | solution.py:22
  2.0 1.3 %collective-permute-start.2 = (bf16[128,640]{1,0:T(8,128)(2,1)}, bf16[128,640]{1,0:T(8,128)(2,1)S(1)}, u32[]{:S(2)}, u32[]{:S(2)}) collective-permute-start(bf16[128,640]{1,0:T(8,128)(2,1)} %jac_ref.1), channel_id=1, source_target_pairs={{0,2},{1,3},{2,0},{3,1},{4,6},{5,7},{6,4},{7,5},{8,10},{9,11},{10,... | collective-permute-start | bytes 491528 | tf_op jit(solution)/shard_map/ppermute | solution.py:27
  3.3 0.0 copy-done.2
  3.3 0.0 copy-start
  3.3 0.9 %copy-done = bf16[128,640]{1,0:T(8,128)(2,1)S(1)} copy-done((bf16[128,640]{1,0:T(8,128)(2,1)S(1)}, bf16[128,640]{1,0:T(8,128)(2,1)}, u32[]{:S(2)}) %copy-start) | copy-done | bytes 163864
  4.2 0.0 copy-start.1
  4.2 0.7 %copy-done.1 = f32[2,640]{1,0:T(2,128)S(1)} copy-done((f32[2,640]{1,0:T(2,128)S(1)}, f32[2,640]{1,0:T(2,128)}, u32[]{:S(2)}) %copy-start.1) | copy-done | bytes 5144
  4.9 0.6 %shard_map.37 = (f32[4,640]{1,0:T(4,128)S(1)}, bf16[128,640]{1,0:T(8,128)(2,1)S(1)}) custom-call(f32[2,4]{1,0:T(2,128)S(1)} %bitcast.1, f32[2,640]{1,0:T(2,128)S(1)} %copy-done.1, bf16[128,640]{1,0:T(8,128)(2,1)S(1)} %copy-done), custom_call_target="tpu_custom_call" | custom-call | tf_op jit(solution)/shard_map/pallas_call | solution.py:67
  5.5 0.0 collective-permute-done.refs_1_
  5.5 3.0 %collective-permute-start.1 = (bf16[128,640]{1,0:T(8,128)(2,1)S(1)}, bf16[128,640]{1,0:T(8,128)(2,1)S(1)}, u32[]{:S(2)}, u32[]{:S(2)}) collective-permute-start(bf16[128,640]{1,0:T(8,128)(2,1)S(1)} %collective-permute-done.refs_1_), channel_id=1, source_target_pairs={{4,8},{8,12},{5,9},{9,13},{6,10},{10,14},{7,11},{11,15},{20,24},{2... | collective-permute-start | bytes 491528 | tf_op jit(solution)/shard_map/ppermute | solution.py:22
  8.5 1.9 %collective-permute-start.6 = (bf16[128,640]{1,0:T(8,128)(2,1)S(1)}, bf16[128,640]{1,0:T(8,128)(2,1)S(1)}, u32[]{:S(2)}, u32[]{:S(2)}) collective-permute-start(bf16[128,640]{1,0:T(8,128)(2,1)S(1)} %collective-permute-done.refs_1_), channel_id=1, source_target_pairs={{0,1},{1,0},{2,3},{3,2},{4,5},{5,4},{6,7},{7,6},{8,9},{9,8},{10,11... | collective-permute-start | bytes 491528 | tf_op jit(solution)/shard_map/ppermute | solution.py:27
  10.4 0.1 collective-permute-start.5
  10.5 0.0 collective-permute-done.4.refs_2_
  10.5 0.4 %collective-permute-start.7 = (bf16[128,640]{1,0:T(8,128)(2,1)S(1)}, bf16[128,640]{1,0:T(8,128)(2,1)S(1)}, u32[]{:S(2)}, u32[]{:S(2)}) collective-permute-start(bf16[128,640]{1,0:T(8,128)(2,1)S(1)} %collective-permute-done.4.refs_2_), channel_id=1, source_target_pairs={{0,1},{1,0},{2,3},{3,2},{4,5},{5,4},{6,7},{7,6},{8,9},{9,8},{10,11... | collective-permute-start | bytes 491528 | tf_op jit(solution)/shard_map/ppermute | solution.py:27
  10.9 0.0 collective-permute-done.2.refs_1_
  10.9 0.3 shard_map.38
  11.2 1.1 %collective-permute-done.1.refs_3_ = bf16[128,640]{1,0:T(8,128)(2,1)S(1)} collective-permute-done((bf16[128,640]{1,0:T(8,128)(2,1)S(1)}, bf16[128,640]{1,0:T(8,128)(2,1)S(1)}, u32[]{:S(2)}, u32[]{:S(2)}) %collective-permute-start.1) | collective-permute-done | bytes 163872 | tf_op jit(solution)/shard_map/ppermute | solution.py:22
  12.3 2.0 %collective-permute-start.3 = (bf16[128,640]{1,0:T(8,128)(2,1)S(1)}, bf16[128,640]{1,0:T(8,128)(2,1)S(1)}, u32[]{:S(2)}, u32[]{:S(2)}) collective-permute-start(bf16[128,640]{1,0:T(8,128)(2,1)S(1)} %collective-permute-done.1.refs_3_), channel_id=1, source_target_pairs={{0,1},{1,0},{2,3},{3,2},{4,5},{5,4},{6,7},{7,6},{8,9},{9,8},{10,11... | collective-permute-start | bytes 491528 | tf_op jit(solution)/shard_map/ppermute | solution.py:27
  14.3 0.0 collective-permute-done.7.refs_6_
  14.3 0.0 collective-permute-done.6.refs_5_
  14.3 0.0 collective-permute-done.5.refs_4_
  14.3 1.4 %shard_map.39 = (f32[128,512]{1,0:T(8,128)S(1)}, f32[144,512]{1,0:T(8,128)S(1)}, f32[144,512]{1,0:T(8,128)S(1)}, f32[144,512]{1,0:T(8,128)S(1)}) custom-call(bf16[2,256,640]{2,1,0:T(8,128)(2,1)S(1)} %get-tuple-element.30.high_ref, bf16[2,256,640]{2,1,0:T(8,128)(2,1)S(1)} %get-tuple-element.31.low_ref, bf16[128,640]{1,0:T(8,128)(2,1)S(1)} %get-tuple-element.27.refs_0_, ...), custom_call_target="tpu_custom_call" | custom-call | tf_op jit(solution)/shard_map/pallas_call | solution.py:154
  15.7 0.0 collective-permute-done.3.refs_0_
  15.7 0.6 %shard_map.40 = (f32[128,512]{1,0:T(8,128)S(1)}, f32[144,512]{1,0:T(8,128)S(1)}, f32[144,512]{1,0:T(8,128)S(1)}, f32[144,512]{1,0:T(8,128)S(1)}) custom-call(bf16[2,256,640]{2,1,0:T(8,128)(2,1)S(1)} %get-tuple-element.30.high_ref, bf16[2,256,640]{2,1,0:T(8,128)(2,1)S(1)} %get-tuple-element.31.low_ref, bf16[128,640]{1,0:T(8,128)(2,1)S(1)} %collective-permute-done.3.refs_0_, ...), custom_call_target="tpu_custom_call" | custom-call | tf_op jit(solution)/shard_map/pallas_call | solution.py:161
  16.3 1.3 %collective-permute-start.10 = (f16[144,512]{1,0:T(8,128)(2,1)S(1)}, f16[144,512]{1,0:T(8,128)(2,1)S(1)}, u32[]{:S(2)}, u32[]{:S(2)}) collective-permute-start(f16[144,512]{1,0:T(8,128)(2,1)S(1)} %convert_element_type.22), channel_id=1, source_target_pairs={{0,18},{1,19},{2,16},{3,17},{16,2},{17,3},{18,0},{19,1},{4,22},{5,... | collective-permute-start | bytes 442376 | tf_op jit(solution)/shard_map/ppermute | solution.py:35
  17.6 1.2 %collective-permute-start.9 = (f16[144,512]{1,0:T(8,128)(2,1)S(1)}, f16[144,512]{1,0:T(8,128)(2,1)S(1)}, u32[]{:S(2)}, u32[]{:S(2)}) collective-permute-start(f16[144,512]{1,0:T(8,128)(2,1)S(1)} %convert_element_type.20), channel_id=1, source_target_pairs={{0,16},{1,17},{2,18},{3,19},{16,0},{17,1},{18,2},{19,3},{4,20},{5,... | collective-permute-start | bytes 442376 | tf_op jit(solution)/shard_map/ppermute | solution.py:35
  18.8 0.3 %collective-permute-start.8 = (f16[144,512]{1,0:T(8,128)(2,1)S(1)}, f16[144,512]{1,0:T(8,128)(2,1)S(1)}, u32[]{:S(2)}, u32[]{:S(2)}) collective-permute-start(f16[144,512]{1,0:T(8,128)(2,1)S(1)} %convert_element_type.18), channel_id=1, source_target_pairs={{0,2},{1,3},{2,0},{3,1},{16,18},{17,19},{18,16},{19,17},{4,6},{5,7... | collective-permute-start | bytes 442376 | tf_op jit(solution)/shard_map/ppermute | solution.py:35
  19.1 3.6 %collective-permute-done.10 = f16[144,512]{1,0:T(8,128)(2,1)S(1)} collective-permute-done((f16[144,512]{1,0:T(8,128)(2,1)S(1)}, f16[144,512]{1,0:T(8,128)(2,1)S(1)}, u32[]{:S(2)}, u32[]{:S(2)}) %collective-permute-start.10) | collective-permute-done | bytes 147488 | tf_op jit(solution)/shard_map/ppermute | solution.py:35
  22.8 3.2 %collective-permute-done.9 = f16[144,512]{1,0:T(8,128)(2,1)S(1)} collective-permute-done((f16[144,512]{1,0:T(8,128)(2,1)S(1)}, f16[144,512]{1,0:T(8,128)(2,1)S(1)}, u32[]{:S(2)}, u32[]{:S(2)}) %collective-permute-start.9) | collective-permute-done | bytes 147488 | tf_op jit(solution)/shard_map/ppermute | solution.py:35
  26.0 0.2 collective-permute-done.8
  26.3 1.0 %shard_map.41 = f32[128,1024]{1,0:T(8,128)} custom-call(f32[128,512]{1,0:T(8,128)S(1)} %get-tuple-element.37.refs_0_, f32[144,512]{1,0:T(8,128)S(1)} %convert_element_type.19.refs_1_, f32[144,512]{1,0:T(8,128)S(1)} %convert_element_type.21.refs_2_, f32[144,512]{1,0:T(8,128)S(1)} %convert_element_type.23.refs_3_), custom_call_target="tpu_custom_call" | custom-call | tf_op jit(solution)/shard_map/pallas_call | solution.py:197
  (6 shorter events, 0.1 us)
Async XLA Ops:
  0.0 3.3 %copy-start.2 = (f32[4,2]{0,1:T(2,128)S(1)}, f32[4,2]{0,1:T(2,128)}, u32[]{:S(2)}) copy-start(f32[4,2]{0,1:T(2,128)} %param.4) | copy-start | bytes 100
  0.0 5.5 %collective-permute-start = (bf16[128,640]{1,0:T(8,128)(2,1)}, bf16[128,640]{1,0:T(8,128)(2,1)S(1)}, u32[]{:S(2)}, u32[]{:S(2)}) collective-permute-start(bf16[128,640]{1,0:T(8,128)(2,1)} %jac_ref.1), channel_id=1, source_target_pairs={{0,4},{4,8},{8,12},{12,0},{1,5},{5,9},{9,13},{13,1},{2,6},{6,10},{... | collective-permute-start | bytes 491528 | tf_op jit(solution)/shard_map/ppermute | solution.py:18
  1.3 9.2 %collective-permute-start.4 = (bf16[128,640]{1,0:T(8,128)(2,1)}, bf16[128,640]{1,0:T(8,128)(2,1)S(1)}, u32[]{:S(2)}, u32[]{:S(2)}) collective-permute-start(bf16[128,640]{1,0:T(8,128)(2,1)} %jac_ref.1), channel_id=1, source_target_pairs={{0,12},{1,13},{2,14},{3,15},{16,28},{17,29},{18,30},{19,31}} | collective-permute-start | bytes 491528 | tf_op jit(solution)/shard_map/ppermute | solution.py:22
  2.0 8.9 %collective-permute-start.2 = (bf16[128,640]{1,0:T(8,128)(2,1)}, bf16[128,640]{1,0:T(8,128)(2,1)S(1)}, u32[]{:S(2)}, u32[]{:S(2)}) collective-permute-start(bf16[128,640]{1,0:T(8,128)(2,1)} %jac_ref.1), channel_id=1, source_target_pairs={{0,2},{1,3},{2,0},{3,1},{4,6},{5,7},{6,4},{7,5},{8,10},{9,11},{10,... | collective-permute-start | bytes 491528 | tf_op jit(solution)/shard_map/ppermute | solution.py:27
  3.3 0.9 %copy-start = (bf16[128,640]{1,0:T(8,128)(2,1)S(1)}, bf16[128,640]{1,0:T(8,128)(2,1)}, u32[]{:S(2)}) copy-start(bf16[128,640]{1,0:T(8,128)(2,1)} %jac_ref.1) | copy-start | bytes 491524
  4.2 0.7 %copy-start.1 = (f32[2,640]{1,0:T(2,128)S(1)}, f32[2,640]{1,0:T(2,128)}, u32[]{:S(2)}) copy-start(f32[2,640]{1,0:T(2,128)} %prior_ref.1) | copy-start | bytes 15364
  5.5 6.8 %collective-permute-start.1 = (bf16[128,640]{1,0:T(8,128)(2,1)S(1)}, bf16[128,640]{1,0:T(8,128)(2,1)S(1)}, u32[]{:S(2)}, u32[]{:S(2)}) collective-permute-start(bf16[128,640]{1,0:T(8,128)(2,1)S(1)} %collective-permute-done.refs_1_), channel_id=1, source_target_pairs={{4,8},{8,12},{5,9},{9,13},{6,10},{10,14},{7,11},{11,15},{20,24},{2... | collective-permute-start | bytes 491528 | tf_op jit(solution)/shard_map/ppermute | solution.py:22
  8.5 5.8 %collective-permute-start.6 = (bf16[128,640]{1,0:T(8,128)(2,1)S(1)}, bf16[128,640]{1,0:T(8,128)(2,1)S(1)}, u32[]{:S(2)}, u32[]{:S(2)}) collective-permute-start(bf16[128,640]{1,0:T(8,128)(2,1)S(1)} %collective-permute-done.refs_1_), channel_id=1, source_target_pairs={{0,1},{1,0},{2,3},{3,2},{4,5},{5,4},{6,7},{7,6},{8,9},{9,8},{10,11... | collective-permute-start | bytes 491528 | tf_op jit(solution)/shard_map/ppermute | solution.py:27
  10.4 3.9 %collective-permute-start.5 = (bf16[128,640]{1,0:T(8,128)(2,1)S(1)}, bf16[128,640]{1,0:T(8,128)(2,1)S(1)}, u32[]{:S(2)}, u32[]{:S(2)}) collective-permute-start(bf16[128,640]{1,0:T(8,128)(2,1)S(1)} %get-tuple-element.27.refs_0_), channel_id=1, source_target_pairs={{0,1},{1,0},{2,3},{3,2},{4,5},{5,4},{6,7},{7,6},{8,9},{9,8},{10,11... | collective-permute-start | bytes 491528 | tf_op jit(solution)/shard_map/ppermute | solution.py:27
  10.5 3.8 %collective-permute-start.7 = (bf16[128,640]{1,0:T(8,128)(2,1)S(1)}, bf16[128,640]{1,0:T(8,128)(2,1)S(1)}, u32[]{:S(2)}, u32[]{:S(2)}) collective-permute-start(bf16[128,640]{1,0:T(8,128)(2,1)S(1)} %collective-permute-done.4.refs_2_), channel_id=1, source_target_pairs={{0,1},{1,0},{2,3},{3,2},{4,5},{5,4},{6,7},{7,6},{8,9},{9,8},{10,11... | collective-permute-start | bytes 491528 | tf_op jit(solution)/shard_map/ppermute | solution.py:27
  12.3 3.4 %collective-permute-start.3 = (bf16[128,640]{1,0:T(8,128)(2,1)S(1)}, bf16[128,640]{1,0:T(8,128)(2,1)S(1)}, u32[]{:S(2)}, u32[]{:S(2)}) collective-permute-start(bf16[128,640]{1,0:T(8,128)(2,1)S(1)} %collective-permute-done.1.refs_3_), channel_id=1, source_target_pairs={{0,1},{1,0},{2,3},{3,2},{4,5},{5,4},{6,7},{7,6},{8,9},{9,8},{10,11... | collective-permute-start | bytes 491528 | tf_op jit(solution)/shard_map/ppermute | solution.py:27
  16.3 6.4 %collective-permute-start.10 = (f16[144,512]{1,0:T(8,128)(2,1)S(1)}, f16[144,512]{1,0:T(8,128)(2,1)S(1)}, u32[]{:S(2)}, u32[]{:S(2)}) collective-permute-start(f16[144,512]{1,0:T(8,128)(2,1)S(1)} %convert_element_type.22), channel_id=1, source_target_pairs={{0,18},{1,19},{2,16},{3,17},{16,2},{17,3},{18,0},{19,1},{4,22},{5,... | collective-permute-start | bytes 442376 | tf_op jit(solution)/shard_map/ppermute | solution.py:35
  17.6 8.4 %collective-permute-start.9 = (f16[144,512]{1,0:T(8,128)(2,1)S(1)}, f16[144,512]{1,0:T(8,128)(2,1)S(1)}, u32[]{:S(2)}, u32[]{:S(2)}) collective-permute-start(f16[144,512]{1,0:T(8,128)(2,1)S(1)} %convert_element_type.20), channel_id=1, source_target_pairs={{0,16},{1,17},{2,18},{3,19},{16,0},{17,1},{18,2},{19,3},{4,20},{5,... | collective-permute-start | bytes 442376 | tf_op jit(solution)/shard_map/ppermute | solution.py:35
  18.8 7.4 %collective-permute-start.8 = (f16[144,512]{1,0:T(8,128)(2,1)S(1)}, f16[144,512]{1,0:T(8,128)(2,1)S(1)}, u32[]{:S(2)}, u32[]{:S(2)}) collective-permute-start(f16[144,512]{1,0:T(8,128)(2,1)S(1)} %convert_element_type.18), channel_id=1, source_target_pairs={{0,2},{1,3},{2,0},{3,1},{16,18},{17,19},{18,16},{19,17},{4,6},{5,7... | collective-permute-start | bytes 442376 | tf_op jit(solution)/shard_map/ppermute | solution.py:35

commit v6 on v4

--- a/solution.py
+++ b/solution.py
@@ -130,27 +130,37 @@
                 for i in range(len(near)):
                     cols_ref[i, n * tile : (n + 1) * tile] = pieces[k * len(near) + i][...]
 
-    for i in range(len(near)):
-        total = 0.0
-        for part in (high_ref, low_ref):
-            total += lax.dot_general(
-                part[i], cols_ref[i], (((1,), (1,)), ((), ())), preferred_element_type=jnp.float32
-            )
-        for n, (t, p) in enumerate(parts):
-            to = (p * len(near) + i) * tile
-            for j in range(len(far)):
-                outs[t * len(far) + j][:tile, to : to + tile] = total[
-                    j * tile : (j + 1) * tile, n * tile : (n + 1) * tile
-                ]
-    for out in outs[1:]:
-        largest = jnp.max(jnp.abs(out[:tile]), axis=(0, 1), keepdims=True)
-        power = jnp.floor(jnp.log2(jnp.maximum(largest, 1e-30))) - 13.0
-        out[:tile] *= jnp.exp2(-power)
-        out[tile:] = jnp.broadcast_to(power, out[tile:].shape)
-
-
-def multiply(high, low, pieces, vox, phases, far, near):
-    levels = len(pieces)
+    slots = levels // vox
+    owners = [choose(o, z, p, slots, levels)[0] + o * slots for o in range(vox) for p in phases]
+    needed = functools.reduce(jnp.logical_or, [at <= z for at in owners])
+
+    @pl.when(jnp.logical_not(needed))
+    def _():
+        for out in outs:
+            out[...] = jnp.zeros_like(out)
+
+    @pl.when(needed)
+    def _():
+        for i in range(len(near)):
+            total = 0.0
+            for part in (high_ref, low_ref):
+                total += lax.dot_general(
+                    part[i], cols_ref[i], (((1,), (1,)), ((), ())), preferred_element_type=jnp.float32
+                )
+            for n, (t, p) in enumerate(parts):
+                to = (p * len(near) + i) * tile
+                for j in range(len(far)):
+                    outs[t * len(far) + j][:tile, to : to + tile] = total[
+                        j * tile : (j + 1) * tile, n * tile : (n + 1) * tile
+                    ]
+        for out in outs[1:]:
+            largest = jnp.max(jnp.abs(out[:tile]), axis=(0, 1), keepdims=True)
+            power = jnp.floor(jnp.log2(jnp.maximum(largest, 1e-30))) - 13.0
+            out[:tile] *= jnp.exp2(-power)
+            out[tile:] = jnp.broadcast_to(power, out[tile:].shape)
+
+
+def multiply(high, low, pieces, levels, vox, phases, far, near):
     tile, depth = pieces[0][0].shape
     dists = sorted(set().union(*[used(p, levels // vox, levels) for p in phases]))
     flat = [pieces[d][i] for d in dists for i in range(len(near))]
@@ -166,7 +176,7 @@
 
 
 def place_kernel(vox, levels, lines, groups, far, near, *refs):
-    blocks, out_ref = refs[:-1], refs[-1]
+    blocks, out_ref = refs[-2::-1], refs[-1]
     tile, slots = out_ref.shape[0], levels // vox
     v, z, w = (lax.axis_index(a) for a in ("vox", "row", "wl"))
     rows = (z * lines + w) * tile + lax.broadcasted_iota(jnp.int32, (tile, tile), 0)
@@ -193,16 +203,16 @@
         [VMEM] * len(blocks),
         [jax.ShapeDtypeStruct((tile, levels // vox * lines * tile), jnp.float32)],
     )
-    return call(*blocks)[0]
+    return call(*blocks[::-1])[0]
 
 
 def on_device(jac, extinction, prior_var):
     vox, levels, lines = (lax.axis_size(a) for a in ("vox", "row", "wl"))
-    slots = levels // vox
+    tile, slots = jac.shape[0], levels // vox
     far = [0, lines // 2] if lines > 1 else [0]
     near = list(range(max(lines // 2, 1)))
 
-    groups = [list(range(slots))]
+    groups = [[p] for p in range(slots)]
 
     below = {0: jac}
     if levels > 1:
@@ -217,20 +227,29 @@
         below[d] = climb(below[d - 1], 1, d, levels - d)
     high, low = weigh(weights, [own] + others, far, near)
     below[0] = own
-    for d in range(2, levels - 1):
-        below[d], high, low = lax.optimization_barrier([below[d], high, low])
-    pieces = [[below[d]] + [swap(below[d], "wl", e) for e in near[1:]] for d in range(levels)]
-
+
+    def both(d):
+        cuts = (below[d],) if d == 0 else (below[d][: tile // 2], below[d][tile // 2 :])
+        swapped = [[swap(x, "wl", e) for x in cuts] for e in near[1:]]
+        return [below[d]] + [jnp.concatenate(xs, axis=0) if d else xs[0] for xs in swapped]
+
+    pieces = {d: both(d) for d in (0, 1, levels - 1)}
     blocks = []
     for phases in groups:
-        shares = multiply(high, low, pieces, vox, phases, far, near)
-        for t in range(vox):
-            for j, f in enumerate(far):
-                share = shares[t * len(far) + j]
-                if t or f:
-                    share = send(share.astype(jnp.float16), t, f).astype(jnp.float32)
-                blocks.append(share)
-    return place(blocks, vox, levels, lines, groups, far, near)
+        dists = sorted(set().union(*[used(p, slots, levels) for p in phases]))
+        late = [d for d in dists if d not in pieces]
+        if late:
+            flat = lax.optimization_barrier([below[d] for d in late] + blocks)
+            blocks = list(flat[len(late) :])
+            for d, x in zip(late, flat):
+                pieces[d] = [x] + [swap(x, "wl", e) for e in near[1:]]
+        shares = multiply(high, low, pieces, levels, vox, phases, far, near)
+        blocks += [share.astype(jnp.float16) if k else share for k, share in enumerate(shares)]
+    sent = []
+    for k, share in enumerate(blocks):
+        t, j = divmod(k % (vox * len(far)), len(far))
+        sent.append(send(share, t, far[j]).astype(jnp.float32) if t or j else share)
+    return place(sent, vox, levels, lines, groups, far, near)
 
 
 def solution(mesh):

time: 27.9 us -> 27.2 us (0.975); the launches traced: 27.4 us -> 27 us
  waiting for transfers between devices: 8.52 us -> 4.29 us
  starting transfers between devices: 13.8 us -> 17.8 us
  Pallas kernels: 3.19 us -> 2.82 us
    ppermute x3 -> x6, starting transfers between devices: 3.62 us -> 6.95 us  [send(): return lax.ppermute(x, ('vox', 'wl'), pairs)]
    ppermute x3 -> x6, waiting for transfers between devices: 6.44 us -> 3.11 us  [send(): return lax.ppermute(x, ('vox', 'wl'), pairs)]
    ppermute x5 -> x7, waiting for transfers between devices: 2.07 us -> 1.17 us  [swap(): return lax.ppermute(x, axis, [(i, i ^ bit) for i in range(size)])]
    ppermute x5 -> x7, starting transfers between devices: 2.38 us -> 3.03 us  [swap(): return lax.ppermute(x, axis, [(i, i ^ bit) for i in range(size)])]
    pallas_call x1 -> x2, Pallas kernels: 1.36 us -> 1.01 us  [multiply(): return call(high, low, *flat)]
    unnamed x6 -> x7, local copies, waits for them, and re-layouts: 1.64 us -> 1.64 us
  transfers between devices with their start and end apart: 11 -> 16, of which waited for: 5 -> 5; matrix products, arithmetic and copies ran while one was open for 0% -> 1% of each run, Pallas kernels for 3% -> 7%
where the time goes in v6:
time: 27.2 us; the launch traced here: 27 us
  starting transfers between devices  17.8 us (65%)
  waiting for transfers between devices  4.29 us (16%)
  Pallas kernels  2.82 us (10%)
  local copies, waits for them, and re-layouts  1.69 us (6%)
    ppermute x6, starting transfers between devices, send(): return lax.ppermute(x, ('vox', 'wl'), pairs)  6.95 us
    ppermute x2, starting transfers between devices, climb(): lax.ppermute(x, 'row', [(i - by, i) for i in range(lowest, lowest + count)])  4.82 us
    ppermute x6, waiting for transfers between devices, send(): return lax.ppermute(x, ('vox', 'wl'), pairs)  3.11 us
    ppermute x7, starting transfers between devices, swap(): return lax.ppermute(x, axis, [(i, i ^ bit) for i in range(size)])  3.03 us
    ppermute x1, starting transfers between devices, shift(): return lax.ppermute(x, axis, [(i, (i + by) % size) for i in range(size)])  3.02 us
    unnamed x7, local copies, waits for them, and re-layouts  1.64 us
    ppermute x7, waiting for transfers between devices, swap(): return lax.ppermute(x, axis, [(i, i ^ bit) for i in range(size)])  1.17 us
    pallas_call x2, Pallas kernels, multiply(): return call(high, low, *flat)  1.01 us
  transfers between devices with their start and end apart: 16, of which 5 were waited for; matrix products, arithmetic and copies ran while one was open for 1% of the time, Pallas kernels for 7%

profile of v6, /device:TPU:0, one launch (start us, length us, event | category | flops | bytes accessed | tf_op | source)
XLA Modules:
  0.0 27.0 jit_solution(16279198265901736135)
XLA Ops:
  0.0 0.0 copy-start.2
  0.0 3.0 %collective-permute-start = (bf16[128,640]{1,0:T(8,128)(2,1)}, bf16[128,640]{1,0:T(8,128)(2,1)S(1)}, u32[]{:S(2)}, u32[]{:S(2)}) collective-permute-start(bf16[128,640]{1,0:T(8,128)(2,1)} %jac_ref.1), channel_id=1, source_target_pairs={{0,4},{4,8},{8,12},{12,0},{1,5},{5,9},{9,13},{13,1},{2,6},{6,10},{... | collective-permute-start | bytes 491528 | tf_op jit(solution)/shard_map/ppermute | solution.py:18
  3.0 1.5 %collective-permute-start.1 = (bf16[128,640]{1,0:T(8,128)(2,1)}, bf16[128,640]{1,0:T(8,128)(2,1)S(1)}, u32[]{:S(2)}, u32[]{:S(2)}) collective-permute-start(bf16[128,640]{1,0:T(8,128)(2,1)} %jac_ref.1), channel_id=1, source_target_pairs={{0,2},{1,3},{2,0},{3,1},{4,6},{5,7},{6,4},{7,5},{8,10},{9,11},{10,... | collective-permute-start | bytes 491528 | tf_op jit(solution)/shard_map/ppermute | solution.py:27
  4.5 4.1 %collective-permute-start.6 = (bf16[128,640]{1,0:T(8,128)(2,1)}, bf16[128,640]{1,0:T(8,128)(2,1)S(1)}, u32[]{:S(2)}, u32[]{:S(2)}) collective-permute-start(bf16[128,640]{1,0:T(8,128)(2,1)} %jac_ref.1), channel_id=1, source_target_pairs={{0,12},{1,13},{2,14},{3,15},{16,28},{17,29},{18,30},{19,31}} | collective-permute-start | bytes 491528 | tf_op jit(solution)/shard_map/ppermute | solution.py:22
  8.7 0.0 copy-done.2
  8.7 0.0 copy-start
  8.7 0.9 %copy-done = bf16[128,640]{1,0:T(8,128)(2,1)S(1)} copy-done((bf16[128,640]{1,0:T(8,128)(2,1)S(1)}, bf16[128,640]{1,0:T(8,128)(2,1)}, u32[]{:S(2)}) %copy-start) | copy-done | bytes 163864
  9.7 0.0 copy-start.1
  9.7 0.7 %copy-done.1 = f32[2,640]{1,0:T(2,128)S(1)} copy-done((f32[2,640]{1,0:T(2,128)S(1)}, f32[2,640]{1,0:T(2,128)}, u32[]{:S(2)}) %copy-start.1) | copy-done | bytes 5144
  10.4 0.6 %shard_map.37 = (f32[4,640]{1,0:T(4,128)S(1)}, bf16[128,640]{1,0:T(8,128)(2,1)S(1)}) custom-call(f32[2,4]{1,0:T(2,128)S(1)} %bitcast.1, f32[2,640]{1,0:T(2,128)S(1)} %copy-done.1, bf16[128,640]{1,0:T(8,128)(2,1)S(1)} %copy-done), custom_call_target="tpu_custom_call" | custom-call | tf_op jit(solution)/shard_map/pallas_call | solution.py:96
  10.9 0.0 collective-permute-done.refs_2_
  11.0 0.7 %collective-permute-start.5 = (bf16[128,640]{1,0:T(8,128)(2,1)S(1)}, bf16[128,640]{1,0:T(8,128)(2,1)S(1)}, u32[]{:S(2)}, u32[]{:S(2)}) collective-permute-start(bf16[128,640]{1,0:T(8,128)(2,1)S(1)} %collective-permute-done.refs_2_), channel_id=1, source_target_pairs={{4,8},{8,12},{5,9},{9,13},{6,10},{10,14},{7,11},{11,15},{20,24},{2... | collective-permute-start | bytes 491528 | tf_op jit(solution)/shard_map/ppermute | solution.py:22
  11.7 0.1 collective-permute-start.3
  11.7 0.5 %collective-permute-start.4 = (bf16[64,640]{1,0:T(8,128)(2,1)S(1)}, bf16[64,640]{1,0:T(8,128)(2,1)S(1)}, u32[]{:S(2)}, u32[]{:S(2)}) collective-permute-start(bf16[64,640]{1,0:T(8,128)(2,1)S(1)} %get-tuple-element.47), channel_id=1, source_target_pairs={{0,1},{1,0},{2,3},{3,2},{4,5},{5,4},{6,7},{7,6},{8,9},{9,8},{10,11... | collective-permute-start | bytes 245768 | tf_op jit(solution)/shard_map/ppermute | solution.py:27
  12.2 0.0 collective-permute-done.6.refs_4_
  12.2 0.1 collective-permute-start.2
  12.3 0.0 collective-permute-done.1.refs_1_
  12.3 0.5 %collective-permute-start.7 = (bf16[64,640]{1,0:T(8,128)(2,1)S(1)}, bf16[64,640]{1,0:T(8,128)(2,1)S(1)}, u32[]{:S(2)}, u32[]{:S(2)}) collective-permute-start(bf16[64,640]{1,0:T(8,128)(2,1)S(1)} %get-tuple-element.45), channel_id=1, source_target_pairs={{0,1},{1,0},{2,3},{3,2},{4,5},{5,4},{6,7},{7,6},{8,9},{9,8},{10,11... | collective-permute-start | bytes 245768 | tf_op jit(solution)/shard_map/ppermute | solution.py:27
  12.8 0.3 shard_map.38
  13.1 0.0 collective-permute-done.3
  13.1 0.1 collective-permute-start.8
  13.3 0.0 collective-permute-done.4
  13.3 0.5 %collective-permute-done.7 = bf16[64,640]{1,0:T(8,128)(2,1)S(1)} collective-permute-done((bf16[64,640]{1,0:T(8,128)(2,1)S(1)}, bf16[64,640]{1,0:T(8,128)(2,1)S(1)}, u32[]{:S(2)}, u32[]{:S(2)}) %collective-permute-start.7) | collective-permute-done | bytes 81952 | tf_op jit(solution)/shard_map/ppermute | solution.py:27
  13.8 0.7 %collective-permute-done.8 = bf16[64,640]{1,0:T(8,128)(2,1)S(1)} collective-permute-done((bf16[64,640]{1,0:T(8,128)(2,1)S(1)}, bf16[64,640]{1,0:T(8,128)(2,1)S(1)}, u32[]{:S(2)}, u32[]{:S(2)}) %collective-permute-start.8) | collective-permute-done | bytes 81952 | tf_op jit(solution)/shard_map/ppermute | solution.py:27
  14.5 0.0 collective-permute-done.2.refs_1_
  14.5 0.9 %shard_map.39 = (f32[128,256]{1,0:T(8,128)S(1)}, f32[144,256]{1,0:T(8,128)S(1)}, f32[144,256]{1,0:T(8,128)S(1)}, f32[144,256]{1,0:T(8,128)S(1)}) custom-call(bf16[2,256,640]{2,1,0:T(8,128)(2,1)S(1)} %get-tuple-element.29.high_ref, bf16[2,256,640]{2,1,0:T(8,128)(2,1)S(1)} %get-tuple-element.30.low_ref, bf16[128,640]{1,0:T(8,128)(2,1)S(1)} %get-tuple-element.28.refs_0_, ...), custom_call_target="tpu_custom_call" | custom-call | tf_op jit(solution)/shard_map/pallas_call | solution.py:175
  15.4 0.0 collective-permute-done.5.refs_4_
  15.4 0.2 collective-permute-start.9
  15.7 1.4 %collective-permute-start.13 = (f16[144,256]{1,0:T(8,128)(2,1)S(1)}, f16[144,256]{1,0:T(8,128)(2,1)S(1)}, u32[]{:S(2)}, u32[]{:S(2)}) collective-permute-start(f16[144,256]{1,0:T(8,128)(2,1)S(1)} %convert_element_type.38), channel_id=1, source_target_pairs={{0,18},{1,19},{2,16},{3,17},{16,2},{17,3},{18,0},{19,1},{4,22},{5,... | collective-permute-start | bytes 221192 | tf_op jit(solution)/shard_map/ppermute | solution.py:35
  17.1 0.4 %collective-permute-start.14 = (f16[144,256]{1,0:T(8,128)(2,1)S(1)}, f16[144,256]{1,0:T(8,128)(2,1)S(1)}, u32[]{:S(2)}, u32[]{:S(2)}) collective-permute-start(f16[144,256]{1,0:T(8,128)(2,1)S(1)} %convert_element_type.37), channel_id=1, source_target_pairs={{0,16},{1,17},{2,18},{3,19},{16,0},{17,1},{18,2},{19,3},{4,20},{5,... | collective-permute-start | bytes 221192 | tf_op jit(solution)/shard_map/ppermute | solution.py:35
  17.5 1.7 %collective-permute-start.15 = (f16[144,256]{1,0:T(8,128)(2,1)S(1)}, f16[144,256]{1,0:T(8,128)(2,1)S(1)}, u32[]{:S(2)}, u32[]{:S(2)}) collective-permute-start(f16[144,256]{1,0:T(8,128)(2,1)S(1)} %convert_element_type.36), channel_id=1, source_target_pairs={{0,2},{1,3},{2,0},{3,1},{16,18},{17,19},{18,16},{19,17},{4,6},{5,7... | collective-permute-start | bytes 221192 | tf_op jit(solution)/shard_map/ppermute | solution.py:35
  19.2 0.0 collective-permute-done.9.refs_5_
  19.2 0.1 shard_map.40
  19.3 1.5 %collective-permute-start.10 = (f16[144,256]{1,0:T(8,128)(2,1)S(1)}, f16[144,256]{1,0:T(8,128)(2,1)S(1)}, u32[]{:S(2)}, u32[]{:S(2)}) collective-permute-start(f16[144,256]{1,0:T(8,128)(2,1)S(1)} %convert_element_type.39), channel_id=1, source_target_pairs={{0,18},{1,19},{2,16},{3,17},{16,2},{17,3},{18,0},{19,1},{4,22},{5,... | collective-permute-start | bytes 221192 | tf_op jit(solution)/shard_map/ppermute | solution.py:35
  20.8 0.4 %collective-permute-start.11 = (f16[144,256]{1,0:T(8,128)(2,1)S(1)}, f16[144,256]{1,0:T(8,128)(2,1)S(1)}, u32[]{:S(2)}, u32[]{:S(2)}) collective-permute-start(f16[144,256]{1,0:T(8,128)(2,1)S(1)} %convert_element_type.41), channel_id=1, source_target_pairs={{0,16},{1,17},{2,18},{3,19},{16,0},{17,1},{18,2},{19,3},{4,20},{5,... | collective-permute-start | bytes 221192 | tf_op jit(solution)/shard_map/ppermute | solution.py:35
  21.3 0.2 collective-permute-done.13
  21.5 1.5 %collective-permute-start.12 = (f16[144,256]{1,0:T(8,128)(2,1)S(1)}, f16[144,256]{1,0:T(8,128)(2,1)S(1)}, u32[]{:S(2)}, u32[]{:S(2)}) collective-permute-start(f16[144,256]{1,0:T(8,128)(2,1)S(1)} %convert_element_type.43), channel_id=1, source_target_pairs={{0,2},{1,3},{2,0},{3,1},{16,18},{17,19},{18,16},{19,17},{4,6},{5,7... | collective-permute-start | bytes 221192 | tf_op jit(solution)/shard_map/ppermute | solution.py:35
  23.0 0.0 collective-permute-done.14
  23.1 0.0 collective-permute-done.15
  23.1 2.2 %collective-permute-done.10 = f16[144,256]{1,0:T(8,128)(2,1)S(1)} collective-permute-done((f16[144,256]{1,0:T(8,128)(2,1)S(1)}, f16[144,256]{1,0:T(8,128)(2,1)S(1)}, u32[]{:S(2)}, u32[]{:S(2)}) %collective-permute-start.10) | collective-permute-done | bytes 73760 | tf_op jit(solution)/shard_map/ppermute | solution.py:35
  25.3 0.0 collective-permute-done.11
  25.3 0.7 %collective-permute-done.12 = f16[144,256]{1,0:T(8,128)(2,1)S(1)} collective-permute-done((f16[144,256]{1,0:T(8,128)(2,1)S(1)}, f16[144,256]{1,0:T(8,128)(2,1)S(1)}, u32[]{:S(2)}, u32[]{:S(2)}) %collective-permute-start.12) | collective-permute-done | bytes 73760 | tf_op jit(solution)/shard_map/ppermute | solution.py:35
  26.1 1.0 %shard_map.41 = f32[128,1024]{1,0:T(8,128)} custom-call(f32[144,256]{1,0:T(8,128)S(1)} %convert_element_type.40.refs_0_, f32[144,256]{1,0:T(8,128)S(1)} %convert_element_type.42.refs_1_, f32[144,256]{1,0:T(8,128)S(1)} %convert_element_type.44.refs_2_, f32[128,256]{1,0:T(8,128)S(1)} %get-tuple-element.40.refs_3_, ...), custom_call_target="tpu_custom_call" | custom-call | tf_op jit(solution)/shard_map/pallas_call | solution.py:206
  (17 shorter events, 0.2 us)
Async XLA Ops:
  0.0 8.7 %copy-start.2 = (f32[4,2]{0,1:T(2,128)S(1)}, f32[4,2]{0,1:T(2,128)}, u32[]{:S(2)}) copy-start(f32[4,2]{0,1:T(2,128)} %param.4) | copy-start | bytes 100
  0.0 10.9 %collective-permute-start = (bf16[128,640]{1,0:T(8,128)(2,1)}, bf16[128,640]{1,0:T(8,128)(2,1)S(1)}, u32[]{:S(2)}, u32[]{:S(2)}) collective-permute-start(bf16[128,640]{1,0:T(8,128)(2,1)} %jac_ref.1), channel_id=1, source_target_pairs={{0,4},{4,8},{8,12},{12,0},{1,5},{5,9},{9,13},{13,1},{2,6},{6,10},{... | collective-permute-start | bytes 491528 | tf_op jit(solution)/shard_map/ppermute | solution.py:18
  3.0 9.3 %collective-permute-start.1 = (bf16[128,640]{1,0:T(8,128)(2,1)}, bf16[128,640]{1,0:T(8,128)(2,1)S(1)}, u32[]{:S(2)}, u32[]{:S(2)}) collective-permute-start(bf16[128,640]{1,0:T(8,128)(2,1)} %jac_ref.1), channel_id=1, source_target_pairs={{0,2},{1,3},{2,0},{3,1},{4,6},{5,7},{6,4},{7,5},{8,10},{9,11},{10,... | collective-permute-start | bytes 491528 | tf_op jit(solution)/shard_map/ppermute | solution.py:27
  4.5 7.7 %collective-permute-start.6 = (bf16[128,640]{1,0:T(8,128)(2,1)}, bf16[128,640]{1,0:T(8,128)(2,1)S(1)}, u32[]{:S(2)}, u32[]{:S(2)}) collective-permute-start(bf16[128,640]{1,0:T(8,128)(2,1)} %jac_ref.1), channel_id=1, source_target_pairs={{0,12},{1,13},{2,14},{3,15},{16,28},{17,29},{18,30},{19,31}} | collective-permute-start | bytes 491528 | tf_op jit(solution)/shard_map/ppermute | solution.py:22
  8.7 1.0 %copy-start = (bf16[128,640]{1,0:T(8,128)(2,1)S(1)}, bf16[128,640]{1,0:T(8,128)(2,1)}, u32[]{:S(2)}) copy-start(bf16[128,640]{1,0:T(8,128)(2,1)} %jac_ref.1) | copy-start | bytes 491524
  9.7 0.7 %copy-start.1 = (f32[2,640]{1,0:T(2,128)S(1)}, f32[2,640]{1,0:T(2,128)}, u32[]{:S(2)}) copy-start(f32[2,640]{1,0:T(2,128)} %prior_ref.1) | copy-start | bytes 15364
  11.0 4.5 %collective-permute-start.5 = (bf16[128,640]{1,0:T(8,128)(2,1)S(1)}, bf16[128,640]{1,0:T(8,128)(2,1)S(1)}, u32[]{:S(2)}, u32[]{:S(2)}) collective-permute-start(bf16[128,640]{1,0:T(8,128)(2,1)S(1)} %collective-permute-done.refs_2_), channel_id=1, source_target_pairs={{4,8},{8,12},{5,9},{9,13},{6,10},{10,14},{7,11},{11,15},{20,24},{2... | collective-permute-start | bytes 491528 | tf_op jit(solution)/shard_map/ppermute | solution.py:22
  11.7 1.4 %collective-permute-start.3 = (bf16[64,640]{1,0:T(8,128)(2,1)S(1)}, bf16[64,640]{1,0:T(8,128)(2,1)S(1)}, u32[]{:S(2)}, u32[]{:S(2)}) collective-permute-start(bf16[64,640]{1,0:T(8,128)(2,1)S(1)} %get-tuple-element.48), channel_id=1, source_target_pairs={{0,1},{1,0},{2,3},{3,2},{4,5},{5,4},{6,7},{7,6},{8,9},{9,8},{10,11... | collective-permute-start | bytes 245768 | tf_op jit(solution)/shard_map/ppermute | solution.py:27
  11.7 1.5 %collective-permute-start.4 = (bf16[64,640]{1,0:T(8,128)(2,1)S(1)}, bf16[64,640]{1,0:T(8,128)(2,1)S(1)}, u32[]{:S(2)}, u32[]{:S(2)}) collective-permute-start(bf16[64,640]{1,0:T(8,128)(2,1)S(1)} %get-tuple-element.47), channel_id=1, source_target_pairs={{0,1},{1,0},{2,3},{3,2},{4,5},{5,4},{6,7},{7,6},{8,9},{9,8},{10,11... | collective-permute-start | bytes 245768 | tf_op jit(solution)/shard_map/ppermute | solution.py:27
  12.2 2.2 %collective-permute-start.2 = (bf16[128,640]{1,0:T(8,128)(2,1)S(1)}, bf16[128,640]{1,0:T(8,128)(2,1)S(1)}, u32[]{:S(2)}, u32[]{:S(2)}) collective-permute-start(bf16[128,640]{1,0:T(8,128)(2,1)S(1)} %get-tuple-element.28.refs_0_), channel_id=1, source_target_pairs={{0,1},{1,0},{2,3},{3,2},{4,5},{5,4},{6,7},{7,6},{8,9},{9,8},{10,11... | collective-permute-start | bytes 491528 | tf_op jit(solution)/shard_map/ppermute | solution.py:27
  12.3 1.4 %collective-permute-start.7 = (bf16[64,640]{1,0:T(8,128)(2,1)S(1)}, bf16[64,640]{1,0:T(8,128)(2,1)S(1)}, u32[]{:S(2)}, u32[]{:S(2)}) collective-permute-start(bf16[64,640]{1,0:T(8,128)(2,1)S(1)} %get-tuple-element.45), channel_id=1, source_target_pairs={{0,1},{1,0},{2,3},{3,2},{4,5},{5,4},{6,7},{7,6},{8,9},{9,8},{10,11... | collective-permute-start | bytes 245768 | tf_op jit(solution)/shard_map/ppermute | solution.py:27
  13.1 1.3 %collective-permute-start.8 = (bf16[64,640]{1,0:T(8,128)(2,1)S(1)}, bf16[64,640]{1,0:T(8,128)(2,1)S(1)}, u32[]{:S(2)}, u32[]{:S(2)}) collective-permute-start(bf16[64,640]{1,0:T(8,128)(2,1)S(1)} %get-tuple-element.46), channel_id=1, source_target_pairs={{0,1},{1,0},{2,3},{3,2},{4,5},{5,4},{6,7},{7,6},{8,9},{9,8},{10,11... | collective-permute-start | bytes 245768 | tf_op jit(solution)/shard_map/ppermute | solution.py:27
  15.4 3.7 %collective-permute-start.9 = (bf16[128,640]{1,0:T(8,128)(2,1)S(1)}, bf16[128,640]{1,0:T(8,128)(2,1)S(1)}, u32[]{:S(2)}, u32[]{:S(2)}) collective-permute-start(bf16[128,640]{1,0:T(8,128)(2,1)S(1)} %collective-permute-done.5.refs_4_), channel_id=1, source_target_pairs={{0,1},{1,0},{2,3},{3,2},{4,5},{5,4},{6,7},{7,6},{8,9},{9,8},{10,11... | collective-permute-start | bytes 491528 | tf_op jit(solution)/shard_map/ppermute | solution.py:27
  15.7 5.8 %collective-permute-start.13 = (f16[144,256]{1,0:T(8,128)(2,1)S(1)}, f16[144,256]{1,0:T(8,128)(2,1)S(1)}, u32[]{:S(2)}, u32[]{:S(2)}) collective-permute-start(f16[144,256]{1,0:T(8,128)(2,1)S(1)} %convert_element_type.38), channel_id=1, source_target_pairs={{0,18},{1,19},{2,16},{3,17},{16,2},{17,3},{18,0},{19,1},{4,22},{5,... | collective-permute-start | bytes 221192 | tf_op jit(solution)/shard_map/ppermute | solution.py:35
  17.1 6.0 %collective-permute-start.14 = (f16[144,256]{1,0:T(8,128)(2,1)S(1)}, f16[144,256]{1,0:T(8,128)(2,1)S(1)}, u32[]{:S(2)}, u32[]{:S(2)}) collective-permute-start(f16[144,256]{1,0:T(8,128)(2,1)S(1)} %convert_element_type.37), channel_id=1, source_target_pairs={{0,16},{1,17},{2,18},{3,19},{16,0},{17,1},{18,2},{19,3},{4,20},{5,... | collective-permute-start | bytes 221192 | tf_op jit(solution)/shard_map/ppermute | solution.py:35
  17.5 5.6 %collective-permute-start.15 = (f16[144,256]{1,0:T(8,128)(2,1)S(1)}, f16[144,256]{1,0:T(8,128)(2,1)S(1)}, u32[]{:S(2)}, u32[]{:S(2)}) collective-permute-start(f16[144,256]{1,0:T(8,128)(2,1)S(1)} %convert_element_type.36), channel_id=1, source_target_pairs={{0,2},{1,3},{2,0},{3,1},{16,18},{17,19},{18,16},{19,17},{4,6},{5,7... | collective-permute-start | bytes 221192 | tf_op jit(solution)/shard_map/ppermute | solution.py:35
  19.3 6.0 %collective-permute-start.10 = (f16[144,256]{1,0:T(8,128)(2,1)S(1)}, f16[144,256]{1,0:T(8,128)(2,1)S(1)}, u32[]{:S(2)}, u32[]{:S(2)}) collective-permute-start(f16[144,256]{1,0:T(8,128)(2,1)S(1)} %convert_element_type.39), channel_id=1, source_target_pairs={{0,18},{1,19},{2,16},{3,17},{16,2},{17,3},{18,0},{19,1},{4,22},{5,... | collective-permute-start | bytes 221192 | tf_op jit(solution)/shard_map/ppermute | solution.py:35
  20.8 4.5 %collective-permute-start.11 = (f16[144,256]{1,0:T(8,128)(2,1)S(1)}, f16[144,256]{1,0:T(8,128)(2,1)S(1)}, u32[]{:S(2)}, u32[]{:S(2)}) collective-permute-start(f16[144,256]{1,0:T(8,128)(2,1)S(1)} %convert_element_type.41), channel_id=1, source_target_pairs={{0,16},{1,17},{2,18},{3,19},{16,0},{17,1},{18,2},{19,3},{4,20},{5,... | collective-permute-start | bytes 221192 | tf_op jit(solution)/shard_map/ppermute | solution.py:35
  21.5 4.5 %collective-permute-start.12 = (f16[144,256]{1,0:T(8,128)(2,1)S(1)}, f16[144,256]{1,0:T(8,128)(2,1)S(1)}, u32[]{:S(2)}, u32[]{:S(2)}) collective-permute-start(f16[144,256]{1,0:T(8,128)(2,1)S(1)} %convert_element_type.43), channel_id=1, source_target_pairs={{0,2},{1,3},{2,0},{3,1},{16,18},{17,19},{18,16},{19,17},{4,6},{5,7... | collective-permute-start | bytes 221192 | tf_op jit(solution)/shard_map/ppermute | solution.py:35

commit v7 on v6

--- a/solution.py
+++ b/solution.py
@@ -35,7 +35,7 @@
     return lax.ppermute(x, ("vox", "wl"), pairs)
 
 
-def kernel_call(kernel, ins, outs, scratch=()):
+def kernel_call(kernel, ins, outs, scratch=(), cost=None):
     return functools.partial(
         pl.pallas_call,
         kernel,
@@ -44,6 +44,7 @@
         out_shape=outs,
         scratch_shapes=scratch,
         compiler_params=pltpu.CompilerParams(vmem_limit_bytes=LIMIT),
+        cost_estimate=cost,
     )()
 
 
@@ -92,7 +93,7 @@
 def prepare(extinction, prior, jac, far, near):
     weights = jax.ShapeDtypeStruct((len(far) * len(near), jac.shape[1]), jnp.float32)
     own = jax.ShapeDtypeStruct(jac.shape, jac.dtype)
-    call = kernel_call(functools.partial(prepare_kernel, far, near), [SMEM, VMEM, VMEM], [weights, own])
+    call = kernel_call(functools.partial(prepare_kernel, far, near), [SMEM, VMEM, VMEM], [weights, own], cost=pl.CostEstimate(flops=1, bytes_accessed=8000000, transcendentals=0))
     return call(extinction, prior, jac)
 
 
@@ -111,7 +112,7 @@
 def weigh(weights, rows, far, near):
     tile, depth = rows[0].shape
     like = jax.ShapeDtypeStruct((len(near), len(far) * tile, depth), jnp.bfloat16)
-    call = kernel_call(functools.partial(weigh_kernel, far, near), [VMEM] * (1 + len(rows)), [like, like])
+    call = kernel_call(functools.partial(weigh_kernel, far, near), [VMEM] * (1 + len(rows)), [like, like], cost=pl.CostEstimate(flops=1, bytes_accessed=1, transcendentals=0))
     return call(weights, *rows)
 
 
@@ -171,12 +172,14 @@
         [VMEM] * (2 + len(flat)),
         [jax.ShapeDtypeStruct((height, width), jnp.float32) for height in heights],
         [pltpu.VMEM((len(near), vox * len(phases) * tile, depth), jnp.bfloat16)],
+        None if phases[0] == 0 else None,
     )
     return call(high, low, *flat)
 
 
 def place_kernel(vox, levels, lines, groups, far, near, *refs):
-    blocks, out_ref = refs[-2::-1], refs[-1]
+    perm = [7, 6, 5, 4, 3, 1, 2, 0] if len(refs) == 9 else range(len(refs) - 1)
+    blocks, out_ref = [refs[list(perm).index(k)] for k in range(len(refs) - 1)], refs[-1]
     tile, slots = out_ref.shape[0], levels // vox
     v, z, w = (lax.axis_index(a) for a in ("vox", "row", "wl"))
     rows = (z * lines + w) * tile + lax.broadcasted_iota(jnp.int32, (tile, tile), 0)
@@ -203,7 +206,8 @@
         [VMEM] * len(blocks),
         [jax.ShapeDtypeStruct((tile, levels // vox * lines * tile), jnp.float32)],
     )
-    return call(*blocks[::-1])[0]
+    perm = [7, 6, 5, 4, 3, 1, 2, 0] if len(blocks) == 8 else range(len(blocks))
+    return call(*[blocks[k] for k in perm])[0]
 
 
 def on_device(jac, extinction, prior_var):
@@ -229,9 +233,10 @@
     below[0] = own
 
     def both(d):
-        cuts = (below[d],) if d == 0 else (below[d][: tile // 2], below[d][tile // 2 :])
+        n = {0: 1, 1: 2}.get(d, 2)
+        cuts = [below[d][k * tile // n : (k + 1) * tile // n] for k in range(n)]
         swapped = [[swap(x, "wl", e) for x in cuts] for e in near[1:]]
-        return [below[d]] + [jnp.concatenate(xs, axis=0) if d else xs[0] for xs in swapped]
+        return [below[d]] + [jnp.concatenate(xs, axis=0) if len(xs) > 1 else xs[0] for xs in swapped]
 
     pieces = {d: both(d) for d in (0, 1, levels - 1)}
     blocks = []

time: 27.2 us -> 27.2 us (level)
  transfers between devices with their start and end apart: 16 -> 16, of which waited for: 5 -> 6; matrix products, arithmetic and copies ran while one was open for 1% -> 1% of each run, Pallas kernels for 7% -> 7%
where the time goes in v7:
time: 27.2 us; the launch traced here: 27 us
  starting transfers between devices  18 us (66%)
  waiting for transfers between devices  4.04 us (15%)
  Pallas kernels  2.82 us (10%)
  local copies, waits for them, and re-layouts  1.69 us (6%)
    ppermute x6, starting transfers between devices, send(): return lax.ppermute(x, ('vox', 'wl'), pairs)  7.17 us
    ppermute x2, starting transfers between devices, climb(): lax.ppermute(x, 'row', [(i - by, i) for i in range(lowest, lowest + count)])  4.82 us
    ppermute x7, starting transfers between devices, swap(): return lax.ppermute(x, axis, [(i, i ^ bit) for i in range(size)])  3.03 us
    ppermute x1, starting transfers between devices, shift(): return lax.ppermute(x, axis, [(i, (i + by) % size) for i in range(size)])  3.02 us
    ppermute x6, waiting for transfers between devices, send(): return lax.ppermute(x, ('vox', 'wl'), pairs)  2.87 us
    unnamed x7, local copies, waits for them, and re-layouts  1.64 us
    ppermute x7, waiting for transfers between devices, swap(): return lax.ppermute(x, axis, [(i, i ^ bit) for i in range(size)])  1.17 us
    pallas_call x2, Pallas kernels, multiply(): return call(high, low, *flat)  1.01 us
  transfers between devices with their start and end apart: 16, of which 6 were waited for; matrix products, arithmetic and copies ran while one was open for 1% of the time, Pallas kernels for 7%

profile of v7, /device:TPU:0, one launch (start us, length us, event | category | flops | bytes accessed | tf_op | source)
XLA Modules:
  0.0 27.0 jit_solution(14764133427887128344)
XLA Ops:
  0.0 0.0 copy-start.2
  0.0 3.0 %collective-permute-start = (bf16[128,640]{1,0:T(8,128)(2,1)}, bf16[128,640]{1,0:T(8,128)(2,1)S(1)}, u32[]{:S(2)}, u32[]{:S(2)}) collective-permute-start(bf16[128,640]{1,0:T(8,128)(2,1)} %jac_ref.1), channel_id=1, source_target_pairs={{0,4},{4,8},{8,12},{12,0},{1,5},{5,9},{9,13},{13,1},{2,6},{6,10},{... | collective-permute-start | bytes 491528 | tf_op jit(solution)/shard_map/ppermute | solution.py:18
  3.0 1.5 %collective-permute-start.1 = (bf16[128,640]{1,0:T(8,128)(2,1)}, bf16[128,640]{1,0:T(8,128)(2,1)S(1)}, u32[]{:S(2)}, u32[]{:S(2)}) collective-permute-start(bf16[128,640]{1,0:T(8,128)(2,1)} %jac_ref.1), channel_id=1, source_target_pairs={{0,2},{1,3},{2,0},{3,1},{4,6},{5,7},{6,4},{7,5},{8,10},{9,11},{10,... | collective-permute-start | bytes 491528 | tf_op jit(solution)/shard_map/ppermute | solution.py:27
  4.5 4.1 %collective-permute-start.6 = (bf16[128,640]{1,0:T(8,128)(2,1)}, bf16[128,640]{1,0:T(8,128)(2,1)S(1)}, u32[]{:S(2)}, u32[]{:S(2)}) collective-permute-start(bf16[128,640]{1,0:T(8,128)(2,1)} %jac_ref.1), channel_id=1, source_target_pairs={{0,12},{1,13},{2,14},{3,15},{16,28},{17,29},{18,30},{19,31}} | collective-permute-start | bytes 491528 | tf_op jit(solution)/shard_map/ppermute | solution.py:22
  8.7 0.0 copy-done.2
  8.7 0.0 copy-start
  8.7 0.9 %copy-done = bf16[128,640]{1,0:T(8,128)(2,1)S(1)} copy-done((bf16[128,640]{1,0:T(8,128)(2,1)S(1)}, bf16[128,640]{1,0:T(8,128)(2,1)}, u32[]{:S(2)}) %copy-start) | copy-done | bytes 163864
  9.7 0.0 copy-start.1
  9.7 0.7 %copy-done.1 = f32[2,640]{1,0:T(2,128)S(1)} copy-done((f32[2,640]{1,0:T(2,128)S(1)}, f32[2,640]{1,0:T(2,128)}, u32[]{:S(2)}) %copy-start.1) | copy-done | bytes 5144
  10.4 0.6 %shard_map.37 = (f32[4,640]{1,0:T(4,128)S(1)}, bf16[128,640]{1,0:T(8,128)(2,1)S(1)}) custom-call(f32[2,4]{1,0:T(2,128)S(1)} %bitcast.1, f32[2,640]{1,0:T(2,128)S(1)} %copy-done.1, bf16[128,640]{1,0:T(8,128)(2,1)S(1)} %copy-done), custom_call_target="tpu_custom_call" | custom-call | flops 1 | bytes 8000000 | tf_op jit(solution)/shard_map/pallas_call | solution.py:97
  10.9 0.0 collective-permute-done.refs_2_
  11.0 0.7 %collective-permute-start.5 = (bf16[128,640]{1,0:T(8,128)(2,1)S(1)}, bf16[128,640]{1,0:T(8,128)(2,1)S(1)}, u32[]{:S(2)}, u32[]{:S(2)}) collective-permute-start(bf16[128,640]{1,0:T(8,128)(2,1)S(1)} %collective-permute-done.refs_2_), channel_id=1, source_target_pairs={{4,8},{8,12},{5,9},{9,13},{6,10},{10,14},{7,11},{11,15},{20,24},{2... | collective-permute-start | bytes 491528 | tf_op jit(solution)/shard_map/ppermute | solution.py:22
  11.7 0.1 collective-permute-start.3
  11.7 0.5 %collective-permute-start.4 = (bf16[64,640]{1,0:T(8,128)(2,1)S(1)}, bf16[64,640]{1,0:T(8,128)(2,1)S(1)}, u32[]{:S(2)}, u32[]{:S(2)}) collective-permute-start(bf16[64,640]{1,0:T(8,128)(2,1)S(1)} %get-tuple-element.47), channel_id=1, source_target_pairs={{0,1},{1,0},{2,3},{3,2},{4,5},{5,4},{6,7},{7,6},{8,9},{9,8},{10,11... | collective-permute-start | bytes 245768 | tf_op jit(solution)/shard_map/ppermute | solution.py:27
  12.2 0.0 collective-permute-done.6.refs_4_
  12.2 0.1 collective-permute-start.2
  12.3 0.0 collective-permute-done.1.refs_1_
  12.3 0.5 %collective-permute-start.7 = (bf16[64,640]{1,0:T(8,128)(2,1)S(1)}, bf16[64,640]{1,0:T(8,128)(2,1)S(1)}, u32[]{:S(2)}, u32[]{:S(2)}) collective-permute-start(bf16[64,640]{1,0:T(8,128)(2,1)S(1)} %get-tuple-element.45), channel_id=1, source_target_pairs={{0,1},{1,0},{2,3},{3,2},{4,5},{5,4},{6,7},{7,6},{8,9},{9,8},{10,11... | collective-permute-start | bytes 245768 | tf_op jit(solution)/shard_map/ppermute | solution.py:27
  12.8 0.3 shard_map.38
  13.1 0.0 collective-permute-done.3
  13.1 0.1 collective-permute-start.8
  13.3 0.0 collective-permute-done.4
  13.3 0.5 %collective-permute-done.7 = bf16[64,640]{1,0:T(8,128)(2,1)S(1)} collective-permute-done((bf16[64,640]{1,0:T(8,128)(2,1)S(1)}, bf16[64,640]{1,0:T(8,128)(2,1)S(1)}, u32[]{:S(2)}, u32[]{:S(2)}) %collective-permute-start.7) | collective-permute-done | bytes 81952 | tf_op jit(solution)/shard_map/ppermute | solution.py:27
  13.8 0.7 %collective-permute-done.8 = bf16[64,640]{1,0:T(8,128)(2,1)S(1)} collective-permute-done((bf16[64,640]{1,0:T(8,128)(2,1)S(1)}, bf16[64,640]{1,0:T(8,128)(2,1)S(1)}, u32[]{:S(2)}, u32[]{:S(2)}) %collective-permute-start.8) | collective-permute-done | bytes 81952 | tf_op jit(solution)/shard_map/ppermute | solution.py:27
  14.5 0.0 collective-permute-done.2.refs_1_
  14.5 0.9 %shard_map.39 = (f32[128,256]{1,0:T(8,128)S(1)}, f32[144,256]{1,0:T(8,128)S(1)}, f32[144,256]{1,0:T(8,128)S(1)}, f32[144,256]{1,0:T(8,128)S(1)}) custom-call(bf16[2,256,640]{2,1,0:T(8,128)(2,1)S(1)} %get-tuple-element.29.high_ref, bf16[2,256,640]{2,1,0:T(8,128)(2,1)S(1)} %get-tuple-element.30.low_ref, bf16[128,640]{1,0:T(8,128)(2,1)S(1)} %get-tuple-element.28.refs_0_, ...), custom_call_target="tpu_custom_call" | custom-call | tf_op jit(solution)/shard_map/pallas_call | solution.py:177
  15.4 0.0 collective-permute-done.5.refs_4_
  15.4 0.2 collective-permute-start.9
  15.7 1.4 %collective-permute-start.13 = (f16[144,256]{1,0:T(8,128)(2,1)S(1)}, f16[144,256]{1,0:T(8,128)(2,1)S(1)}, u32[]{:S(2)}, u32[]{:S(2)}) collective-permute-start(f16[144,256]{1,0:T(8,128)(2,1)S(1)} %convert_element_type.38), channel_id=1, source_target_pairs={{0,18},{1,19},{2,16},{3,17},{16,2},{17,3},{18,0},{19,1},{4,22},{5,... | collective-permute-start | bytes 221192 | tf_op jit(solution)/shard_map/ppermute | solution.py:35
  17.1 1.5 %collective-permute-start.14 = (f16[144,256]{1,0:T(8,128)(2,1)S(1)}, f16[144,256]{1,0:T(8,128)(2,1)S(1)}, u32[]{:S(2)}, u32[]{:S(2)}) collective-permute-start(f16[144,256]{1,0:T(8,128)(2,1)S(1)} %convert_element_type.36), channel_id=1, source_target_pairs={{0,2},{1,3},{2,0},{3,1},{16,18},{17,19},{18,16},{19,17},{4,6},{5,7... | collective-permute-start | bytes 221192 | tf_op jit(solution)/shard_map/ppermute | solution.py:35
  18.6 0.5 %collective-permute-start.15 = (f16[144,256]{1,0:T(8,128)(2,1)S(1)}, f16[144,256]{1,0:T(8,128)(2,1)S(1)}, u32[]{:S(2)}, u32[]{:S(2)}) collective-permute-start(f16[144,256]{1,0:T(8,128)(2,1)S(1)} %convert_element_type.37), channel_id=1, source_target_pairs={{0,16},{1,17},{2,18},{3,19},{16,0},{17,1},{18,2},{19,3},{4,20},{5,... | collective-permute-start | bytes 221192 | tf_op jit(solution)/shard_map/ppermute | solution.py:35
  19.2 0.0 collective-permute-done.9.refs_5_
  19.2 0.1 shard_map.40
  19.3 1.5 %collective-permute-start.10 = (f16[144,256]{1,0:T(8,128)(2,1)S(1)}, f16[144,256]{1,0:T(8,128)(2,1)S(1)}, u32[]{:S(2)}, u32[]{:S(2)}) collective-permute-start(f16[144,256]{1,0:T(8,128)(2,1)S(1)} %convert_element_type.39), channel_id=1, source_target_pairs={{0,18},{1,19},{2,16},{3,17},{16,2},{17,3},{18,0},{19,1},{4,22},{5,... | collective-permute-start | bytes 221192 | tf_op jit(solution)/shard_map/ppermute | solution.py:35
  20.8 0.4 %collective-permute-start.11 = (f16[144,256]{1,0:T(8,128)(2,1)S(1)}, f16[144,256]{1,0:T(8,128)(2,1)S(1)}, u32[]{:S(2)}, u32[]{:S(2)}) collective-permute-start(f16[144,256]{1,0:T(8,128)(2,1)S(1)} %convert_element_type.41), channel_id=1, source_target_pairs={{0,16},{1,17},{2,18},{3,19},{16,0},{17,1},{18,2},{19,3},{4,20},{5,... | collective-permute-start | bytes 221192 | tf_op jit(solution)/shard_map/ppermute | solution.py:35
  21.3 0.0 collective-permute-done.13
  21.3 1.7 %collective-permute-start.12 = (f16[144,256]{1,0:T(8,128)(2,1)S(1)}, f16[144,256]{1,0:T(8,128)(2,1)S(1)}, u32[]{:S(2)}, u32[]{:S(2)}) collective-permute-start(f16[144,256]{1,0:T(8,128)(2,1)S(1)} %convert_element_type.43), channel_id=1, source_target_pairs={{0,2},{1,3},{2,0},{3,1},{16,18},{17,19},{18,16},{19,17},{4,6},{5,7... | collective-permute-start | bytes 221192 | tf_op jit(solution)/shard_map/ppermute | solution.py:35
  23.0 0.0 collective-permute-done.14
  23.1 0.7 %collective-permute-done.15 = f16[144,256]{1,0:T(8,128)(2,1)S(1)} collective-permute-done((f16[144,256]{1,0:T(8,128)(2,1)S(1)}, f16[144,256]{1,0:T(8,128)(2,1)S(1)}, u32[]{:S(2)}, u32[]{:S(2)}) %collective-permute-start.15) | collective-permute-done | bytes 73760 | tf_op jit(solution)/shard_map/ppermute | solution.py:35
  23.8 1.5 %collective-permute-done.10 = f16[144,256]{1,0:T(8,128)(2,1)S(1)} collective-permute-done((f16[144,256]{1,0:T(8,128)(2,1)S(1)}, f16[144,256]{1,0:T(8,128)(2,1)S(1)}, u32[]{:S(2)}, u32[]{:S(2)}) %collective-permute-start.10) | collective-permute-done | bytes 73760 | tf_op jit(solution)/shard_map/ppermute | solution.py:35
  25.3 0.4 %collective-permute-done.11 = f16[144,256]{1,0:T(8,128)(2,1)S(1)} collective-permute-done((f16[144,256]{1,0:T(8,128)(2,1)S(1)}, f16[144,256]{1,0:T(8,128)(2,1)S(1)}, u32[]{:S(2)}, u32[]{:S(2)}) %collective-permute-start.11) | collective-permute-done | bytes 73760 | tf_op jit(solution)/shard_map/ppermute | solution.py:35
  25.8 0.2 collective-permute-done.12
  26.0 1.0 %shard_map.41 = f32[128,1024]{1,0:T(8,128)} custom-call(f32[144,256]{1,0:T(8,128)S(1)} %convert_element_type.40.refs_0_, f32[144,256]{1,0:T(8,128)S(1)} %convert_element_type.42.refs_1_, f32[144,256]{1,0:T(8,128)S(1)} %convert_element_type.44.refs_2_, f32[128,256]{1,0:T(8,128)S(1)} %get-tuple-element.40.refs_3_, ...), custom_call_target="tpu_custom_call" | custom-call | tf_op jit(solution)/shard_map/pallas_call | solution.py:210
  (17 shorter events, 0.2 us)
Async XLA Ops:
  0.0 8.7 %copy-start.2 = (f32[4,2]{0,1:T(2,128)S(1)}, f32[4,2]{0,1:T(2,128)}, u32[]{:S(2)}) copy-start(f32[4,2]{0,1:T(2,128)} %param.4) | copy-start | bytes 100
  0.0 10.9 %collective-permute-start = (bf16[128,640]{1,0:T(8,128)(2,1)}, bf16[128,640]{1,0:T(8,128)(2,1)S(1)}, u32[]{:S(2)}, u32[]{:S(2)}) collective-permute-start(bf16[128,640]{1,0:T(8,128)(2,1)} %jac_ref.1), channel_id=1, source_target_pairs={{0,4},{4,8},{8,12},{12,0},{1,5},{5,9},{9,13},{13,1},{2,6},{6,10},{... | collective-permute-start | bytes 491528 | tf_op jit(solution)/shard_map/ppermute | solution.py:18
  3.0 9.3 %collective-permute-start.1 = (bf16[128,640]{1,0:T(8,128)(2,1)}, bf16[128,640]{1,0:T(8,128)(2,1)S(1)}, u32[]{:S(2)}, u32[]{:S(2)}) collective-permute-start(bf16[128,640]{1,0:T(8,128)(2,1)} %jac_ref.1), channel_id=1, source_target_pairs={{0,2},{1,3},{2,0},{3,1},{4,6},{5,7},{6,4},{7,5},{8,10},{9,11},{10,... | collective-permute-start | bytes 491528 | tf_op jit(solution)/shard_map/ppermute | solution.py:27
  4.5 7.7 %collective-permute-start.6 = (bf16[128,640]{1,0:T(8,128)(2,1)}, bf16[128,640]{1,0:T(8,128)(2,1)S(1)}, u32[]{:S(2)}, u32[]{:S(2)}) collective-permute-start(bf16[128,640]{1,0:T(8,128)(2,1)} %jac_ref.1), channel_id=1, source_target_pairs={{0,12},{1,13},{2,14},{3,15},{16,28},{17,29},{18,30},{19,31}} | collective-permute-start | bytes 491528 | tf_op jit(solution)/shard_map/ppermute | solution.py:22
  8.7 1.0 %copy-start = (bf16[128,640]{1,0:T(8,128)(2,1)S(1)}, bf16[128,640]{1,0:T(8,128)(2,1)}, u32[]{:S(2)}) copy-start(bf16[128,640]{1,0:T(8,128)(2,1)} %jac_ref.1) | copy-start | bytes 491524
  9.7 0.7 %copy-start.1 = (f32[2,640]{1,0:T(2,128)S(1)}, f32[2,640]{1,0:T(2,128)}, u32[]{:S(2)}) copy-start(f32[2,640]{1,0:T(2,128)} %prior_ref.1) | copy-start | bytes 15364
  11.0 4.5 %collective-permute-start.5 = (bf16[128,640]{1,0:T(8,128)(2,1)S(1)}, bf16[128,640]{1,0:T(8,128)(2,1)S(1)}, u32[]{:S(2)}, u32[]{:S(2)}) collective-permute-start(bf16[128,640]{1,0:T(8,128)(2,1)S(1)} %collective-permute-done.refs_2_), channel_id=1, source_target_pairs={{4,8},{8,12},{5,9},{9,13},{6,10},{10,14},{7,11},{11,15},{20,24},{2... | collective-permute-start | bytes 491528 | tf_op jit(solution)/shard_map/ppermute | solution.py:22
  11.7 1.4 %collective-permute-start.3 = (bf16[64,640]{1,0:T(8,128)(2,1)S(1)}, bf16[64,640]{1,0:T(8,128)(2,1)S(1)}, u32[]{:S(2)}, u32[]{:S(2)}) collective-permute-start(bf16[64,640]{1,0:T(8,128)(2,1)S(1)} %get-tuple-element.48), channel_id=1, source_target_pairs={{0,1},{1,0},{2,3},{3,2},{4,5},{5,4},{6,7},{7,6},{8,9},{9,8},{10,11... | collective-permute-start | bytes 245768 | tf_op jit(solution)/shard_map/ppermute | solution.py:27
  11.7 1.5 %collective-permute-start.4 = (bf16[64,640]{1,0:T(8,128)(2,1)S(1)}, bf16[64,640]{1,0:T(8,128)(2,1)S(1)}, u32[]{:S(2)}, u32[]{:S(2)}) collective-permute-start(bf16[64,640]{1,0:T(8,128)(2,1)S(1)} %get-tuple-element.47), channel_id=1, source_target_pairs={{0,1},{1,0},{2,3},{3,2},{4,5},{5,4},{6,7},{7,6},{8,9},{9,8},{10,11... | collective-permute-start | bytes 245768 | tf_op jit(solution)/shard_map/ppermute | solution.py:27
  12.2 2.2 %collective-permute-start.2 = (bf16[128,640]{1,0:T(8,128)(2,1)S(1)}, bf16[128,640]{1,0:T(8,128)(2,1)S(1)}, u32[]{:S(2)}, u32[]{:S(2)}) collective-permute-start(bf16[128,640]{1,0:T(8,128)(2,1)S(1)} %get-tuple-element.28.refs_0_), channel_id=1, source_target_pairs={{0,1},{1,0},{2,3},{3,2},{4,5},{5,4},{6,7},{7,6},{8,9},{9,8},{10,11... | collective-permute-start | bytes 491528 | tf_op jit(solution)/shard_map/ppermute | solution.py:27
  12.3 1.4 %collective-permute-start.7 = (bf16[64,640]{1,0:T(8,128)(2,1)S(1)}, bf16[64,640]{1,0:T(8,128)(2,1)S(1)}, u32[]{:S(2)}, u32[]{:S(2)}) collective-permute-start(bf16[64,640]{1,0:T(8,128)(2,1)S(1)} %get-tuple-element.45), channel_id=1, source_target_pairs={{0,1},{1,0},{2,3},{3,2},{4,5},{5,4},{6,7},{7,6},{8,9},{9,8},{10,11... | collective-permute-start | bytes 245768 | tf_op jit(solution)/shard_map/ppermute | solution.py:27
  13.1 1.3 %collective-permute-start.8 = (bf16[64,640]{1,0:T(8,128)(2,1)S(1)}, bf16[64,640]{1,0:T(8,128)(2,1)S(1)}, u32[]{:S(2)}, u32[]{:S(2)}) collective-permute-start(bf16[64,640]{1,0:T(8,128)(2,1)S(1)} %get-tuple-element.46), channel_id=1, source_target_pairs={{0,1},{1,0},{2,3},{3,2},{4,5},{5,4},{6,7},{7,6},{8,9},{9,8},{10,11... | collective-permute-start | bytes 245768 | tf_op jit(solution)/shard_map/ppermute | solution.py:27
  15.4 3.7 %collective-permute-start.9 = (bf16[128,640]{1,0:T(8,128)(2,1)S(1)}, bf16[128,640]{1,0:T(8,128)(2,1)S(1)}, u32[]{:S(2)}, u32[]{:S(2)}) collective-permute-start(bf16[128,640]{1,0:T(8,128)(2,1)S(1)} %collective-permute-done.5.refs_4_), channel_id=1, source_target_pairs={{0,1},{1,0},{2,3},{3,2},{4,5},{5,4},{6,7},{7,6},{8,9},{9,8},{10,11... | collective-permute-start | bytes 491528 | tf_op jit(solution)/shard_map/ppermute | solution.py:27
  15.7 5.6 %collective-permute-start.13 = (f16[144,256]{1,0:T(8,128)(2,1)S(1)}, f16[144,256]{1,0:T(8,128)(2,1)S(1)}, u32[]{:S(2)}, u32[]{:S(2)}) collective-permute-start(f16[144,256]{1,0:T(8,128)(2,1)S(1)} %convert_element_type.38), channel_id=1, source_target_pairs={{0,18},{1,19},{2,16},{3,17},{16,2},{17,3},{18,0},{19,1},{4,22},{5,... | collective-permute-start | bytes 221192 | tf_op jit(solution)/shard_map/ppermute | solution.py:35
  17.1 6.0 %collective-permute-start.14 = (f16[144,256]{1,0:T(8,128)(2,1)S(1)}, f16[144,256]{1,0:T(8,128)(2,1)S(1)}, u32[]{:S(2)}, u32[]{:S(2)}) collective-permute-start(f16[144,256]{1,0:T(8,128)(2,1)S(1)} %convert_element_type.36), channel_id=1, source_target_pairs={{0,2},{1,3},{2,0},{3,1},{16,18},{17,19},{18,16},{19,17},{4,6},{5,7... | collective-permute-start | bytes 221192 | tf_op jit(solution)/shard_map/ppermute | solution.py:35
  18.6 5.2 %collective-permute-start.15 = (f16[144,256]{1,0:T(8,128)(2,1)S(1)}, f16[144,256]{1,0:T(8,128)(2,1)S(1)}, u32[]{:S(2)}, u32[]{:S(2)}) collective-permute-start(f16[144,256]{1,0:T(8,128)(2,1)S(1)} %convert_element_type.37), channel_id=1, source_target_pairs={{0,16},{1,17},{2,18},{3,19},{16,0},{17,1},{18,2},{19,3},{4,20},{5,... | collective-permute-start | bytes 221192 | tf_op jit(solution)/shard_map/ppermute | solution.py:35
  19.3 6.0 %collective-permute-start.10 = (f16[144,256]{1,0:T(8,128)(2,1)S(1)}, f16[144,256]{1,0:T(8,128)(2,1)S(1)}, u32[]{:S(2)}, u32[]{:S(2)}) collective-permute-start(f16[144,256]{1,0:T(8,128)(2,1)S(1)} %convert_element_type.39), channel_id=1, source_target_pairs={{0,18},{1,19},{2,16},{3,17},{16,2},{17,3},{18,0},{19,1},{4,22},{5,... | collective-permute-start | bytes 221192 | tf_op jit(solution)/shard_map/ppermute | solution.py:35
  20.8 4.9 %collective-permute-start.11 = (f16[144,256]{1,0:T(8,128)(2,1)S(1)}, f16[144,256]{1,0:T(8,128)(2,1)S(1)}, u32[]{:S(2)}, u32[]{:S(2)}) collective-permute-start(f16[144,256]{1,0:T(8,128)(2,1)S(1)} %convert_element_type.41), channel_id=1, source_target_pairs={{0,16},{1,17},{2,18},{3,19},{16,0},{17,1},{18,2},{19,3},{4,20},{5,... | collective-permute-start | bytes 221192 | tf_op jit(solution)/shard_map/ppermute | solution.py:35
  21.3 4.7 %collective-permute-start.12 = (f16[144,256]{1,0:T(8,128)(2,1)S(1)}, f16[144,256]{1,0:T(8,128)(2,1)S(1)}, u32[]{:S(2)}, u32[]{:S(2)}) collective-permute-start(f16[144,256]{1,0:T(8,128)(2,1)S(1)} %convert_element_type.43), channel_id=1, source_target_pairs={{0,2},{1,3},{2,0},{3,1},{16,18},{17,19},{18,16},{19,17},{4,6},{5,7... | collective-permute-start | bytes 221192 | tf_op jit(solution)/shard_map/ppermute | solution.py:35

commit v8 on v7

--- a/solution.py
+++ b/solution.py
@@ -178,8 +178,9 @@
 
 
 def place_kernel(vox, levels, lines, groups, far, near, *refs):
-    perm = [7, 6, 5, 4, 3, 1, 2, 0] if len(refs) == 9 else range(len(refs) - 1)
-    blocks, out_ref = [refs[list(perm).index(k)] for k in range(len(refs) - 1)], refs[-1]
+    perm = [7, 6, 5, 4, 3, 1, 2, 0] if len(refs) == 11 else range(len(refs) - 3)
+    blocks, (out_ref, held, sems) = [refs[list(perm).index(k)] for k in range(len(refs) - 3)], refs[-3:]
+    copies = []
     tile, slots = out_ref.shape[0], levels // vox
     v, z, w = (lax.axis_index(a) for a in ("vox", "row", "wl"))
     rows = (z * lines + w) * tile + lax.broadcasted_iota(jnp.int32, (tile, tile), 0)
@@ -196,18 +197,26 @@
                         total += block[:tile, src] * scale
                     at = pl.multiple_of((slot * lines + (w ^ f ^ e)) * tile, tile)
                     cols = v * (slots * lines * tile) + at + lax.broadcasted_iota(jnp.int32, (tile, tile), 1)
-                    out_ref[:, pl.ds(at, tile)] = jnp.where(cols <= rows, total, 0.0)
+                    n = len(copies)
+                    held[n] = jnp.where(cols <= rows, total, 0.0)
+                    copies.append(pltpu.make_async_copy(held.at[n], out_ref.at[:, pl.ds(at, tile)], sems.at[n]))
+                    copies[-1].start()
+    for copy in copies:
+        copy.wait()
 
 
 def place(blocks, vox, levels, lines, groups, far, near):
     tile = blocks[0].shape[0]
-    call = kernel_call(
+    count = levels // vox * lines
+    perm = [7, 6, 5, 4, 3, 1, 2, 0] if len(blocks) == 8 else range(len(blocks))
+    return pl.pallas_call(
         functools.partial(place_kernel, vox, levels, lines, groups, far, near),
-        [VMEM] * len(blocks),
-        [jax.ShapeDtypeStruct((tile, levels // vox * lines * tile), jnp.float32)],
-    )
-    perm = [7, 6, 5, 4, 3, 1, 2, 0] if len(blocks) == 8 else range(len(blocks))
-    return call(*[blocks[k] for k in perm])[0]
+        in_specs=[VMEM] * len(blocks),
+        out_specs=pl.BlockSpec(memory_space=pl.ANY),
+        out_shape=jax.ShapeDtypeStruct((tile, count * tile), jnp.float32),
+        scratch_shapes=[pltpu.VMEM((count, tile, tile), jnp.float32), pltpu.SemaphoreType.DMA((count,))],
+        compiler_params=pltpu.CompilerParams(vmem_limit_bytes=LIMIT),
+    )(*[blocks[k] for k in perm])
 
 
 def on_device(jac, extinction, prior_var):

time: 27.2 us -> 27.1 us (level)
  no operation moved by 1% of the time
where the time goes in v8:
time: 27.1 us; the launch traced here: 26.9 us
  starting transfers between devices  18 us (66%)
  waiting for transfers between devices  4.04 us (15%)
  Pallas kernels  2.78 us (10%)
  local copies, waits for them, and re-layouts  1.69 us (6%)
    ppermute x6, starting transfers between devices, send(): return lax.ppermute(x, ('vox', 'wl'), pairs)  7.17 us
    ppermute x2, starting transfers between devices, climb(): lax.ppermute(x, 'row', [(i - by, i) for i in range(lowest, lowest + count)])  4.82 us
    ppermute x7, starting transfers between devices, swap(): return lax.ppermute(x, axis, [(i, i ^ bit) for i in range(size)])  3.03 us
    ppermute x1, starting transfers between devices, shift(): return lax.ppermute(x, axis, [(i, (i + by) % size) for i in range(size)])  3.02 us
    ppermute x6, waiting for transfers between devices, send(): return lax.ppermute(x, ('vox', 'wl'), pairs)  2.87 us
    unnamed x7, local copies, waits for them, and re-layouts  1.64 us
    ppermute x7, waiting for transfers between devices, swap(): return lax.ppermute(x, axis, [(i, i ^ bit) for i in range(size)])  1.17 us
    pallas_call x2, Pallas kernels, multiply(): return call(high, low, *flat)  1.01 us
  transfers between devices with their start and end apart: 16, of which 6 were waited for; matrix products, arithmetic and copies ran while one was open for 1% of the time, Pallas kernels for 7%

profile of v8, /device:TPU:0, one launch (start us, length us, event | category | flops | bytes accessed | tf_op | source)
XLA Modules:
  0.0 26.9 jit_solution(14977573194679235423)
XLA Ops:
  0.0 0.0 copy-start.2
  0.0 3.0 %collective-permute-start = (bf16[128,640]{1,0:T(8,128)(2,1)}, bf16[128,640]{1,0:T(8,128)(2,1)S(1)}, u32[]{:S(2)}, u32[]{:S(2)}) collective-permute-start(bf16[128,640]{1,0:T(8,128)(2,1)} %jac_ref.1), channel_id=1, source_target_pairs={{0,4},{4,8},{8,12},{12,0},{1,5},{5,9},{9,13},{13,1},{2,6},{6,10},{... | collective-permute-start | bytes 491528 | tf_op jit(solution)/shard_map/ppermute | solution.py:18
  3.0 1.5 %collective-permute-start.1 = (bf16[128,640]{1,0:T(8,128)(2,1)}, bf16[128,640]{1,0:T(8,128)(2,1)S(1)}, u32[]{:S(2)}, u32[]{:S(2)}) collective-permute-start(bf16[128,640]{1,0:T(8,128)(2,1)} %jac_ref.1), channel_id=1, source_target_pairs={{0,2},{1,3},{2,0},{3,1},{4,6},{5,7},{6,4},{7,5},{8,10},{9,11},{10,... | collective-permute-start | bytes 491528 | tf_op jit(solution)/shard_map/ppermute | solution.py:27
  4.5 4.1 %collective-permute-start.6 = (bf16[128,640]{1,0:T(8,128)(2,1)}, bf16[128,640]{1,0:T(8,128)(2,1)S(1)}, u32[]{:S(2)}, u32[]{:S(2)}) collective-permute-start(bf16[128,640]{1,0:T(8,128)(2,1)} %jac_ref.1), channel_id=1, source_target_pairs={{0,12},{1,13},{2,14},{3,15},{16,28},{17,29},{18,30},{19,31}} | collective-permute-start | bytes 491528 | tf_op jit(solution)/shard_map/ppermute | solution.py:22
  8.7 0.0 copy-done.2
  8.7 0.0 copy-start
  8.7 0.9 %copy-done = bf16[128,640]{1,0:T(8,128)(2,1)S(1)} copy-done((bf16[128,640]{1,0:T(8,128)(2,1)S(1)}, bf16[128,640]{1,0:T(8,128)(2,1)}, u32[]{:S(2)}) %copy-start) | copy-done | bytes 163864
  9.7 0.0 copy-start.1
  9.7 0.7 %copy-done.1 = f32[2,640]{1,0:T(2,128)S(1)} copy-done((f32[2,640]{1,0:T(2,128)S(1)}, f32[2,640]{1,0:T(2,128)}, u32[]{:S(2)}) %copy-start.1) | copy-done | bytes 5144
  10.4 0.6 %shard_map.37 = (f32[4,640]{1,0:T(4,128)S(1)}, bf16[128,640]{1,0:T(8,128)(2,1)S(1)}) custom-call(f32[2,4]{1,0:T(2,128)S(1)} %bitcast.1, f32[2,640]{1,0:T(2,128)S(1)} %copy-done.1, bf16[128,640]{1,0:T(8,128)(2,1)S(1)} %copy-done), custom_call_target="tpu_custom_call" | custom-call | flops 1 | bytes 8000000 | tf_op jit(solution)/shard_map/pallas_call | solution.py:97
  10.9 0.0 collective-permute-done.refs_2_
  11.0 0.7 %collective-permute-start.5 = (bf16[128,640]{1,0:T(8,128)(2,1)S(1)}, bf16[128,640]{1,0:T(8,128)(2,1)S(1)}, u32[]{:S(2)}, u32[]{:S(2)}) collective-permute-start(bf16[128,640]{1,0:T(8,128)(2,1)S(1)} %collective-permute-done.refs_2_), channel_id=1, source_target_pairs={{4,8},{8,12},{5,9},{9,13},{6,10},{10,14},{7,11},{11,15},{20,24},{2... | collective-permute-start | bytes 491528 | tf_op jit(solution)/shard_map/ppermute | solution.py:22
  11.7 0.1 collective-permute-start.3
  11.7 0.5 %collective-permute-start.4 = (bf16[64,640]{1,0:T(8,128)(2,1)S(1)}, bf16[64,640]{1,0:T(8,128)(2,1)S(1)}, u32[]{:S(2)}, u32[]{:S(2)}) collective-permute-start(bf16[64,640]{1,0:T(8,128)(2,1)S(1)} %get-tuple-element.47), channel_id=1, source_target_pairs={{0,1},{1,0},{2,3},{3,2},{4,5},{5,4},{6,7},{7,6},{8,9},{9,8},{10,11... | collective-permute-start | bytes 245768 | tf_op jit(solution)/shard_map/ppermute | solution.py:27
  12.2 0.0 collective-permute-done.6.refs_4_
  12.2 0.1 collective-permute-start.2
  12.3 0.0 collective-permute-done.1.refs_1_
  12.3 0.5 %collective-permute-start.7 = (bf16[64,640]{1,0:T(8,128)(2,1)S(1)}, bf16[64,640]{1,0:T(8,128)(2,1)S(1)}, u32[]{:S(2)}, u32[]{:S(2)}) collective-permute-start(bf16[64,640]{1,0:T(8,128)(2,1)S(1)} %get-tuple-element.45), channel_id=1, source_target_pairs={{0,1},{1,0},{2,3},{3,2},{4,5},{5,4},{6,7},{7,6},{8,9},{9,8},{10,11... | collective-permute-start | bytes 245768 | tf_op jit(solution)/shard_map/ppermute | solution.py:27
  12.8 0.3 shard_map.38
  13.1 0.0 collective-permute-done.3
  13.1 0.1 collective-permute-start.8
  13.3 0.0 collective-permute-done.4
  13.3 0.5 %collective-permute-done.7 = bf16[64,640]{1,0:T(8,128)(2,1)S(1)} collective-permute-done((bf16[64,640]{1,0:T(8,128)(2,1)S(1)}, bf16[64,640]{1,0:T(8,128)(2,1)S(1)}, u32[]{:S(2)}, u32[]{:S(2)}) %collective-permute-start.7) | collective-permute-done | bytes 81952 | tf_op jit(solution)/shard_map/ppermute | solution.py:27
  13.8 0.7 %collective-permute-done.8 = bf16[64,640]{1,0:T(8,128)(2,1)S(1)} collective-permute-done((bf16[64,640]{1,0:T(8,128)(2,1)S(1)}, bf16[64,640]{1,0:T(8,128)(2,1)S(1)}, u32[]{:S(2)}, u32[]{:S(2)}) %collective-permute-start.8) | collective-permute-done | bytes 81952 | tf_op jit(solution)/shard_map/ppermute | solution.py:27
  14.5 0.0 collective-permute-done.2.refs_1_
  14.5 0.9 %shard_map.39 = (f32[128,256]{1,0:T(8,128)S(1)}, f32[144,256]{1,0:T(8,128)S(1)}, f32[144,256]{1,0:T(8,128)S(1)}, f32[144,256]{1,0:T(8,128)S(1)}) custom-call(bf16[2,256,640]{2,1,0:T(8,128)(2,1)S(1)} %get-tuple-element.29.high_ref, bf16[2,256,640]{2,1,0:T(8,128)(2,1)S(1)} %get-tuple-element.30.low_ref, bf16[128,640]{1,0:T(8,128)(2,1)S(1)} %get-tuple-element.28.refs_0_, ...), custom_call_target="tpu_custom_call" | custom-call | tf_op jit(solution)/shard_map/pallas_call | solution.py:177
  15.4 0.0 collective-permute-done.5.refs_4_
  15.4 0.2 collective-permute-start.9
  15.7 1.4 %collective-permute-start.13 = (f16[144,256]{1,0:T(8,128)(2,1)S(1)}, f16[144,256]{1,0:T(8,128)(2,1)S(1)}, u32[]{:S(2)}, u32[]{:S(2)}) collective-permute-start(f16[144,256]{1,0:T(8,128)(2,1)S(1)} %convert_element_type.38), channel_id=1, source_target_pairs={{0,18},{1,19},{2,16},{3,17},{16,2},{17,3},{18,0},{19,1},{4,22},{5,... | collective-permute-start | bytes 221192 | tf_op jit(solution)/shard_map/ppermute | solution.py:35
  17.1 1.5 %collective-permute-start.14 = (f16[144,256]{1,0:T(8,128)(2,1)S(1)}, f16[144,256]{1,0:T(8,128)(2,1)S(1)}, u32[]{:S(2)}, u32[]{:S(2)}) collective-permute-start(f16[144,256]{1,0:T(8,128)(2,1)S(1)} %convert_element_type.36), channel_id=1, source_target_pairs={{0,2},{1,3},{2,0},{3,1},{16,18},{17,19},{18,16},{19,17},{4,6},{5,7... | collective-permute-start | bytes 221192 | tf_op jit(solution)/shard_map/ppermute | solution.py:35
  18.6 0.5 %collective-permute-start.15 = (f16[144,256]{1,0:T(8,128)(2,1)S(1)}, f16[144,256]{1,0:T(8,128)(2,1)S(1)}, u32[]{:S(2)}, u32[]{:S(2)}) collective-permute-start(f16[144,256]{1,0:T(8,128)(2,1)S(1)} %convert_element_type.37), channel_id=1, source_target_pairs={{0,16},{1,17},{2,18},{3,19},{16,0},{17,1},{18,2},{19,3},{4,20},{5,... | collective-permute-start | bytes 221192 | tf_op jit(solution)/shard_map/ppermute | solution.py:35
  19.2 0.0 collective-permute-done.9.refs_5_
  19.2 0.1 shard_map.40
  19.3 1.5 %collective-permute-start.10 = (f16[144,256]{1,0:T(8,128)(2,1)S(1)}, f16[144,256]{1,0:T(8,128)(2,1)S(1)}, u32[]{:S(2)}, u32[]{:S(2)}) collective-permute-start(f16[144,256]{1,0:T(8,128)(2,1)S(1)} %convert_element_type.39), channel_id=1, source_target_pairs={{0,18},{1,19},{2,16},{3,17},{16,2},{17,3},{18,0},{19,1},{4,22},{5,... | collective-permute-start | bytes 221192 | tf_op jit(solution)/shard_map/ppermute | solution.py:35
  20.8 0.4 %collective-permute-start.11 = (f16[144,256]{1,0:T(8,128)(2,1)S(1)}, f16[144,256]{1,0:T(8,128)(2,1)S(1)}, u32[]{:S(2)}, u32[]{:S(2)}) collective-permute-start(f16[144,256]{1,0:T(8,128)(2,1)S(1)} %convert_element_type.41), channel_id=1, source_target_pairs={{0,16},{1,17},{2,18},{3,19},{16,0},{17,1},{18,2},{19,3},{4,20},{5,... | collective-permute-start | bytes 221192 | tf_op jit(solution)/shard_map/ppermute | solution.py:35
  21.3 0.0 collective-permute-done.13
  21.3 1.7 %collective-permute-start.12 = (f16[144,256]{1,0:T(8,128)(2,1)S(1)}, f16[144,256]{1,0:T(8,128)(2,1)S(1)}, u32[]{:S(2)}, u32[]{:S(2)}) collective-permute-start(f16[144,256]{1,0:T(8,128)(2,1)S(1)} %convert_element_type.43), channel_id=1, source_target_pairs={{0,2},{1,3},{2,0},{3,1},{16,18},{17,19},{18,16},{19,17},{4,6},{5,7... | collective-permute-start | bytes 221192 | tf_op jit(solution)/shard_map/ppermute | solution.py:35
  23.0 0.0 collective-permute-done.14
  23.1 0.7 %collective-permute-done.15 = f16[144,256]{1,0:T(8,128)(2,1)S(1)} collective-permute-done((f16[144,256]{1,0:T(8,128)(2,1)S(1)}, f16[144,256]{1,0:T(8,128)(2,1)S(1)}, u32[]{:S(2)}, u32[]{:S(2)}) %collective-permute-start.15) | collective-permute-done | bytes 73760 | tf_op jit(solution)/shard_map/ppermute | solution.py:35
  23.8 1.5 %collective-permute-done.10 = f16[144,256]{1,0:T(8,128)(2,1)S(1)} collective-permute-done((f16[144,256]{1,0:T(8,128)(2,1)S(1)}, f16[144,256]{1,0:T(8,128)(2,1)S(1)}, u32[]{:S(2)}, u32[]{:S(2)}) %collective-permute-start.10) | collective-permute-done | bytes 73760 | tf_op jit(solution)/shard_map/ppermute | solution.py:35
  25.3 0.4 %collective-permute-done.11 = f16[144,256]{1,0:T(8,128)(2,1)S(1)} collective-permute-done((f16[144,256]{1,0:T(8,128)(2,1)S(1)}, f16[144,256]{1,0:T(8,128)(2,1)S(1)}, u32[]{:S(2)}, u32[]{:S(2)}) %collective-permute-start.11) | collective-permute-done | bytes 73760 | tf_op jit(solution)/shard_map/ppermute | solution.py:35
  25.8 0.2 collective-permute-done.12
  26.0 0.9 %shard_map.41 = f32[128,1024]{1,0:T(8,128)} custom-call(f32[144,256]{1,0:T(8,128)S(1)} %convert_element_type.40.refs_0_, f32[144,256]{1,0:T(8,128)S(1)} %convert_element_type.42.refs_1_, f32[144,256]{1,0:T(8,128)S(1)} %convert_element_type.44.refs_2_, f32[128,256]{1,0:T(8,128)S(1)} %get-tuple-element.40.refs_3_, ...), custom_call_target="tpu_custom_call" | custom-call | tf_op jit(solution)/shard_map/pallas_call | solution.py:212
  (17 shorter events, 0.2 us)
Async XLA Ops:
  0.0 8.7 %copy-start.2 = (f32[4,2]{0,1:T(2,128)S(1)}, f32[4,2]{0,1:T(2,128)}, u32[]{:S(2)}) copy-start(f32[4,2]{0,1:T(2,128)} %param.4) | copy-start | bytes 100
  0.0 10.9 %collective-permute-start = (bf16[128,640]{1,0:T(8,128)(2,1)}, bf16[128,640]{1,0:T(8,128)(2,1)S(1)}, u32[]{:S(2)}, u32[]{:S(2)}) collective-permute-start(bf16[128,640]{1,0:T(8,128)(2,1)} %jac_ref.1), channel_id=1, source_target_pairs={{0,4},{4,8},{8,12},{12,0},{1,5},{5,9},{9,13},{13,1},{2,6},{6,10},{... | collective-permute-start | bytes 491528 | tf_op jit(solution)/shard_map/ppermute | solution.py:18
  3.0 9.3 %collective-permute-start.1 = (bf16[128,640]{1,0:T(8,128)(2,1)}, bf16[128,640]{1,0:T(8,128)(2,1)S(1)}, u32[]{:S(2)}, u32[]{:S(2)}) collective-permute-start(bf16[128,640]{1,0:T(8,128)(2,1)} %jac_ref.1), channel_id=1, source_target_pairs={{0,2},{1,3},{2,0},{3,1},{4,6},{5,7},{6,4},{7,5},{8,10},{9,11},{10,... | collective-permute-start | bytes 491528 | tf_op jit(solution)/shard_map/ppermute | solution.py:27
  4.5 7.7 %collective-permute-start.6 = (bf16[128,640]{1,0:T(8,128)(2,1)}, bf16[128,640]{1,0:T(8,128)(2,1)S(1)}, u32[]{:S(2)}, u32[]{:S(2)}) collective-permute-start(bf16[128,640]{1,0:T(8,128)(2,1)} %jac_ref.1), channel_id=1, source_target_pairs={{0,12},{1,13},{2,14},{3,15},{16,28},{17,29},{18,30},{19,31}} | collective-permute-start | bytes 491528 | tf_op jit(solution)/shard_map/ppermute | solution.py:22
  8.7 1.0 %copy-start = (bf16[128,640]{1,0:T(8,128)(2,1)S(1)}, bf16[128,640]{1,0:T(8,128)(2,1)}, u32[]{:S(2)}) copy-start(bf16[128,640]{1,0:T(8,128)(2,1)} %jac_ref.1) | copy-start | bytes 491524
  9.7 0.7 %copy-start.1 = (f32[2,640]{1,0:T(2,128)S(1)}, f32[2,640]{1,0:T(2,128)}, u32[]{:S(2)}) copy-start(f32[2,640]{1,0:T(2,128)} %prior_ref.1) | copy-start | bytes 15364
  11.0 4.5 %collective-permute-start.5 = (bf16[128,640]{1,0:T(8,128)(2,1)S(1)}, bf16[128,640]{1,0:T(8,128)(2,1)S(1)}, u32[]{:S(2)}, u32[]{:S(2)}) collective-permute-start(bf16[128,640]{1,0:T(8,128)(2,1)S(1)} %collective-permute-done.refs_2_), channel_id=1, source_target_pairs={{4,8},{8,12},{5,9},{9,13},{6,10},{10,14},{7,11},{11,15},{20,24},{2... | collective-permute-start | bytes 491528 | tf_op jit(solution)/shard_map/ppermute | solution.py:22
  11.7 1.4 %collective-permute-start.3 = (bf16[64,640]{1,0:T(8,128)(2,1)S(1)}, bf16[64,640]{1,0:T(8,128)(2,1)S(1)}, u32[]{:S(2)}, u32[]{:S(2)}) collective-permute-start(bf16[64,640]{1,0:T(8,128)(2,1)S(1)} %get-tuple-element.48), channel_id=1, source_target_pairs={{0,1},{1,0},{2,3},{3,2},{4,5},{5,4},{6,7},{7,6},{8,9},{9,8},{10,11... | collective-permute-start | bytes 245768 | tf_op jit(solution)/shard_map/ppermute | solution.py:27
  11.7 1.5 %collective-permute-start.4 = (bf16[64,640]{1,0:T(8,128)(2,1)S(1)}, bf16[64,640]{1,0:T(8,128)(2,1)S(1)}, u32[]{:S(2)}, u32[]{:S(2)}) collective-permute-start(bf16[64,640]{1,0:T(8,128)(2,1)S(1)} %get-tuple-element.47), channel_id=1, source_target_pairs={{0,1},{1,0},{2,3},{3,2},{4,5},{5,4},{6,7},{7,6},{8,9},{9,8},{10,11... | collective-permute-start | bytes 245768 | tf_op jit(solution)/shard_map/ppermute | solution.py:27
  12.2 2.2 %collective-permute-start.2 = (bf16[128,640]{1,0:T(8,128)(2,1)S(1)}, bf16[128,640]{1,0:T(8,128)(2,1)S(1)}, u32[]{:S(2)}, u32[]{:S(2)}) collective-permute-start(bf16[128,640]{1,0:T(8,128)(2,1)S(1)} %get-tuple-element.28.refs_0_), channel_id=1, source_target_pairs={{0,1},{1,0},{2,3},{3,2},{4,5},{5,4},{6,7},{7,6},{8,9},{9,8},{10,11... | collective-permute-start | bytes 491528 | tf_op jit(solution)/shard_map/ppermute | solution.py:27
  12.3 1.4 %collective-permute-start.7 = (bf16[64,640]{1,0:T(8,128)(2,1)S(1)}, bf16[64,640]{1,0:T(8,128)(2,1)S(1)}, u32[]{:S(2)}, u32[]{:S(2)}) collective-permute-start(bf16[64,640]{1,0:T(8,128)(2,1)S(1)} %get-tuple-element.45), channel_id=1, source_target_pairs={{0,1},{1,0},{2,3},{3,2},{4,5},{5,4},{6,7},{7,6},{8,9},{9,8},{10,11... | collective-permute-start | bytes 245768 | tf_op jit(solution)/shard_map/ppermute | solution.py:27
  13.1 1.3 %collective-permute-start.8 = (bf16[64,640]{1,0:T(8,128)(2,1)S(1)}, bf16[64,640]{1,0:T(8,128)(2,1)S(1)}, u32[]{:S(2)}, u32[]{:S(2)}) collective-permute-start(bf16[64,640]{1,0:T(8,128)(2,1)S(1)} %get-tuple-element.46), channel_id=1, source_target_pairs={{0,1},{1,0},{2,3},{3,2},{4,5},{5,4},{6,7},{7,6},{8,9},{9,8},{10,11... | collective-permute-start | bytes 245768 | tf_op jit(solution)/shard_map/ppermute | solution.py:27
  15.4 3.7 %collective-permute-start.9 = (bf16[128,640]{1,0:T(8,128)(2,1)S(1)}, bf16[128,640]{1,0:T(8,128)(2,1)S(1)}, u32[]{:S(2)}, u32[]{:S(2)}) collective-permute-start(bf16[128,640]{1,0:T(8,128)(2,1)S(1)} %collective-permute-done.5.refs_4_), channel_id=1, source_target_pairs={{0,1},{1,0},{2,3},{3,2},{4,5},{5,4},{6,7},{7,6},{8,9},{9,8},{10,11... | collective-permute-start | bytes 491528 | tf_op jit(solution)/shard_map/ppermute | solution.py:27
  15.7 5.6 %collective-permute-start.13 = (f16[144,256]{1,0:T(8,128)(2,1)S(1)}, f16[144,256]{1,0:T(8,128)(2,1)S(1)}, u32[]{:S(2)}, u32[]{:S(2)}) collective-permute-start(f16[144,256]{1,0:T(8,128)(2,1)S(1)} %convert_element_type.38), channel_id=1, source_target_pairs={{0,18},{1,19},{2,16},{3,17},{16,2},{17,3},{18,0},{19,1},{4,22},{5,... | collective-permute-start | bytes 221192 | tf_op jit(solution)/shard_map/ppermute | solution.py:35
  17.1 6.0 %collective-permute-start.14 = (f16[144,256]{1,0:T(8,128)(2,1)S(1)}, f16[144,256]{1,0:T(8,128)(2,1)S(1)}, u32[]{:S(2)}, u32[]{:S(2)}) collective-permute-start(f16[144,256]{1,0:T(8,128)(2,1)S(1)} %convert_element_type.36), channel_id=1, source_target_pairs={{0,2},{1,3},{2,0},{3,1},{16,18},{17,19},{18,16},{19,17},{4,6},{5,7... | collective-permute-start | bytes 221192 | tf_op jit(solution)/shard_map/ppermute | solution.py:35
  18.6 5.2 %collective-permute-start.15 = (f16[144,256]{1,0:T(8,128)(2,1)S(1)}, f16[144,256]{1,0:T(8,128)(2,1)S(1)}, u32[]{:S(2)}, u32[]{:S(2)}) collective-permute-start(f16[144,256]{1,0:T(8,128)(2,1)S(1)} %convert_element_type.37), channel_id=1, source_target_pairs={{0,16},{1,17},{2,18},{3,19},{16,0},{17,1},{18,2},{19,3},{4,20},{5,... | collective-permute-start | bytes 221192 | tf_op jit(solution)/shard_map/ppermute | solution.py:35
  19.3 6.0 %collective-permute-start.10 = (f16[144,256]{1,0:T(8,128)(2,1)S(1)}, f16[144,256]{1,0:T(8,128)(2,1)S(1)}, u32[]{:S(2)}, u32[]{:S(2)}) collective-permute-start(f16[144,256]{1,0:T(8,128)(2,1)S(1)} %convert_element_type.39), channel_id=1, source_target_pairs={{0,18},{1,19},{2,16},{3,17},{16,2},{17,3},{18,0},{19,1},{4,22},{5,... | collective-permute-start | bytes 221192 | tf_op jit(solution)/shard_map/ppermute | solution.py:35
  20.8 4.9 %collective-permute-start.11 = (f16[144,256]{1,0:T(8,128)(2,1)S(1)}, f16[144,256]{1,0:T(8,128)(2,1)S(1)}, u32[]{:S(2)}, u32[]{:S(2)}) collective-permute-start(f16[144,256]{1,0:T(8,128)(2,1)S(1)} %convert_element_type.41), channel_id=1, source_target_pairs={{0,16},{1,17},{2,18},{3,19},{16,0},{17,1},{18,2},{19,3},{4,20},{5,... | collective-permute-start | bytes 221192 | tf_op jit(solution)/shard_map/ppermute | solution.py:35
  21.3 4.7 %collective-permute-start.12 = (f16[144,256]{1,0:T(8,128)(2,1)S(1)}, f16[144,256]{1,0:T(8,128)(2,1)S(1)}, u32[]{:S(2)}, u32[]{:S(2)}) collective-permute-start(f16[144,256]{1,0:T(8,128)(2,1)S(1)} %convert_element_type.43), channel_id=1, source_target_pairs={{0,2},{1,3},{2,0},{3,1},{16,18},{17,19},{18,16},{19,17},{4,6},{5,7... | collective-permute-start | bytes 221192 | tf_op jit(solution)/shard_map/ppermute | solution.py:35

commit v9 on v7

--- a/solution.py
+++ b/solution.py
@@ -93,7 +93,7 @@
 def prepare(extinction, prior, jac, far, near):
     weights = jax.ShapeDtypeStruct((len(far) * len(near), jac.shape[1]), jnp.float32)
     own = jax.ShapeDtypeStruct(jac.shape, jac.dtype)
-    call = kernel_call(functools.partial(prepare_kernel, far, near), [SMEM, VMEM, VMEM], [weights, own], cost=pl.CostEstimate(flops=1, bytes_accessed=8000000, transcendentals=0))
+    call = kernel_call(functools.partial(prepare_kernel, far, near), [SMEM, VMEM, VMEM], [weights, own])
     return call(extinction, prior, jac)
 
 
@@ -112,7 +112,7 @@
 def weigh(weights, rows, far, near):
     tile, depth = rows[0].shape
     like = jax.ShapeDtypeStruct((len(near), len(far) * tile, depth), jnp.bfloat16)
-    call = kernel_call(functools.partial(weigh_kernel, far, near), [VMEM] * (1 + len(rows)), [like, like], cost=pl.CostEstimate(flops=1, bytes_accessed=1, transcendentals=0))
+    call = kernel_call(functools.partial(weigh_kernel, far, near), [VMEM] * (1 + len(rows)), [like, like])
     return call(weights, *rows)
 
 
@@ -172,7 +172,6 @@
         [VMEM] * (2 + len(flat)),
         [jax.ShapeDtypeStruct((height, width), jnp.float32) for height in heights],
         [pltpu.VMEM((len(near), vox * len(phases) * tile, depth), jnp.bfloat16)],
-        None if phases[0] == 0 else None,
     )
     return call(high, low, *flat)
 

time: 27.2 us -> 27.2 us (level)
  no operation moved by 1% of the time
where the time goes in v9:
time: 27.2 us; the launch traced here: 27 us
  starting transfers between devices  18 us (66%)
  waiting for transfers between devices  4.04 us (15%)
  Pallas kernels  2.82 us (10%)
  local copies, waits for them, and re-layouts  1.69 us (6%)
    ppermute x6, starting transfers between devices, send(): return lax.ppermute(x, ('vox', 'wl'), pairs)  7.17 us
    ppermute x2, starting transfers between devices, climb(): lax.ppermute(x, 'row', [(i - by, i) for i in range(lowest, lowest + count)])  4.82 us
    ppermute x7, starting transfers between devices, swap(): return lax.ppermute(x, axis, [(i, i ^ bit) for i in range(size)])  3.03 us
    ppermute x1, starting transfers between devices, shift(): return lax.ppermute(x, axis, [(i, (i + by) % size) for i in range(size)])  3.02 us
    ppermute x6, waiting for transfers between devices, send(): return lax.ppermute(x, ('vox', 'wl'), pairs)  2.87 us
    unnamed x7, local copies, waits for them, and re-layouts  1.64 us
    ppermute x7, waiting for transfers between devices, swap(): return lax.ppermute(x, axis, [(i, i ^ bit) for i in range(size)])  1.17 us
    pallas_call x2, Pallas kernels, multiply(): return call(high, low, *flat)  1.01 us
  transfers between devices with their start and end apart: 16, of which 6 were waited for; matrix products, arithmetic and copies ran while one was open for 1% of the time, Pallas kernels for 7%

profile of v9, /device:TPU:0, one launch (start us, length us, event | category | flops | bytes accessed | tf_op | source)
XLA Modules:
  0.0 27.0 jit_solution(14764133427887128344)
XLA Ops:
  0.0 0.0 copy-start.2
  0.0 3.0 %collective-permute-start = (bf16[128,640]{1,0:T(8,128)(2,1)}, bf16[128,640]{1,0:T(8,128)(2,1)S(1)}, u32[]{:S(2)}, u32[]{:S(2)}) collective-permute-start(bf16[128,640]{1,0:T(8,128)(2,1)} %jac_ref.1), channel_id=1, source_target_pairs={{0,4},{4,8},{8,12},{12,0},{1,5},{5,9},{9,13},{13,1},{2,6},{6,10},{... | collective-permute-start | bytes 491528 | tf_op jit(solution)/shard_map/ppermute | solution.py:18
  3.0 1.5 %collective-permute-start.1 = (bf16[128,640]{1,0:T(8,128)(2,1)}, bf16[128,640]{1,0:T(8,128)(2,1)S(1)}, u32[]{:S(2)}, u32[]{:S(2)}) collective-permute-start(bf16[128,640]{1,0:T(8,128)(2,1)} %jac_ref.1), channel_id=1, source_target_pairs={{0,2},{1,3},{2,0},{3,1},{4,6},{5,7},{6,4},{7,5},{8,10},{9,11},{10,... | collective-permute-start | bytes 491528 | tf_op jit(solution)/shard_map/ppermute | solution.py:27
  4.5 4.1 %collective-permute-start.6 = (bf16[128,640]{1,0:T(8,128)(2,1)}, bf16[128,640]{1,0:T(8,128)(2,1)S(1)}, u32[]{:S(2)}, u32[]{:S(2)}) collective-permute-start(bf16[128,640]{1,0:T(8,128)(2,1)} %jac_ref.1), channel_id=1, source_target_pairs={{0,12},{1,13},{2,14},{3,15},{16,28},{17,29},{18,30},{19,31}} | collective-permute-start | bytes 491528 | tf_op jit(solution)/shard_map/ppermute | solution.py:22
  8.7 0.0 copy-done.2
  8.7 0.0 copy-start
  8.7 0.9 %copy-done = bf16[128,640]{1,0:T(8,128)(2,1)S(1)} copy-done((bf16[128,640]{1,0:T(8,128)(2,1)S(1)}, bf16[128,640]{1,0:T(8,128)(2,1)}, u32[]{:S(2)}) %copy-start) | copy-done | bytes 163864
  9.7 0.0 copy-start.1
  9.7 0.7 %copy-done.1 = f32[2,640]{1,0:T(2,128)S(1)} copy-done((f32[2,640]{1,0:T(2,128)S(1)}, f32[2,640]{1,0:T(2,128)}, u32[]{:S(2)}) %copy-start.1) | copy-done | bytes 5144
  10.4 0.6 %shard_map.37 = (f32[4,640]{1,0:T(4,128)S(1)}, bf16[128,640]{1,0:T(8,128)(2,1)S(1)}) custom-call(f32[2,4]{1,0:T(2,128)S(1)} %bitcast.1, f32[2,640]{1,0:T(2,128)S(1)} %copy-done.1, bf16[128,640]{1,0:T(8,128)(2,1)S(1)} %copy-done), custom_call_target="tpu_custom_call" | custom-call | tf_op jit(solution)/shard_map/pallas_call | solution.py:97
  10.9 0.0 collective-permute-done.refs_2_
  11.0 0.7 %collective-permute-start.5 = (bf16[128,640]{1,0:T(8,128)(2,1)S(1)}, bf16[128,640]{1,0:T(8,128)(2,1)S(1)}, u32[]{:S(2)}, u32[]{:S(2)}) collective-permute-start(bf16[128,640]{1,0:T(8,128)(2,1)S(1)} %collective-permute-done.refs_2_), channel_id=1, source_target_pairs={{4,8},{8,12},{5,9},{9,13},{6,10},{10,14},{7,11},{11,15},{20,24},{2... | collective-permute-start | bytes 491528 | tf_op jit(solution)/shard_map/ppermute | solution.py:22
  11.7 0.1 collective-permute-start.3
  11.7 0.5 %collective-permute-start.4 = (bf16[64,640]{1,0:T(8,128)(2,1)S(1)}, bf16[64,640]{1,0:T(8,128)(2,1)S(1)}, u32[]{:S(2)}, u32[]{:S(2)}) collective-permute-start(bf16[64,640]{1,0:T(8,128)(2,1)S(1)} %get-tuple-element.47), channel_id=1, source_target_pairs={{0,1},{1,0},{2,3},{3,2},{4,5},{5,4},{6,7},{7,6},{8,9},{9,8},{10,11... | collective-permute-start | bytes 245768 | tf_op jit(solution)/shard_map/ppermute | solution.py:27
  12.2 0.0 collective-permute-done.6.refs_4_
  12.2 0.1 collective-permute-start.2
  12.3 0.0 collective-permute-done.1.refs_1_
  12.3 0.5 %collective-permute-start.7 = (bf16[64,640]{1,0:T(8,128)(2,1)S(1)}, bf16[64,640]{1,0:T(8,128)(2,1)S(1)}, u32[]{:S(2)}, u32[]{:S(2)}) collective-permute-start(bf16[64,640]{1,0:T(8,128)(2,1)S(1)} %get-tuple-element.45), channel_id=1, source_target_pairs={{0,1},{1,0},{2,3},{3,2},{4,5},{5,4},{6,7},{7,6},{8,9},{9,8},{10,11... | collective-permute-start | bytes 245768 | tf_op jit(solution)/shard_map/ppermute | solution.py:27
  12.8 0.3 shard_map.38
  13.1 0.0 collective-permute-done.3
  13.1 0.1 collective-permute-start.8
  13.3 0.0 collective-permute-done.4
  13.3 0.5 %collective-permute-done.7 = bf16[64,640]{1,0:T(8,128)(2,1)S(1)} collective-permute-done((bf16[64,640]{1,0:T(8,128)(2,1)S(1)}, bf16[64,640]{1,0:T(8,128)(2,1)S(1)}, u32[]{:S(2)}, u32[]{:S(2)}) %collective-permute-start.7) | collective-permute-done | bytes 81952 | tf_op jit(solution)/shard_map/ppermute | solution.py:27
  13.8 0.7 %collective-permute-done.8 = bf16[64,640]{1,0:T(8,128)(2,1)S(1)} collective-permute-done((bf16[64,640]{1,0:T(8,128)(2,1)S(1)}, bf16[64,640]{1,0:T(8,128)(2,1)S(1)}, u32[]{:S(2)}, u32[]{:S(2)}) %collective-permute-start.8) | collective-permute-done | bytes 81952 | tf_op jit(solution)/shard_map/ppermute | solution.py:27
  14.5 0.0 collective-permute-done.2.refs_1_
  14.5 0.9 %shard_map.39 = (f32[128,256]{1,0:T(8,128)S(1)}, f32[144,256]{1,0:T(8,128)S(1)}, f32[144,256]{1,0:T(8,128)S(1)}, f32[144,256]{1,0:T(8,128)S(1)}) custom-call(bf16[2,256,640]{2,1,0:T(8,128)(2,1)S(1)} %get-tuple-element.29.high_ref, bf16[2,256,640]{2,1,0:T(8,128)(2,1)S(1)} %get-tuple-element.30.low_ref, bf16[128,640]{1,0:T(8,128)(2,1)S(1)} %get-tuple-element.28.refs_0_, ...), custom_call_target="tpu_custom_call" | custom-call | tf_op jit(solution)/shard_map/pallas_call | solution.py:176
  15.4 0.0 collective-permute-done.5.refs_4_
  15.4 0.2 collective-permute-start.9
  15.7 1.4 %collective-permute-start.13 = (f16[144,256]{1,0:T(8,128)(2,1)S(1)}, f16[144,256]{1,0:T(8,128)(2,1)S(1)}, u32[]{:S(2)}, u32[]{:S(2)}) collective-permute-start(f16[144,256]{1,0:T(8,128)(2,1)S(1)} %convert_element_type.38), channel_id=1, source_target_pairs={{0,18},{1,19},{2,16},{3,17},{16,2},{17,3},{18,0},{19,1},{4,22},{5,... | collective-permute-start | bytes 221192 | tf_op jit(solution)/shard_map/ppermute | solution.py:35
  17.1 1.5 %collective-permute-start.14 = (f16[144,256]{1,0:T(8,128)(2,1)S(1)}, f16[144,256]{1,0:T(8,128)(2,1)S(1)}, u32[]{:S(2)}, u32[]{:S(2)}) collective-permute-start(f16[144,256]{1,0:T(8,128)(2,1)S(1)} %convert_element_type.36), channel_id=1, source_target_pairs={{0,2},{1,3},{2,0},{3,1},{16,18},{17,19},{18,16},{19,17},{4,6},{5,7... | collective-permute-start | bytes 221192 | tf_op jit(solution)/shard_map/ppermute | solution.py:35
  18.6 0.5 %collective-permute-start.15 = (f16[144,256]{1,0:T(8,128)(2,1)S(1)}, f16[144,256]{1,0:T(8,128)(2,1)S(1)}, u32[]{:S(2)}, u32[]{:S(2)}) collective-permute-start(f16[144,256]{1,0:T(8,128)(2,1)S(1)} %convert_element_type.37), channel_id=1, source_target_pairs={{0,16},{1,17},{2,18},{3,19},{16,0},{17,1},{18,2},{19,3},{4,20},{5,... | collective-permute-start | bytes 221192 | tf_op jit(solution)/shard_map/ppermute | solution.py:35
  19.2 0.0 collective-permute-done.9.refs_5_
  19.2 0.1 shard_map.40
  19.3 1.5 %collective-permute-start.10 = (f16[144,256]{1,0:T(8,128)(2,1)S(1)}, f16[144,256]{1,0:T(8,128)(2,1)S(1)}, u32[]{:S(2)}, u32[]{:S(2)}) collective-permute-start(f16[144,256]{1,0:T(8,128)(2,1)S(1)} %convert_element_type.39), channel_id=1, source_target_pairs={{0,18},{1,19},{2,16},{3,17},{16,2},{17,3},{18,0},{19,1},{4,22},{5,... | collective-permute-start | bytes 221192 | tf_op jit(solution)/shard_map/ppermute | solution.py:35
  20.8 0.4 %collective-permute-start.11 = (f16[144,256]{1,0:T(8,128)(2,1)S(1)}, f16[144,256]{1,0:T(8,128)(2,1)S(1)}, u32[]{:S(2)}, u32[]{:S(2)}) collective-permute-start(f16[144,256]{1,0:T(8,128)(2,1)S(1)} %convert_element_type.41), channel_id=1, source_target_pairs={{0,16},{1,17},{2,18},{3,19},{16,0},{17,1},{18,2},{19,3},{4,20},{5,... | collective-permute-start | bytes 221192 | tf_op jit(solution)/shard_map/ppermute | solution.py:35
  21.3 0.0 collective-permute-done.13
  21.3 1.7 %collective-permute-start.12 = (f16[144,256]{1,0:T(8,128)(2,1)S(1)}, f16[144,256]{1,0:T(8,128)(2,1)S(1)}, u32[]{:S(2)}, u32[]{:S(2)}) collective-permute-start(f16[144,256]{1,0:T(8,128)(2,1)S(1)} %convert_element_type.43), channel_id=1, source_target_pairs={{0,2},{1,3},{2,0},{3,1},{16,18},{17,19},{18,16},{19,17},{4,6},{5,7... | collective-permute-start | bytes 221192 | tf_op jit(solution)/shard_map/ppermute | solution.py:35
  23.0 0.0 collective-permute-done.14
  23.1 0.7 %collective-permute-done.15 = f16[144,256]{1,0:T(8,128)(2,1)S(1)} collective-permute-done((f16[144,256]{1,0:T(8,128)(2,1)S(1)}, f16[144,256]{1,0:T(8,128)(2,1)S(1)}, u32[]{:S(2)}, u32[]{:S(2)}) %collective-permute-start.15) | collective-permute-done | bytes 73760 | tf_op jit(solution)/shard_map/ppermute | solution.py:35
  23.8 1.5 %collective-permute-done.10 = f16[144,256]{1,0:T(8,128)(2,1)S(1)} collective-permute-done((f16[144,256]{1,0:T(8,128)(2,1)S(1)}, f16[144,256]{1,0:T(8,128)(2,1)S(1)}, u32[]{:S(2)}, u32[]{:S(2)}) %collective-permute-start.10) | collective-permute-done | bytes 73760 | tf_op jit(solution)/shard_map/ppermute | solution.py:35
  25.3 0.4 %collective-permute-done.11 = f16[144,256]{1,0:T(8,128)(2,1)S(1)} collective-permute-done((f16[144,256]{1,0:T(8,128)(2,1)S(1)}, f16[144,256]{1,0:T(8,128)(2,1)S(1)}, u32[]{:S(2)}, u32[]{:S(2)}) %collective-permute-start.11) | collective-permute-done | bytes 73760 | tf_op jit(solution)/shard_map/ppermute | solution.py:35
  25.8 0.2 collective-permute-done.12
  26.0 1.0 %shard_map.41 = f32[128,1024]{1,0:T(8,128)} custom-call(f32[144,256]{1,0:T(8,128)S(1)} %convert_element_type.40.refs_0_, f32[144,256]{1,0:T(8,128)S(1)} %convert_element_type.42.refs_1_, f32[144,256]{1,0:T(8,128)S(1)} %convert_element_type.44.refs_2_, f32[128,256]{1,0:T(8,128)S(1)} %get-tuple-element.40.refs_3_, ...), custom_call_target="tpu_custom_call" | custom-call | tf_op jit(solution)/shard_map/pallas_call | solution.py:209
  (17 shorter events, 0.2 us)
Async XLA Ops:
  0.0 8.7 %copy-start.2 = (f32[4,2]{0,1:T(2,128)S(1)}, f32[4,2]{0,1:T(2,128)}, u32[]{:S(2)}) copy-start(f32[4,2]{0,1:T(2,128)} %param.4) | copy-start | bytes 100
  0.0 10.9 %collective-permute-start = (bf16[128,640]{1,0:T(8,128)(2,1)}, bf16[128,640]{1,0:T(8,128)(2,1)S(1)}, u32[]{:S(2)}, u32[]{:S(2)}) collective-permute-start(bf16[128,640]{1,0:T(8,128)(2,1)} %jac_ref.1), channel_id=1, source_target_pairs={{0,4},{4,8},{8,12},{12,0},{1,5},{5,9},{9,13},{13,1},{2,6},{6,10},{... | collective-permute-start | bytes 491528 | tf_op jit(solution)/shard_map/ppermute | solution.py:18
  3.0 9.3 %collective-permute-start.1 = (bf16[128,640]{1,0:T(8,128)(2,1)}, bf16[128,640]{1,0:T(8,128)(2,1)S(1)}, u32[]{:S(2)}, u32[]{:S(2)}) collective-permute-start(bf16[128,640]{1,0:T(8,128)(2,1)} %jac_ref.1), channel_id=1, source_target_pairs={{0,2},{1,3},{2,0},{3,1},{4,6},{5,7},{6,4},{7,5},{8,10},{9,11},{10,... | collective-permute-start | bytes 491528 | tf_op jit(solution)/shard_map/ppermute | solution.py:27
  4.5 7.7 %collective-permute-start.6 = (bf16[128,640]{1,0:T(8,128)(2,1)}, bf16[128,640]{1,0:T(8,128)(2,1)S(1)}, u32[]{:S(2)}, u32[]{:S(2)}) collective-permute-start(bf16[128,640]{1,0:T(8,128)(2,1)} %jac_ref.1), channel_id=1, source_target_pairs={{0,12},{1,13},{2,14},{3,15},{16,28},{17,29},{18,30},{19,31}} | collective-permute-start | bytes 491528 | tf_op jit(solution)/shard_map/ppermute | solution.py:22
  8.7 1.0 %copy-start = (bf16[128,640]{1,0:T(8,128)(2,1)S(1)}, bf16[128,640]{1,0:T(8,128)(2,1)}, u32[]{:S(2)}) copy-start(bf16[128,640]{1,0:T(8,128)(2,1)} %jac_ref.1) | copy-start | bytes 491524
  9.7 0.7 %copy-start.1 = (f32[2,640]{1,0:T(2,128)S(1)}, f32[2,640]{1,0:T(2,128)}, u32[]{:S(2)}) copy-start(f32[2,640]{1,0:T(2,128)} %prior_ref.1) | copy-start | bytes 15364
  11.0 4.5 %collective-permute-start.5 = (bf16[128,640]{1,0:T(8,128)(2,1)S(1)}, bf16[128,640]{1,0:T(8,128)(2,1)S(1)}, u32[]{:S(2)}, u32[]{:S(2)}) collective-permute-start(bf16[128,640]{1,0:T(8,128)(2,1)S(1)} %collective-permute-done.refs_2_), channel_id=1, source_target_pairs={{4,8},{8,12},{5,9},{9,13},{6,10},{10,14},{7,11},{11,15},{20,24},{2... | collective-permute-start | bytes 491528 | tf_op jit(solution)/shard_map/ppermute | solution.py:22
  11.7 1.4 %collective-permute-start.3 = (bf16[64,640]{1,0:T(8,128)(2,1)S(1)}, bf16[64,640]{1,0:T(8,128)(2,1)S(1)}, u32[]{:S(2)}, u32[]{:S(2)}) collective-permute-start(bf16[64,640]{1,0:T(8,128)(2,1)S(1)} %get-tuple-element.48), channel_id=1, source_target_pairs={{0,1},{1,0},{2,3},{3,2},{4,5},{5,4},{6,7},{7,6},{8,9},{9,8},{10,11... | collective-permute-start | bytes 245768 | tf_op jit(solution)/shard_map/ppermute | solution.py:27
  11.7 1.5 %collective-permute-start.4 = (bf16[64,640]{1,0:T(8,128)(2,1)S(1)}, bf16[64,640]{1,0:T(8,128)(2,1)S(1)}, u32[]{:S(2)}, u32[]{:S(2)}) collective-permute-start(bf16[64,640]{1,0:T(8,128)(2,1)S(1)} %get-tuple-element.47), channel_id=1, source_target_pairs={{0,1},{1,0},{2,3},{3,2},{4,5},{5,4},{6,7},{7,6},{8,9},{9,8},{10,11... | collective-permute-start | bytes 245768 | tf_op jit(solution)/shard_map/ppermute | solution.py:27
  12.2 2.2 %collective-permute-start.2 = (bf16[128,640]{1,0:T(8,128)(2,1)S(1)}, bf16[128,640]{1,0:T(8,128)(2,1)S(1)}, u32[]{:S(2)}, u32[]{:S(2)}) collective-permute-start(bf16[128,640]{1,0:T(8,128)(2,1)S(1)} %get-tuple-element.28.refs_0_), channel_id=1, source_target_pairs={{0,1},{1,0},{2,3},{3,2},{4,5},{5,4},{6,7},{7,6},{8,9},{9,8},{10,11... | collective-permute-start | bytes 491528 | tf_op jit(solution)/shard_map/ppermute | solution.py:27
  12.3 1.4 %collective-permute-start.7 = (bf16[64,640]{1,0:T(8,128)(2,1)S(1)}, bf16[64,640]{1,0:T(8,128)(2,1)S(1)}, u32[]{:S(2)}, u32[]{:S(2)}) collective-permute-start(bf16[64,640]{1,0:T(8,128)(2,1)S(1)} %get-tuple-element.45), channel_id=1, source_target_pairs={{0,1},{1,0},{2,3},{3,2},{4,5},{5,4},{6,7},{7,6},{8,9},{9,8},{10,11... | collective-permute-start | bytes 245768 | tf_op jit(solution)/shard_map/ppermute | solution.py:27
  13.1 1.3 %collective-permute-start.8 = (bf16[64,640]{1,0:T(8,128)(2,1)S(1)}, bf16[64,640]{1,0:T(8,128)(2,1)S(1)}, u32[]{:S(2)}, u32[]{:S(2)}) collective-permute-start(bf16[64,640]{1,0:T(8,128)(2,1)S(1)} %get-tuple-element.46), channel_id=1, source_target_pairs={{0,1},{1,0},{2,3},{3,2},{4,5},{5,4},{6,7},{7,6},{8,9},{9,8},{10,11... | collective-permute-start | bytes 245768 | tf_op jit(solution)/shard_map/ppermute | solution.py:27
  15.4 3.7 %collective-permute-start.9 = (bf16[128,640]{1,0:T(8,128)(2,1)S(1)}, bf16[128,640]{1,0:T(8,128)(2,1)S(1)}, u32[]{:S(2)}, u32[]{:S(2)}) collective-permute-start(bf16[128,640]{1,0:T(8,128)(2,1)S(1)} %collective-permute-done.5.refs_4_), channel_id=1, source_target_pairs={{0,1},{1,0},{2,3},{3,2},{4,5},{5,4},{6,7},{7,6},{8,9},{9,8},{10,11... | collective-permute-start | bytes 491528 | tf_op jit(solution)/shard_map/ppermute | solution.py:27
  15.7 5.6 %collective-permute-start.13 = (f16[144,256]{1,0:T(8,128)(2,1)S(1)}, f16[144,256]{1,0:T(8,128)(2,1)S(1)}, u32[]{:S(2)}, u32[]{:S(2)}) collective-permute-start(f16[144,256]{1,0:T(8,128)(2,1)S(1)} %convert_element_type.38), channel_id=1, source_target_pairs={{0,18},{1,19},{2,16},{3,17},{16,2},{17,3},{18,0},{19,1},{4,22},{5,... | collective-permute-start | bytes 221192 | tf_op jit(solution)/shard_map/ppermute | solution.py:35
  17.1 6.0 %collective-permute-start.14 = (f16[144,256]{1,0:T(8,128)(2,1)S(1)}, f16[144,256]{1,0:T(8,128)(2,1)S(1)}, u32[]{:S(2)}, u32[]{:S(2)}) collective-permute-start(f16[144,256]{1,0:T(8,128)(2,1)S(1)} %convert_element_type.36), channel_id=1, source_target_pairs={{0,2},{1,3},{2,0},{3,1},{16,18},{17,19},{18,16},{19,17},{4,6},{5,7... | collective-permute-start | bytes 221192 | tf_op jit(solution)/shard_map/ppermute | solution.py:35
  18.6 5.2 %collective-permute-start.15 = (f16[144,256]{1,0:T(8,128)(2,1)S(1)}, f16[144,256]{1,0:T(8,128)(2,1)S(1)}, u32[]{:S(2)}, u32[]{:S(2)}) collective-permute-start(f16[144,256]{1,0:T(8,128)(2,1)S(1)} %convert_element_type.37), channel_id=1, source_target_pairs={{0,16},{1,17},{2,18},{3,19},{16,0},{17,1},{18,2},{19,3},{4,20},{5,... | collective-permute-start | bytes 221192 | tf_op jit(solution)/shard_map/ppermute | solution.py:35
  19.3 6.0 %collective-permute-start.10 = (f16[144,256]{1,0:T(8,128)(2,1)S(1)}, f16[144,256]{1,0:T(8,128)(2,1)S(1)}, u32[]{:S(2)}, u32[]{:S(2)}) collective-permute-start(f16[144,256]{1,0:T(8,128)(2,1)S(1)} %convert_element_type.39), channel_id=1, source_target_pairs={{0,18},{1,19},{2,16},{3,17},{16,2},{17,3},{18,0},{19,1},{4,22},{5,... | collective-permute-start | bytes 221192 | tf_op jit(solution)/shard_map/ppermute | solution.py:35
  20.8 4.9 %collective-permute-start.11 = (f16[144,256]{1,0:T(8,128)(2,1)S(1)}, f16[144,256]{1,0:T(8,128)(2,1)S(1)}, u32[]{:S(2)}, u32[]{:S(2)}) collective-permute-start(f16[144,256]{1,0:T(8,128)(2,1)S(1)} %convert_element_type.41), channel_id=1, source_target_pairs={{0,16},{1,17},{2,18},{3,19},{16,0},{17,1},{18,2},{19,3},{4,20},{5,... | collective-permute-start | bytes 221192 | tf_op jit(solution)/shard_map/ppermute | solution.py:35
  21.3 4.7 %collective-permute-start.12 = (f16[144,256]{1,0:T(8,128)(2,1)S(1)}, f16[144,256]{1,0:T(8,128)(2,1)S(1)}, u32[]{:S(2)}, u32[]{:S(2)}) collective-permute-start(f16[144,256]{1,0:T(8,128)(2,1)S(1)} %convert_element_type.43), channel_id=1, source_target_pairs={{0,2},{1,3},{2,0},{3,1},{16,18},{17,19},{18,16},{19,17},{4,6},{5,7... | collective-permute-start | bytes 221192 | tf_op jit(solution)/shard_map/ppermute | solution.py:35
